TPU v7x, 32 devices: a whole 2x2x4 slice. The times are simulated.
32 devices in a mesh: layer: 8 (over z, x), tile: 4 (over y, core).
Axes of the slice: x: 2, y: 2, z: 4, core: 2. Of those that a mesh axis runs over, the one named last changes fastest.
Arguments:
- sources: float32 [8, 2, 2, 32, 8192], P('layer', None, None, None, 'tile'), may hold values from -6 to 6
- green: float32 [8, 80, 2, 128, 128], P('layer', 'tile'), may hold values from -0.25 to 0.25
- rowcol: int32 [8, 80, 2], P('layer', 'tile'), may hold values from 0 to 63, as said below
- counts: int32 [8, 16], P('layer', 'tile'), may hold values from 1 to 5, as said below
Outputs:
- traces: float32 [8, 2, 2, 32, 8192], P('layer', None, None, None, 'tile')
Inputs may be any that keep to these rules, and one draw needn't show every extreme that they name: `rowcol`: the row tile of a slot of tile device t lies in t * 16 to (t + 1) * 16 - 1; its column tile differs from its row tile by at most 4. Kind 0 has 2 or more live slots; the four counts of one tile device sum to at most 10; in every layer some tile device has 5 live slots of kind 0 and 10 live slots in all.
All inputs are finite; a program needn't handle non-finite values.
Results may differ from a plain program's by a relative error of at most 0.0003.
Values sent between devices are 32-bit elements; how exact they have to be, the bound alone decides.
No kernel may reach another device: no remote copies, remote signals or barrier semaphores. Data moves between devices by JAX's collectives and lax.ppermute only.
A program may use at most 64 MiB of HBM per device.

v0:
```python
import jax
import jax.numpy as jnp
from jax import lax
from jax.sharding import PartitionSpec as P

TILE = 128
CAP = 5
BAND = 4
TICKS = 6


def from_behind(block, axis, distance):
    devices = range(lax.axis_size(axis))
    route = [(i - distance, i) for i in devices if i - distance in devices]
    return lax.ppermute(block, axis, route)


def padded(cells, sides, width):
    for axis, dim in sides:
        count = lax.axis_size(axis)
        ends = count - 1
        head = lax.slice_in_dim(cells, 0, width, axis=dim)
        tail = lax.slice_in_dim(cells, cells.shape[dim] - width, cells.shape[dim], axis=dim)
        cells = jnp.concatenate(
            [
                lax.ppermute(tail, axis, [(i, (i + 1) % count) for i in range(ends)]),
                cells,
                lax.ppermute(head, axis, [((i + 1) % count, i) for i in range(ends)]),
            ],
            axis=dim,
        )
    return cells


def complex_term(picked, blocks, pattern):
    prod = jnp.einsum(pattern, picked, blocks, precision=lax.Precision.HIGHEST)
    return jnp.stack([prod[0, 0] - prod[1, 1], prod[0, 1] + prod[1, 0]])


def place_terms(terms, target, live, tiles_dev):
    onehot = (
        (target[:, None] == jnp.arange(2 * tiles_dev, dtype=jnp.int32)[None, :]) & live[:, None]
    ).astype(jnp.float32)
    onehot = onehot.reshape(target.shape[0], 2, tiles_dev)
    return jnp.einsum("csni,ngr->gcsri", terms, onehot, precision=lax.Precision.HIGHEST)


def live_update(tiled, blocks, row_local, col_local, live_counts, tiles_dev):
    slot = jnp.arange(4 * CAP, dtype=jnp.int32)
    group = slot // CAP
    live = slot % CAP < live_counts[group]
    score = jnp.where(live, 0, 4 * CAP).astype(jnp.int32) + slot
    order = jnp.argsort(score)[: 2 * CAP]
    kinds = group[order]
    anchor = jnp.where((kinds == 1) | (kinds == 2), 1, 0).astype(jnp.int32)
    picked = tiled[anchor, :, :, col_local[order]]
    chosen_blocks = jnp.take(blocks, order, axis=0)
    terms = complex_term(picked, chosen_blocks, "ncsj,ndij->cdsni")
    target = jnp.where(kinds < 2, 0, 1) * tiles_dev + row_local[order]
    return place_terms(terms, target, live[order], tiles_dev)


def body(sources, green, rowcol, counts):
    width = sources.shape[-1]
    shots = sources.shape[3]
    tiles_dev = width // TILE
    place = lax.axis_index("tile")
    blocks = green[0]
    pairs = rowcol[0]
    live_counts = counts[0]
    row_local = pairs[:, 0] - place * tiles_dev
    col_local = pairs[:, 1] - place * tiles_dev + BAND
    local_sources = sources[0]
    waves = local_sources
    for sweep in range(TICKS - 1):
        prev_down = from_behind(waves[0], "layer", 1)
        next_up = from_behind(waves[1], "layer", -1)
        incoming = jnp.stack([prev_down, next_up])
        widened = padded(incoming, (("tile", 3),), BAND * TILE)
        tiled = widened.reshape(2, 2, shots, tiles_dev + 2 * BAND, TILE)
        update = live_update(tiled, blocks, row_local, col_local, live_counts, tiles_dev)
        waves = local_sources + update.reshape(2, 2, shots, width)
    return waves[None]


def solution(mesh):
    return jax.shard_map(
        body,
        mesh=mesh,
        in_specs=(
            P("layer", None, None, None, "tile"),
            P("layer", "tile", None, None, None),
            P("layer", "tile", None),
            P("layer", "tile"),
        ),
        out_specs=P("layer", None, None, None, "tile"),
        check_vma=False,
    )
```

profile of v0, /device:TPU:9, one launch (start us, length us, event | category | flops | bytes accessed | tf_op | source)
XLA Modules:
  0.0 245.1 jit_solution(4394603352845774893)
XLA Ops:
  0.0 2.4 slice_bitcast_fusion.9
  2.4 3.1 %collective-permute-start = (f32[2,32,2048]{2,1,0:T(8,128)}, f32[2,32,2048]{2,1,0:T(8,128)S(1)}, u32[]{:S(2)}, u32[]{:S(2)}) collective-permute-start(f32[2,32,2048]{2,1,0:T(8,128)} %get-tuple-element.30), channel_id=1, source_target_pairs={{0,4},{4,8},{8,12},{12,16},{16,20},{20,24},{24,28},{1,5},{5,9},{9,... | collective-permute-start | bytes 1572872 | tf_op jit(solution)/shard_map/ppermute | solution.py:15
  5.6 3.1 %collective-permute-start.1 = (f32[2,32,2048]{2,1,0:T(8,128)}, f32[2,32,2048]{2,1,0:T(8,128)}, u32[]{:S(2)}, u32[]{:S(2)}) collective-permute-start(f32[2,32,2048]{2,1,0:T(8,128)} %get-tuple-element.31), channel_id=1, source_target_pairs={{4,0},{8,4},{12,8},{16,12},{20,16},{24,20},{28,24},{5,1},{9,5},{13... | collective-permute-start | bytes 1572872 | tf_op jit(solution)/shard_map/ppermute | solution.py:15
  9.3 2.5 %iota_add_fusion = (s32[20]{0:T(128)S(1)}, pred[20]{0:T(512)(128)(4,1)S(1)}) fusion(s32[]{:T(128)} %bitcast.3, s32[]{:T(128)} %bitcast.2, s32[]{:T(128)} %bitcast.1, s32[]{:T(128)} %bitcast), kind=kLoop, calls=%fused_computation.182 | loop fusion | flops 520 | bytes 116 | tf_op jit(solution)/shard_map/add | solution.py:52
  14.8 12.8 %collective-permute-done = f32[2,32,2048]{2,1,0:T(8,128)S(1)} collective-permute-done((f32[2,32,2048]{2,1,0:T(8,128)}, f32[2,32,2048]{2,1,0:T(8,128)S(1)}, u32[]{:S(2)}, u32[]{:S(2)}) %collective-permute-start) | collective-permute-done | bytes 524320 | tf_op jit(solution)/shard_map/ppermute | solution.py:15
  27.7 2.9 %collective-permute-done.1 = f32[2,32,2048]{2,1,0:T(8,128)} collective-permute-done((f32[2,32,2048]{2,1,0:T(8,128)}, f32[2,32,2048]{2,1,0:T(8,128)}, u32[]{:S(2)}, u32[]{:S(2)}) %collective-permute-start.1) | collective-permute-done | bytes 524320 | tf_op jit(solution)/shard_map/ppermute | solution.py:15
  30.6 1.8 pad_maximum_fusion.14
  32.4 3.5 %collective-permute-start.2 = (f32[2,2,32,512]{3,2,1,0:T(8,128)}, f32[2,2,32,512]{3,2,1,0:T(8,128)S(1)}, u32[]{:S(2)}, u32[]{:S(2)}) collective-permute-start(f32[2,2,32,512]{3,2,1,0:T(8,128)} %get-tuple-element.28), channel_id=1, source_target_pairs={{0,1},{1,2},{2,3},{4,5},{5,6},{6,7},{8,9},{9,10},{10,11},{12,13},{... | collective-permute-start | bytes 786440 | tf_op jit(solution)/shard_map/ppermute | solution.py:26
  35.9 1.9 collective-permute-start.3
  39.2 1.7 gather_fusion.9
  40.9 3.0 %collective-permute-done.3 = f32[2,2,32,512]{3,2,1,0:T(8,128)} collective-permute-done((f32[2,2,32,512]{3,2,1,0:T(8,128)}, f32[2,2,32,512]{3,2,1,0:T(8,128)}, u32[]{:S(2)}, u32[]{:S(2)}) %collective-permute-start.3) | collective-permute-done | bytes 262176 | tf_op jit(solution)/shard_map/ppermute | solution.py:28
  43.9 2.5 %copy_bitcast_fusion.4 = f32[2,2,32,24,128]{4,2,3,1,0:T(8,128)} fusion(f32[2,2,32,512]{3,2,1,0:T(8,128)} %collective-permute-done.3, f32[1,2,32,2048]{3,2,1,0:T(8,128)} %bitcast.18, f32[1,2,32,2048]{3,2,1,0:T(8,128)S(1)} %bitcast.265, f32[2,2,32,512]{3,2,1,0:T(8,128)S(1)} %collective-permute-done.2), kind=kLoop, calls=%fused_computation.14 | loop fusion | flops 1179648 | bytes 3145728 | tf_op jit(solution)/shard_map/reshape | solution.py:80
  46.5 2.0 gather_fusion.4
  48.5 3.0 %fusion.10 = f32[2,2,32,10,128]{4,2,0,1,3:T(8,128)S(1)} fusion(f32[10,2,128,128]{3,2,1,0:T(8,128)} %gather_fusion.9, pred[10]{0:T(512)(128)(4,1)S(1)} %get-tuple-element.8, f32[10,2,32,128]{3,2,1,0:T(8,128)S(1)} %gather_fusion.4), kind=kOutput, calls=%fused_computation.35 | convolution fusion | flops 251985920 | bytes 2293770 | tf_op jit(solution)/shard_map/ncsj,ndij->cdsni/dot_general | solution.py:36
  51.5 1.7 convolution_bitcast_fusion.4
  53.2 2.4 reshape.340
  55.6 1.7 bitcast_add_fusion.3
  57.3 2.1 collective-permute-start.4
  59.4 4.1 %collective-permute-start.5 = (f32[2,32,2048]{2,1,0:T(8,128)S(1)}, f32[2,32,2048]{2,1,0:T(8,128)S(1)}, u32[]{:S(2)}, u32[]{:S(2)}) collective-permute-start(f32[2,32,2048]{2,1,0:T(8,128)S(1)} %get-tuple-element.27), channel_id=1, source_target_pairs={{4,0},{8,4},{12,8},{16,12},{20,16},{24,20},{28,24},{5,1},{9,5},{13... | collective-permute-start | bytes 1572872 | tf_op jit(solution)/shard_map/ppermute | solution.py:15
  63.5 15.1 %collective-permute-done.4 = f32[2,32,2048]{2,1,0:T(8,128)S(1)} collective-permute-done((f32[2,32,2048]{2,1,0:T(8,128)S(1)}, f32[2,32,2048]{2,1,0:T(8,128)S(1)}, u32[]{:S(2)}, u32[]{:S(2)}) %collective-permute-start.4) | collective-permute-done | bytes 524320 | tf_op jit(solution)/shard_map/ppermute | solution.py:15
  78.6 2.8 %collective-permute-done.5 = f32[2,32,2048]{2,1,0:T(8,128)S(1)} collective-permute-done((f32[2,32,2048]{2,1,0:T(8,128)S(1)}, f32[2,32,2048]{2,1,0:T(8,128)S(1)}, u32[]{:S(2)}, u32[]{:S(2)}) %collective-permute-start.5) | collective-permute-done | bytes 524320 | tf_op jit(solution)/shard_map/ppermute | solution.py:15
  81.5 3.9 %collective-permute-start.6 = (f32[2,2,32,512]{3,2,1,0:T(8,128)S(1)}, f32[2,2,32,512]{3,2,1,0:T(8,128)S(1)}, u32[]{:S(2)}, u32[]{:S(2)}) collective-permute-start(f32[2,2,32,512]{3,2,1,0:T(8,128)S(1)} %get-tuple-element.24), channel_id=1, source_target_pairs={{0,1},{1,2},{2,3},{4,5},{5,6},{6,7},{8,9},{9,10},{10,11},{12,13},{... | collective-permute-start | bytes 786440 | tf_op jit(solution)/shard_map/ppermute | solution.py:26
  85.3 1.9 collective-permute-start.7
  88.6 4.4 %collective-permute-done.7 = f32[2,2,32,512]{3,2,1,0:T(8,128)S(1)} collective-permute-done((f32[2,2,32,512]{3,2,1,0:T(8,128)S(1)}, f32[2,2,32,512]{3,2,1,0:T(8,128)S(1)}, u32[]{:S(2)}, u32[]{:S(2)}) %collective-permute-start.7) | collective-permute-done | bytes 262176 | tf_op jit(solution)/shard_map/ppermute | solution.py:28
  94.4 2.0 gather_fusion.5
  96.4 3.0 %fusion.13 = f32[2,2,32,10,128]{4,2,0,1,3:T(8,128)S(1)} fusion(f32[10,2,128,128]{3,2,1,0:T(8,128)} %gather_fusion.9, pred[10]{0:T(512)(128)(4,1)S(1)} %get-tuple-element.8, f32[10,2,32,128]{3,2,1,0:T(8,128)S(1)} %gather_fusion.5), kind=kOutput, calls=%fused_computation.36 | convolution fusion | flops 251985920 | bytes 2293770 | tf_op jit(solution)/shard_map/ncsj,ndij->cdsni/dot_general | solution.py:36
  99.5 1.7 convolution_bitcast_fusion.3
  101.1 2.4 reshape.342
  103.5 1.7 bitcast_add_fusion.2
  105.3 1.9 collective-permute-start.8
  107.2 4.3 %collective-permute-start.9 = (f32[2,32,2048]{2,1,0:T(8,128)S(1)}, f32[2,32,2048]{2,1,0:T(8,128)S(1)}, u32[]{:S(2)}, u32[]{:S(2)}) collective-permute-start(f32[2,32,2048]{2,1,0:T(8,128)S(1)} %get-tuple-element.23), channel_id=1, source_target_pairs={{4,0},{8,4},{12,8},{16,12},{20,16},{24,20},{28,24},{5,1},{9,5},{13... | collective-permute-start | bytes 1572872 | tf_op jit(solution)/shard_map/ppermute | solution.py:15
  111.5 14.6 %collective-permute-done.8 = f32[2,32,2048]{2,1,0:T(8,128)S(1)} collective-permute-done((f32[2,32,2048]{2,1,0:T(8,128)S(1)}, f32[2,32,2048]{2,1,0:T(8,128)S(1)}, u32[]{:S(2)}, u32[]{:S(2)}) %collective-permute-start.8) | collective-permute-done | bytes 524320 | tf_op jit(solution)/shard_map/ppermute | solution.py:15
  126.1 3.3 %collective-permute-done.9 = f32[2,32,2048]{2,1,0:T(8,128)S(1)} collective-permute-done((f32[2,32,2048]{2,1,0:T(8,128)S(1)}, f32[2,32,2048]{2,1,0:T(8,128)S(1)}, u32[]{:S(2)}, u32[]{:S(2)}) %collective-permute-start.9) | collective-permute-done | bytes 524320 | tf_op jit(solution)/shard_map/ppermute | solution.py:15
  129.4 1.9 collective-permute-start.10
  131.3 2.4 collective-permute-start.11
  134.6 4.4 %collective-permute-done.11 = f32[2,2,32,512]{3,2,1,0:T(8,128)S(1)} collective-permute-done((f32[2,2,32,512]{3,2,1,0:T(8,128)S(1)}, f32[2,2,32,512]{3,2,1,0:T(8,128)S(1)}, u32[]{:S(2)}, u32[]{:S(2)}) %collective-permute-start.11) | collective-permute-done | bytes 262176 | tf_op jit(solution)/shard_map/ppermute | solution.py:28
  140.4 2.0 gather_fusion.6
  142.4 3.0 %fusion.16 = f32[2,2,32,10,128]{4,2,0,1,3:T(8,128)S(1)} fusion(f32[10,2,128,128]{3,2,1,0:T(8,128)} %gather_fusion.9, pred[10]{0:T(512)(128)(4,1)S(1)} %get-tuple-element.8, f32[10,2,32,128]{3,2,1,0:T(8,128)S(1)} %gather_fusion.6), kind=kOutput, calls=%fused_computation.37 | convolution fusion | flops 251985920 | bytes 2293770 | tf_op jit(solution)/shard_map/ncsj,ndij->cdsni/dot_general | solution.py:36
  145.5 1.7 convolution_bitcast_fusion.2
  147.1 2.4 reshape.344
  149.5 1.7 bitcast_add_fusion.1
  151.2 1.9 collective-permute-start.12
  153.2 4.3 %collective-permute-start.13 = (f32[2,32,2048]{2,1,0:T(8,128)S(1)}, f32[2,32,2048]{2,1,0:T(8,128)S(1)}, u32[]{:S(2)}, u32[]{:S(2)}) collective-permute-start(f32[2,32,2048]{2,1,0:T(8,128)S(1)} %get-tuple-element.19), channel_id=1, source_target_pairs={{4,0},{8,4},{12,8},{16,12},{20,16},{24,20},{28,24},{5,1},{9,5},{13... | collective-permute-start | bytes 1572872 | tf_op jit(solution)/shard_map/ppermute | solution.py:15
  157.4 15.1 %collective-permute-done.12 = f32[2,32,2048]{2,1,0:T(8,128)S(1)} collective-permute-done((f32[2,32,2048]{2,1,0:T(8,128)S(1)}, f32[2,32,2048]{2,1,0:T(8,128)S(1)}, u32[]{:S(2)}, u32[]{:S(2)}) %collective-permute-start.12) | collective-permute-done | bytes 524320 | tf_op jit(solution)/shard_map/ppermute | solution.py:15
  172.6 3.3 %collective-permute-done.13 = f32[2,32,2048]{2,1,0:T(8,128)S(1)} collective-permute-done((f32[2,32,2048]{2,1,0:T(8,128)S(1)}, f32[2,32,2048]{2,1,0:T(8,128)S(1)}, u32[]{:S(2)}, u32[]{:S(2)}) %collective-permute-start.13) | collective-permute-done | bytes 524320 | tf_op jit(solution)/shard_map/ppermute | solution.py:15
  175.9 1.9 collective-permute-start.14
  177.8 2.6 %collective-permute-start.15 = (f32[2,2,32,512]{3,2,1,0:T(8,128)S(1)}, f32[2,2,32,512]{3,2,1,0:T(8,128)S(1)}, u32[]{:S(2)}, u32[]{:S(2)}) collective-permute-start(f32[2,2,32,512]{3,2,1,0:T(8,128)S(1)} %get-tuple-element.17), channel_id=1, source_target_pairs={{1,0},{2,1},{3,2},{5,4},{6,5},{7,6},{9,8},{10,9},{11,10},{13,12},{... | collective-permute-start | bytes 786440 | tf_op jit(solution)/shard_map/ppermute | solution.py:28
  181.1 4.4 %collective-permute-done.15 = f32[2,2,32,512]{3,2,1,0:T(8,128)S(1)} collective-permute-done((f32[2,2,32,512]{3,2,1,0:T(8,128)S(1)}, f32[2,2,32,512]{3,2,1,0:T(8,128)S(1)}, u32[]{:S(2)}, u32[]{:S(2)}) %collective-permute-start.15) | collective-permute-done | bytes 262176 | tf_op jit(solution)/shard_map/ppermute | solution.py:28
  186.9 2.0 gather_fusion.7
  188.9 3.0 %fusion.19 = f32[2,2,32,10,128]{4,2,0,1,3:T(8,128)S(1)} fusion(f32[10,2,128,128]{3,2,1,0:T(8,128)} %gather_fusion.9, pred[10]{0:T(512)(128)(4,1)S(1)} %get-tuple-element.8, f32[10,2,32,128]{3,2,1,0:T(8,128)S(1)} %gather_fusion.7), kind=kOutput, calls=%fused_computation.38 | convolution fusion | flops 251985920 | bytes 2293770 | tf_op jit(solution)/shard_map/ncsj,ndij->cdsni/dot_general | solution.py:36
  191.9 1.7 convolution_bitcast_fusion.1
  193.6 2.4 reshape.346
  197.7 1.9 collective-permute-start.16
  199.6 4.3 %collective-permute-start.17 = (f32[2,32,2048]{2,1,0:T(8,128)S(1)}, f32[2,32,2048]{2,1,0:T(8,128)S(1)}, u32[]{:S(2)}, u32[]{:S(2)}) collective-permute-start(f32[2,32,2048]{2,1,0:T(8,128)S(1)} %get-tuple-element.15), channel_id=1, source_target_pairs={{4,0},{8,4},{12,8},{16,12},{20,16},{24,20},{28,24},{5,1},{9,5},{13... | collective-permute-start | bytes 1572872 | tf_op jit(solution)/shard_map/ppermute | solution.py:15
  203.9 15.1 %collective-permute-done.16 = f32[2,32,2048]{2,1,0:T(8,128)S(1)} collective-permute-done((f32[2,32,2048]{2,1,0:T(8,128)S(1)}, f32[2,32,2048]{2,1,0:T(8,128)S(1)}, u32[]{:S(2)}, u32[]{:S(2)}) %collective-permute-start.16) | collective-permute-done | bytes 524320 | tf_op jit(solution)/shard_map/ppermute | solution.py:15
  219.0 3.3 %collective-permute-done.17 = f32[2,32,2048]{2,1,0:T(8,128)S(1)} collective-permute-done((f32[2,32,2048]{2,1,0:T(8,128)S(1)}, f32[2,32,2048]{2,1,0:T(8,128)S(1)}, u32[]{:S(2)}, u32[]{:S(2)}) %collective-permute-start.17) | collective-permute-done | bytes 524320 | tf_op jit(solution)/shard_map/ppermute | solution.py:15
  222.3 1.9 collective-permute-start.18
  224.3 2.4 collective-permute-start.19
  227.6 4.4 %collective-permute-done.19 = f32[2,2,32,512]{3,2,1,0:T(8,128)S(1)} collective-permute-done((f32[2,2,32,512]{3,2,1,0:T(8,128)S(1)}, f32[2,2,32,512]{3,2,1,0:T(8,128)S(1)}, u32[]{:S(2)}, u32[]{:S(2)}) %collective-permute-start.19) | collective-permute-done | bytes 262176 | tf_op jit(solution)/shard_map/ppermute | solution.py:28
  233.4 2.0 gather_fusion.8
  235.4 3.0 %fusion.22 = f32[2,2,32,10,128]{4,2,0,1,3:T(8,128)S(1)} fusion(f32[10,2,128,128]{3,2,1,0:T(8,128)} %gather_fusion.9, pred[10]{0:T(512)(128)(4,1)S(1)} %get-tuple-element.8, f32[10,2,32,128]{3,2,1,0:T(8,128)S(1)} %gather_fusion.8), kind=kOutput, calls=%fused_computation.39 | convolution fusion | flops 251985920 | bytes 2293770 | tf_op jit(solution)/shard_map/ncsj,ndij->cdsni/dot_general | solution.py:36
  238.4 1.7 convolution_bitcast_fusion
  240.1 2.4 reshape.348
  242.5 2.6 %add.211 = f32[1,2,2,32,2048]{4,3,2,1,0:T(8,128)} add(f32[1,2,2,32,2048]{4,3,2,1,0:T(8,128)} %param.6, f32[1,2,2,32,2048]{4,3,2,1,0:T(8,128)} %reshape.348) | non-fusion elementwise | flops 262144 | bytes 3145728 | tf_op jit(solution)/shard_map/add | solution.py:82
  (53 shorter events, 16.8 us)
Async XLA Ops:
  0.0 39.2 %copy-start = (f32[1,20,2,128,128]{4,3,2,1,0:T(8,128)S(1)}, f32[1,20,2,128,128]{4,3,2,1,0:T(8,128)}, u32[]{:S(2)}) copy-start(f32[1,20,2,128,128]{4,3,2,1,0:T(8,128)} %param.7) | copy-start | bytes 7864324
  0.0 8.6 %copy-start.1 = (s32[1,4]{1,0:T(1,128)S(1)}, s32[1,4]{1,0:T(1,128)}, u32[]{:S(2)}) copy-start(s32[1,4]{1,0:T(1,128)} %param.9) | copy-start | bytes 52
  0.0 14.1 %copy-start.2 = (s32[1,20,2]{1,2,0:T(2,128)S(1)}, s32[1,20,2]{1,2,0:T(2,128)}, u32[]{:S(2)}) copy-start(s32[1,20,2]{1,2,0:T(2,128)} %param.8) | copy-start | bytes 484
  2.4 25.2 %collective-permute-start = (f32[2,32,2048]{2,1,0:T(8,128)}, f32[2,32,2048]{2,1,0:T(8,128)S(1)}, u32[]{:S(2)}, u32[]{:S(2)}) collective-permute-start(f32[2,32,2048]{2,1,0:T(8,128)} %get-tuple-element.30), channel_id=1, source_target_pairs={{0,4},{4,8},{8,12},{12,16},{16,20},{20,24},{24,28},{1,5},{5,9},{9,... | collective-permute-start | bytes 1572872 | tf_op jit(solution)/shard_map/ppermute | solution.py:15
  5.6 25.1 %collective-permute-start.1 = (f32[2,32,2048]{2,1,0:T(8,128)}, f32[2,32,2048]{2,1,0:T(8,128)}, u32[]{:S(2)}, u32[]{:S(2)}) collective-permute-start(f32[2,32,2048]{2,1,0:T(8,128)} %get-tuple-element.31), channel_id=1, source_target_pairs={{4,0},{8,4},{12,8},{16,12},{20,16},{24,20},{28,24},{5,1},{9,5},{13... | collective-permute-start | bytes 1572872 | tf_op jit(solution)/shard_map/ppermute | solution.py:15
  32.4 8.5 %collective-permute-start.2 = (f32[2,2,32,512]{3,2,1,0:T(8,128)}, f32[2,2,32,512]{3,2,1,0:T(8,128)S(1)}, u32[]{:S(2)}, u32[]{:S(2)}) collective-permute-start(f32[2,2,32,512]{3,2,1,0:T(8,128)} %get-tuple-element.28), channel_id=1, source_target_pairs={{0,1},{1,2},{2,3},{4,5},{5,6},{6,7},{8,9},{9,10},{10,11},{12,13},{... | collective-permute-start | bytes 786440 | tf_op jit(solution)/shard_map/ppermute | solution.py:26
  35.9 8.0 %collective-permute-start.3 = (f32[2,2,32,512]{3,2,1,0:T(8,128)}, f32[2,2,32,512]{3,2,1,0:T(8,128)}, u32[]{:S(2)}, u32[]{:S(2)}) collective-permute-start(f32[2,2,32,512]{3,2,1,0:T(8,128)} %get-tuple-element.29), channel_id=1, source_target_pairs={{1,0},{2,1},{3,2},{5,4},{6,5},{7,6},{9,8},{10,9},{11,10},{13,12},{... | collective-permute-start | bytes 786440 | tf_op jit(solution)/shard_map/ppermute | solution.py:28
  57.3 21.3 %collective-permute-start.4 = (f32[2,32,2048]{2,1,0:T(8,128)S(1)}, f32[2,32,2048]{2,1,0:T(8,128)S(1)}, u32[]{:S(2)}, u32[]{:S(2)}) collective-permute-start(f32[2,32,2048]{2,1,0:T(8,128)S(1)} %get-tuple-element.26), channel_id=1, source_target_pairs={{0,4},{4,8},{8,12},{12,16},{16,20},{20,24},{24,28},{1,5},{5,9},{9,... | collective-permute-start | bytes 1572872 | tf_op jit(solution)/shard_map/ppermute | solution.py:15
  59.4 22.0 %collective-permute-start.5 = (f32[2,32,2048]{2,1,0:T(8,128)S(1)}, f32[2,32,2048]{2,1,0:T(8,128)S(1)}, u32[]{:S(2)}, u32[]{:S(2)}) collective-permute-start(f32[2,32,2048]{2,1,0:T(8,128)S(1)} %get-tuple-element.27), channel_id=1, source_target_pairs={{4,0},{8,4},{12,8},{16,12},{20,16},{24,20},{28,24},{5,1},{9,5},{13... | collective-permute-start | bytes 1572872 | tf_op jit(solution)/shard_map/ppermute | solution.py:15
  81.5 7.2 %collective-permute-start.6 = (f32[2,2,32,512]{3,2,1,0:T(8,128)S(1)}, f32[2,2,32,512]{3,2,1,0:T(8,128)S(1)}, u32[]{:S(2)}, u32[]{:S(2)}) collective-permute-start(f32[2,2,32,512]{3,2,1,0:T(8,128)S(1)} %get-tuple-element.24), channel_id=1, source_target_pairs={{0,1},{1,2},{2,3},{4,5},{5,6},{6,7},{8,9},{9,10},{10,11},{12,13},{... | collective-permute-start | bytes 786440 | tf_op jit(solution)/shard_map/ppermute | solution.py:26
  85.3 7.7 %collective-permute-start.7 = (f32[2,2,32,512]{3,2,1,0:T(8,128)S(1)}, f32[2,2,32,512]{3,2,1,0:T(8,128)S(1)}, u32[]{:S(2)}, u32[]{:S(2)}) collective-permute-start(f32[2,2,32,512]{3,2,1,0:T(8,128)S(1)} %get-tuple-element.25), channel_id=1, source_target_pairs={{1,0},{2,1},{3,2},{5,4},{6,5},{7,6},{9,8},{10,9},{11,10},{13,12},{... | collective-permute-start | bytes 786440 | tf_op jit(solution)/shard_map/ppermute | solution.py:28
  105.3 20.8 %collective-permute-start.8 = (f32[2,32,2048]{2,1,0:T(8,128)S(1)}, f32[2,32,2048]{2,1,0:T(8,128)S(1)}, u32[]{:S(2)}, u32[]{:S(2)}) collective-permute-start(f32[2,32,2048]{2,1,0:T(8,128)S(1)} %get-tuple-element.22), channel_id=1, source_target_pairs={{0,4},{4,8},{8,12},{12,16},{16,20},{20,24},{24,28},{1,5},{5,9},{9,... | collective-permute-start | bytes 1572872 | tf_op jit(solution)/shard_map/ppermute | solution.py:15
  107.2 22.2 %collective-permute-start.9 = (f32[2,32,2048]{2,1,0:T(8,128)S(1)}, f32[2,32,2048]{2,1,0:T(8,128)S(1)}, u32[]{:S(2)}, u32[]{:S(2)}) collective-permute-start(f32[2,32,2048]{2,1,0:T(8,128)S(1)} %get-tuple-element.23), channel_id=1, source_target_pairs={{4,0},{8,4},{12,8},{16,12},{20,16},{24,20},{28,24},{5,1},{9,5},{13... | collective-permute-start | bytes 1572872 | tf_op jit(solution)/shard_map/ppermute | solution.py:15
  129.4 5.2 %collective-permute-start.10 = (f32[2,2,32,512]{3,2,1,0:T(8,128)S(1)}, f32[2,2,32,512]{3,2,1,0:T(8,128)S(1)}, u32[]{:S(2)}, u32[]{:S(2)}) collective-permute-start(f32[2,2,32,512]{3,2,1,0:T(8,128)S(1)} %get-tuple-element.20), channel_id=1, source_target_pairs={{0,1},{1,2},{2,3},{4,5},{5,6},{6,7},{8,9},{9,10},{10,11},{12,13},{... | collective-permute-start | bytes 786440 | tf_op jit(solution)/shard_map/ppermute | solution.py:26
  131.3 7.7 %collective-permute-start.11 = (f32[2,2,32,512]{3,2,1,0:T(8,128)S(1)}, f32[2,2,32,512]{3,2,1,0:T(8,128)S(1)}, u32[]{:S(2)}, u32[]{:S(2)}) collective-permute-start(f32[2,2,32,512]{3,2,1,0:T(8,128)S(1)} %get-tuple-element.21), channel_id=1, source_target_pairs={{1,0},{2,1},{3,2},{5,4},{6,5},{7,6},{9,8},{10,9},{11,10},{13,12},{... | collective-permute-start | bytes 786440 | tf_op jit(solution)/shard_map/ppermute | solution.py:28
  151.2 21.3 %collective-permute-start.12 = (f32[2,32,2048]{2,1,0:T(8,128)S(1)}, f32[2,32,2048]{2,1,0:T(8,128)S(1)}, u32[]{:S(2)}, u32[]{:S(2)}) collective-permute-start(f32[2,32,2048]{2,1,0:T(8,128)S(1)} %get-tuple-element.18), channel_id=1, source_target_pairs={{0,4},{4,8},{8,12},{12,16},{16,20},{20,24},{24,28},{1,5},{5,9},{9,... | collective-permute-start | bytes 1572872 | tf_op jit(solution)/shard_map/ppermute | solution.py:15
  153.2 22.7 %collective-permute-start.13 = (f32[2,32,2048]{2,1,0:T(8,128)S(1)}, f32[2,32,2048]{2,1,0:T(8,128)S(1)}, u32[]{:S(2)}, u32[]{:S(2)}) collective-permute-start(f32[2,32,2048]{2,1,0:T(8,128)S(1)} %get-tuple-element.19), channel_id=1, source_target_pairs={{4,0},{8,4},{12,8},{16,12},{20,16},{24,20},{28,24},{5,1},{9,5},{13... | collective-permute-start | bytes 1572872 | tf_op jit(solution)/shard_map/ppermute | solution.py:15
  175.9 5.2 %collective-permute-start.14 = (f32[2,2,32,512]{3,2,1,0:T(8,128)S(1)}, f32[2,2,32,512]{3,2,1,0:T(8,128)S(1)}, u32[]{:S(2)}, u32[]{:S(2)}) collective-permute-start(f32[2,2,32,512]{3,2,1,0:T(8,128)S(1)} %get-tuple-element.16), channel_id=1, source_target_pairs={{0,1},{1,2},{2,3},{4,5},{5,6},{6,7},{8,9},{9,10},{10,11},{12,13},{... | collective-permute-start | bytes 786440 | tf_op jit(solution)/shard_map/ppermute | solution.py:26
  177.8 7.7 %collective-permute-start.15 = (f32[2,2,32,512]{3,2,1,0:T(8,128)S(1)}, f32[2,2,32,512]{3,2,1,0:T(8,128)S(1)}, u32[]{:S(2)}, u32[]{:S(2)}) collective-permute-start(f32[2,2,32,512]{3,2,1,0:T(8,128)S(1)} %get-tuple-element.17), channel_id=1, source_target_pairs={{1,0},{2,1},{3,2},{5,4},{6,5},{7,6},{9,8},{10,9},{11,10},{13,12},{... | collective-permute-start | bytes 786440 | tf_op jit(solution)/shard_map/ppermute | solution.py:28
  197.7 21.3 %collective-permute-start.16 = (f32[2,32,2048]{2,1,0:T(8,128)S(1)}, f32[2,32,2048]{2,1,0:T(8,128)S(1)}, u32[]{:S(2)}, u32[]{:S(2)}) collective-permute-start(f32[2,32,2048]{2,1,0:T(8,128)S(1)} %get-tuple-element.14), channel_id=1, source_target_pairs={{0,4},{4,8},{8,12},{12,16},{16,20},{20,24},{24,28},{1,5},{5,9},{9,... | collective-permute-start | bytes 1572872 | tf_op jit(solution)/shard_map/ppermute | solution.py:15
  199.6 22.7 %collective-permute-start.17 = (f32[2,32,2048]{2,1,0:T(8,128)S(1)}, f32[2,32,2048]{2,1,0:T(8,128)S(1)}, u32[]{:S(2)}, u32[]{:S(2)}) collective-permute-start(f32[2,32,2048]{2,1,0:T(8,128)S(1)} %get-tuple-element.15), channel_id=1, source_target_pairs={{4,0},{8,4},{12,8},{16,12},{20,16},{24,20},{28,24},{5,1},{9,5},{13... | collective-permute-start | bytes 1572872 | tf_op jit(solution)/shard_map/ppermute | solution.py:15
  222.3 5.2 %collective-permute-start.18 = (f32[2,2,32,512]{3,2,1,0:T(8,128)S(1)}, f32[2,2,32,512]{3,2,1,0:T(8,128)S(1)}, u32[]{:S(2)}, u32[]{:S(2)}) collective-permute-start(f32[2,2,32,512]{3,2,1,0:T(8,128)S(1)} %get-tuple-element.12), channel_id=1, source_target_pairs={{0,1},{1,2},{2,3},{4,5},{5,6},{6,7},{8,9},{9,10},{10,11},{12,13},{... | collective-permute-start | bytes 786440 | tf_op jit(solution)/shard_map/ppermute | solution.py:26
  224.3 7.7 %collective-permute-start.19 = (f32[2,2,32,512]{3,2,1,0:T(8,128)S(1)}, f32[2,2,32,512]{3,2,1,0:T(8,128)S(1)}, u32[]{:S(2)}, u32[]{:S(2)}) collective-permute-start(f32[2,2,32,512]{3,2,1,0:T(8,128)S(1)} %get-tuple-element.13), channel_id=1, source_target_pairs={{1,0},{2,1},{3,2},{5,4},{6,5},{7,6},{9,8},{10,9},{11,10},{13,12},{... | collective-permute-start | bytes 786440 | tf_op jit(solution)/shard_map/ppermute | solution.py:28
where the time goes:
time: 246 us; the launch traced here: 245 us
  waiting for transfers between devices  113 us (46%)
  starting transfers between devices  55.3 us (22%)
  local copies, waits for them, and re-layouts  29.6 us (12%)
  other arithmetic  23.8 us (10%)
  matrix products  23.1 us (9%)
    ppermute x10, waiting for transfers between devices, from_behind(): return lax.ppermute(block, axis, route)  88.4 us
    ppermute x10, starting transfers between devices, from_behind(): return lax.ppermute(block, axis, route)  30.9 us
    ppermute x5, waiting for transfers between devices, padded(): lax.ppermute(head, axis, [((i + 1) % count, i) for i in range(ends)])  20.6 us
    dot_general x5, matrix products, complex_term(): prod = jnp.einsum(pattern, picked, blocks, precision=lax.Precision.HIGHEST)  14.8 us
    ppermute x5, starting transfers between devices, padded(): lax.ppermute(tail, axis, [(i, (i + 1) % count) for i in range(ends)])  13.1 us
    reshape x5, local copies, waits for them, and re-layouts, body(): waves = local_sources + update.reshape(2, 2, shots, width)  11.9 us
    ppermute x5, starting transfers between devices, padded(): lax.ppermute(head, axis, [((i + 1) % count, i) for i in range(ends)])  11.3 us
    gather x6, local copies, waits for them, and re-layouts, live_update(): picked = tiled[anchor, :, :, col_local[order]]  10.7 us
  transfers between devices with their start and end apart: 20, of which 19 were waited for; matrix products, arithmetic and copies ran while one was open for 4% of the time, Pallas kernels for 0%

commit v1 on v0

v1 whole, which is shorter than its diff:
```python
import functools

import jax
import jax.numpy as jnp
from jax import lax
from jax.experimental import pallas as pl
from jax.experimental.pallas import tpu as pltpu
from jax.sharding import PartitionSpec as P

TILE = 128
CAP = 5
TICKS = 6
KINDS = 4
LIVE = 2 * CAP
SIDE = 2 * CAP - 2

VMEM = pl.BlockSpec(memory_space=pltpu.VMEM)
SMEM = pl.BlockSpec(memory_space=pltpu.SMEM)
LIMIT = 48 * 1024 * 1024


def partner(index, offset, count):
    return index ^ offset if count & (count - 1) == 0 else (index + offset) % count


def swap_tile(block, offset):
    count = lax.axis_size("tile")
    return lax.ppermute(block, "tile", [(i, partner(i, offset, count)) for i in range(count)])


def source_of(place, offset, count):
    return place ^ offset if count & (count - 1) == 0 else lax.rem(place - offset + count, count)


def target_of(place, offset, count):
    return place ^ offset if count & (count - 1) == 0 else lax.rem(place + offset, count)


def gather_groups(own):
    count = lax.axis_size("tile")
    groups = {0: own}
    if count & (count - 1) == 0:
        bit = count // 2
        while bit:
            for offset in list(groups):
                groups[offset ^ bit] = swap_tile(groups[offset], bit)
            bit //= 2
    else:
        for offset in range(1, count):
            groups[offset] = swap_tile(own, offset)
    return [groups[offset] for offset in range(count)]


def swap_layers(first, second):
    layers = lax.axis_size("layer")
    odd = [(i, i + 1) for i in range(1, layers - 1, 2)]
    even = [(i, i + 1) for i in range(0, layers - 1, 2)]
    both = lambda pairs: pairs + [(b, a) for a, b in pairs]
    return lax.ppermute(first, "layer", both(odd)), lax.ppermute(second, "layer", both(even))


def local_codes(pairs, live_counts):
    slot = jnp.arange(KINDS * CAP, dtype=jnp.int32)
    kind = slot // CAP
    bound = jnp.sum(jnp.where(kind[:, None] == jnp.arange(KINDS)[None, :], live_counts[None, :], 0), axis=1)
    live = slot % CAP < bound
    before = slot[None, :] < slot[:, None]
    rank = jnp.sum(jnp.where(before & live[None, :], 1, 0), axis=1)
    hot = live[:, None] & (rank[:, None] == jnp.arange(LIVE, dtype=jnp.int32)[None, :])
    code = pairs[:, 0] * 65536 + pairs[:, 1] * 8 + kind * 2 + 1
    order = jnp.sum(jnp.where(hot, slot[:, None], 0), axis=0)
    codes = jnp.sum(jnp.where(hot, code[:, None], 0), axis=0)
    return order.astype(jnp.int32), codes.astype(jnp.int32)


def lists(codes, layer, place, tiles, cap, cap_read):
    layers, devices, _ = codes.shape
    flat = codes.reshape(layers, devices * LIVE)
    alive = flat & 1
    kind = (flat >> 1) & 3
    col = (flat >> 3) & 8191
    row = flat >> 16
    wdir = kind >> 1
    rdir = (kind ^ (kind >> 1)) & 1
    tile = jnp.arange(tiles, dtype=jnp.int32)
    row_hot = (row[:, :, None] == tile) & (alive[:, :, None] == 1)
    col_hot = (col[:, :, None] == tile) & (alive[:, :, None] == 1)
    written, read = [], []
    for d in range(2):
        written.append(jnp.any(row_hot & (wdir[:, :, None] == d), axis=1))
        read.append(jnp.any(col_hot & (rdir[:, :, None] == d), axis=1))
    none = jnp.zeros((1, tiles), jnp.bool_)
    wanted = jnp.stack([jnp.concatenate([read[0][1:], none]), jnp.concatenate([none, read[1][:-1]])], axis=1)
    sent = wanted & jnp.stack(written, axis=1)
    before = (tile[:, None] < tile[None, :]).astype(jnp.int32)

    def place_in(chosen):
        return jnp.sum(jnp.where(chosen, 1, 0)[..., :, None] * before, axis=-2)

    most = jnp.max(jnp.sum(jnp.where(sent, 1, 0), axis=-1))
    odd = layer & 1

    def mine(table, shift):
        padded = jnp.concatenate([jnp.zeros_like(table[:1]), table, jnp.zeros_like(table[:1])])
        return lax.dynamic_index_in_dim(padded, layer + 1 + shift, axis=0, keepdims=False)

    sent_at = jnp.where(sent, place_in(sent) + 1, 0)
    want_at = jnp.where(wanted, place_in(wanted) + 1, 0)
    my = lambda values: lax.dynamic_index_in_dim(values, layer, axis=0, keepdims=False)
    m_row_hot, m_col_hot, m_wdir, m_rdir = my(row_hot), my(col_hot), my(wdir), my(rdir)

    def look(hot, table, side):
        rows = jnp.where(side[:, None] == 0, table[0][None], table[1][None])
        return jnp.sum(jnp.where(hot, rows, 0), axis=1)

    sent_here = mine(sent_at, 0)
    sent_in = jnp.stack([mine(sent_at, -1)[0], mine(sent_at, 1)[1]])
    want_in = jnp.stack([mine(want_at, -1)[0], mine(want_at, 1)[1]])
    send = look(m_row_hot, sent_here, m_wdir)
    recv = look(m_col_hot, sent_in, m_rdir)
    src = look(m_col_hot, want_in, m_rdir)
    send_buf = jnp.where(odd == 1, m_wdir, 1 - m_wdir)
    recv_buf = jnp.where(odd == 1, 1 - m_rdir, m_rdir)
    send = jnp.where(send > 0, send_buf * cap + send - 1, 2 * cap)
    recv = jnp.where(recv > 0, recv_buf * cap + recv - 1, 2 * cap)
    src = jnp.where(src > 0, recv_buf * cap_read + src - 1, 2 * cap_read)
    per_slot = jnp.stack([send, recv, src]).reshape(3, devices, LIVE)
    per_slot = jnp.concatenate(
        [
            lax.dynamic_index_in_dim(per_slot, source_of(place, k, devices), axis=1, keepdims=False)
            for k in range(devices)
        ],
        axis=1,
    )
    want_here = mine(want_at, 0)
    entry = jnp.arange(1, cap_read + 1, dtype=jnp.int32)
    ids = jnp.sum(jnp.where(want_here[:, None, :] == entry[None, :, None], tile, 0), axis=-1)
    first = jnp.where(odd == 1, 0, 1)
    ids = jnp.where(first == 0, jnp.stack([ids[0], ids[1]]), jnp.stack([ids[1], ids[0]]))
    dirs = jnp.stack([first, 1 - first])
    wanted_ids = jnp.concatenate([ids.reshape(-1), dirs, place[None]]).astype(jnp.int32)
    return per_slot.astype(jnp.int32), wanted_ids, most


def split_kernel(green_ref, high_ref, low_ref):
    for slot in range(green_ref.shape[0]):
        for part in range(2):
            block = green_ref[slot, part].T
            high = block.astype(jnp.bfloat16)
            low = (block - high.astype(jnp.float32)).astype(jnp.bfloat16)
            high_ref[slot, :, part * TILE : (part + 1) * TILE] = high
            low_ref[slot, :, part * TILE : (part + 1) * TILE] = low


def split_green(packed):
    shape = jax.ShapeDtypeStruct((packed.shape[0], TILE, 2 * TILE), jnp.bfloat16)
    return pl.pallas_call(
        split_kernel,
        out_shape=(shape, shape),
        in_specs=[VMEM],
        out_specs=(VMEM, VMEM),
        compiler_params=pltpu.CompilerParams(vmem_limit_bytes=LIMIT),
        name="split_green",
    )(packed)


def pick_kernel(tiles_dev, cap_read, ids_ref, *refs):
    pieces, (first_ref, second_ref) = refs[:-2], refs[-2:]
    devices = len(pieces)
    place = ids_ref[2 * cap_read + 2]
    for half, out_ref in enumerate((first_ref, second_ref)):
        direction = ids_ref[2 * cap_read + half]

        def one(j, carry):
            tile = ids_ref[half * cap_read + j]
            owner = lax.div(tile, tiles_dev)
            start = pl.multiple_of(lax.rem(tile, tiles_dev) * TILE, TILE)
            for offset in range(devices):

                @pl.when(owner == source_of(place, offset, devices))
                def _():
                    for part in range(2):
                        block = pieces[offset][direction, part, :, pl.ds(start, TILE)]
                        out_ref[j, part] = block

            return carry

        lax.fori_loop(0, cap_read, one, 0)


def pick_tiles(ids, pieces, tiles_dev, cap_read):
    sub = pieces[0].shape[2]
    shape = jax.ShapeDtypeStruct((cap_read, 2, sub, TILE), jnp.float32)
    return pl.pallas_call(
        functools.partial(pick_kernel, tiles_dev, cap_read),
        out_shape=(shape, shape),
        in_specs=[SMEM] + [VMEM] * len(pieces),
        out_specs=(VMEM, VMEM),
        compiler_params=pltpu.CompilerParams(vmem_limit_bytes=LIMIT),
        name="pick_tiles",
    )(ids, *pieces)


def either(index, first_ref, second_ref):
    cap = first_ref.shape[0]
    a = first_ref[jnp.minimum(index, cap - 1)]
    b = second_ref[jnp.clip(index - cap, 0, cap - 1)]
    zero = jnp.zeros_like(a)
    return jnp.where(index < cap, a, jnp.where(index < 2 * cap, b, zero))


def block_term(x, high, low):
    parts, sub, _ = x.shape
    flat = x.reshape(parts * sub, TILE)
    top = flat.astype(jnp.bfloat16)
    rest = (flat - top.astype(jnp.float32)).astype(jnp.bfloat16)
    rows = parts * sub
    main = jnp.dot(jnp.concatenate([top, rest], axis=0), high, preferred_element_type=jnp.float32)
    prod = main[:rows] + main[rows:] + jnp.dot(top, low, preferred_element_type=jnp.float32)
    real = prod[:sub, :TILE] - prod[sub:, TILE:]
    imag = prod[:sub, TILE:] + prod[sub:, :TILE]
    return real, imag


def tick_kernel(stage, devices, cap, idx_ref, *refs):
    refs = list(refs)
    highs = [refs.pop(0) for _ in range(devices)]
    lows = [refs.pop(0) for _ in range(devices)]
    if stage == "first":
        src_a, src_b = refs.pop(0), refs.pop(0)
        x_out = refs.pop(2)
    else:
        xs, got_a, got_b = refs.pop(0), refs.pop(0), refs.pop(0)
    if stage == "last":
        outs = refs
    else:
        out_a, out_b, acc = refs
        acc[...] = jnp.zeros_like(acc)
    for group in range(devices):
        for j in range(LIVE):
            slot = group * LIVE + j
            if stage == "first":
                x = either(idx_ref[2, slot], src_a, src_b)
                x_out[slot] = x
            else:
                x = xs[slot] + either(idx_ref[1, slot], got_a, got_b)
            real, imag = block_term(x, highs[group][j], lows[group][j])
            if stage == "last":
                outs[group][j, 0] = real
                outs[group][j, 1] = imag
            else:
                at = idx_ref[0, slot]
                acc[at, 0] += real
                acc[at, 1] += imag
    if stage != "last":
        out_a[...] = acc[:cap]
        out_b[...] = acc[cap : 2 * cap]


def tick(stage, cap, idx, highs, lows, *data):
    devices = len(highs)
    sub = data[0].shape[2]
    slots = devices * LIVE
    tile_shape = lambda count: jax.ShapeDtypeStruct((count, 2, sub, TILE), jnp.float32)
    scratch = []
    if stage == "last":
        out_shape = tuple(tile_shape(LIVE) for _ in range(devices))
    else:
        out_shape = (tile_shape(cap), tile_shape(cap))
        if stage == "first":
            out_shape += (tile_shape(slots),)
        scratch = [pltpu.VMEM((2 * cap + 1, 2, sub, TILE), jnp.float32)]
    operands = (*highs, *lows, *data)
    return pl.pallas_call(
        functools.partial(tick_kernel, stage, devices, cap),
        out_shape=out_shape,
        in_specs=[SMEM] + [VMEM] * len(operands),
        out_specs=tuple(VMEM for _ in out_shape),
        scratch_shapes=scratch,
        compiler_params=pltpu.CompilerParams(vmem_limit_bytes=LIMIT),
        name="tick_" + stage,
    )(idx, *operands)


def finish_kernel(idx_ref, sources_ref, *refs):
    out_ref = refs[-1]
    terms = refs[:-1]
    out_ref[...] = sources_ref[...]
    sub = terms[0].shape[2]
    for j in range(LIVE):
        direction = idx_ref[0, j]
        start = pl.multiple_of(idx_ref[1, j] * TILE, TILE)
        for offset, term in enumerate(terms):
            shot = pl.multiple_of(idx_ref[2, offset] * sub, sub)
            for part in range(2):
                at = (direction, part, pl.ds(shot, sub), pl.ds(start, TILE))
                out_ref[at] += term[j, part]


def finish(idx, sources, terms):
    return pl.pallas_call(
        finish_kernel,
        out_shape=jax.ShapeDtypeStruct(sources.shape, sources.dtype),
        in_specs=[SMEM] + [VMEM] * (1 + len(terms)),
        out_specs=VMEM,
        compiler_params=pltpu.CompilerParams(vmem_limit_bytes=LIMIT),
        name="finish",
    )(idx, sources, *terms)


def body(sources, green, rowcol, counts):
    devices = lax.axis_size("tile")
    layers = lax.axis_size("layer")
    layer = lax.axis_index("layer")
    place = lax.axis_index("tile")
    width = sources.shape[-1]
    shots = sources.shape[3]
    sub = shots // devices
    tiles_dev = width // TILE
    tiles = tiles_dev * devices
    local = sources[0]
    cap = SIDE * devices
    cap_read = SIDE * devices

    order, codes = local_codes(rowcol[0], counts[0])
    packed = jnp.take(green[0], order, axis=0)

    def shots_of(device):
        return lax.dynamic_slice_in_dim(local, device * sub, sub, axis=2)

    pieces = [shots_of(place)]
    for offset in range(1, devices):
        pieces.append(swap_tile(shots_of(target_of(place, offset, devices)), offset))

    groups = gather_groups(packed)
    tray = jnp.zeros((layers * devices, 1, 128), jnp.int32)
    tray = tray + jnp.pad(codes, (0, 128 - LIVE))[None, None, :]
    tray = lax.all_to_all(tray, ("layer", "tile"), 0, 0, tiled=True)
    table = tray[:, 0, :LIVE].reshape(layers, devices, LIVE)
    idx, wanted, _ = lists(table, layer, place, tiles, cap, cap_read)

    picked = pick_tiles(wanted, pieces, tiles_dev, cap_read)
    src = swap_layers(*picked)
    highs, lows = zip(*[split_green(group) for group in groups])

    out_a, out_b, xs = tick("first", cap, idx, highs, lows, *src)
    for _ in range(TICKS - 3):
        got = swap_layers(out_a, out_b)
        out_a, out_b = tick("middle", cap, idx, highs, lows, xs, *got)
    got = swap_layers(out_a, out_b)
    terms = tick("last", cap, idx, highs, lows, xs, *got)

    back = [terms[0]]
    for offset in range(1, devices):
        home = offset if devices & (devices - 1) == 0 else devices - offset
        back.append(swap_tile(terms[offset], home))
    row_local = (codes >> 16) - place * tiles_dev
    live = codes & 1
    where = jnp.zeros((3, 16), jnp.int32)
    where = where.at[0, :LIVE].set(((codes >> 1) & 3) >> 1)
    where = where.at[1, :LIVE].set(jnp.where(live == 1, row_local, 0))
    shot_groups = jnp.stack([target_of(place, k, devices) for k in range(devices)])
    where = where.at[2, :devices].set(shot_groups)
    return finish(where, local, back)[None]


def solution(mesh):
    return jax.shard_map(
        body,
        mesh=mesh,
        in_specs=(
            P("layer", None, None, None, "tile"),
            P("layer", "tile", None, None, None),
            P("layer", "tile", None),
            P("layer", "tile"),
        ),
        out_specs=P("layer", None, None, None, "tile"),
        check_vma=False,
    )
```

time: 246 us -> 176 us (0.72)
  waiting for transfers between devices: 113 us -> 74.9 us
  Pallas kernels: 0 us -> 24.1 us
  matrix products: 23.1 us -> 0 us
  starting transfers between devices: 55.3 us -> 33.9 us
  other arithmetic: 23.8 us -> 16.5 us
  local copies, waits for them, and re-layouts: 29.6 us -> 24.4 us
    ppermute x20 -> x19, waiting for transfers between devices: 113 us -> 58.2 us  [the longest x5 30.8 us: swap_layers(): lax.ppermute(second, 'layer', both(even))]
    ppermute x20 -> x19, starting transfers between devices: 55.3 us -> 28.9 us  [the longest x5 15.1 us: swap_layers(): lax.ppermute(first, 'layer', both(odd))]
    pallas_call x0 -> x11, Pallas kernels: none -> 24.1 us  [the longest x5 11.3 us: tick(): pl.pallas_call(functools.partial(tick_kernel, stage, devices, cap), out_s...]
    dot_general x10 -> x0, matrix products: 23.1 us -> none  [the longest x5 14.8 us: complex_term(): prod = jnp.einsum(pattern, picked, blocks, precision=lax.Precision.HIGHEST)]
    all_to_all x0 -> x1, waiting for transfers between devices: none -> 16.7 us  [body(): tray = lax.all_to_all(tray, ('layer', 'tile'), 0, 0, tiled=True)]
    gather x11 -> x1, local copies, waits for them, and re-layouts: 15 us -> 1.67 us  [body(): packed = jnp.take(green[0], order, axis=0)]
    unnamed x6 -> x50, local copies, waits for them, and re-layouts: 0.01 us -> 12 us
    reshape x5 -> x0, local copies, waits for them, and re-layouts: 11.9 us -> none  [body(): waves = local_sources + update.reshape(2, 2, shots, width)]
  transfers between devices with their start and end apart: 20 -> 20, of which waited for: 19 -> 12; matrix products, arithmetic and copies ran while one was open for 4% -> 13% of each run, Pallas kernels for 0% -> 6%
where the time goes in v1:
time: 176 us; the launch traced here: 174 us
  waiting for transfers between devices  74.9 us (43%)
  starting transfers between devices  33.9 us (19%)
  local copies, waits for them, and re-layouts  24.4 us (14%)
  Pallas kernels  24.1 us (14%)
  other arithmetic  16.5 us (9%)
    ppermute x5, waiting for transfers between devices, swap_layers(): lax.ppermute(second, 'layer', both(even))  30.8 us
    ppermute x5, waiting for transfers between devices, swap_layers(): lax.ppermute(first, 'layer', both(odd))  23.1 us
    all_to_all x1, waiting for transfers between devices, body(): tray = lax.all_to_all(tray, ('layer', 'tile'), 0, 0, tiled=True)  16.7 us
    ppermute x5, starting transfers between devices, swap_layers(): lax.ppermute(first, 'layer', both(odd))  15.1 us
    unnamed x50, local copies, waits for them, and re-layouts  12 us
    pallas_call x5, Pallas kernels, tick(): pl.pallas_call(functools.partial(tick_kernel, stage, devices, cap), out_s...  11.3 us
    pallas_call x4, Pallas kernels, split_green(): pl.pallas_call(split_kernel, out_shape=(shape, shape), in_specs=[VMEM], o...  7.84 us
    ppermute x5, starting transfers between devices, swap_layers(): lax.ppermute(second, 'layer', both(even))  7.21 us
  transfers between devices with their start and end apart: 20, of which 12 were waited for; matrix products, arithmetic and copies ran while one was open for 13% of the time, Pallas kernels for 6%

profile of v1, /device:TPU:9, one launch (start us, length us, event | category | flops | bytes accessed | tf_op | source)
XLA Modules:
  0.0 174.4 jit_solution(15673316126918107860)
XLA Ops:
  0.0 0.9 select_reduce_fusion.7
  1.0 0.8 add_bitcast_fusion.1
  2.0 1.7 gather_fusion
  3.7 2.6 %broadcast_select_fusion.green_ref = f32[10,2,128,128]{3,2,1,0:T(8,128)} fusion(f32[10,2,128,128]{3,2,1,0:T(8,128)} %gather_fusion, pred[10]{0:T(512)(128)(4,1)S(1)} %compare_and_fusion), kind=kLoop, calls=%fused_computation.1 | loop fusion | flops 327680 | bytes 2621450 | tf_op jit(solution)/shard_map/jit(_take)/select_n | solution.py:326
  6.9 1.2 collective-permute-start.1
  8.7 5.0 %all-to-all-start = ((s32[32,1,128]{2,1,0:T(1,128)}), s32[32,1,128]{2,1,0:T(1,128)S(1)}, u32[]{:S(2)}, u32[]{:S(2)}) async-start(s32[32,1,128]{2,1,0:T(1,128)} %add.173), calls=%async_computation | async-start | bytes 32768 | tf_op jit(solution)/shard_map/all_to_all | solution.py:338
  13.8 2.1 %dynamic-slice_bitcast_fusion = (f32[2,2,8,2048]{3,2,1,0:T(8,128)}, f32[2,2,8,2048]{3,2,1,0:T(8,128)}, f32[2,2,8,2048]{3,2,1,0:T(8,128)S(1)}, f32[2,2,8,2048]{3,2,1,0:T(8,128)}) fusion(f32[1,2,2,32,2048]{4,3,2,1,0:T(8,128)} %param.10, s32[]{:T(128)S(6)} %select_n.259, s32[]{:T(128)S(6)} %select_n.257, s32[]{:T(128)S(6)} %select_n.256, s32[]{:T(128)S(6)} %select_n.258), kind=kLoop, calls=%fused_computation.4 | loop fusion | bytes 2097168 | tf_op jit(solution)/shard_map/dynamic_slice | solution.py:329
  16.3 1.2 collective-permute-start.4
  19.2 1.7 split_green.4
  20.9 0.9 copy-done.1
  21.8 16.7 %all-to-all-done = s32[32,1,128]{2,1,0:T(1,128)S(1)} async-done(((s32[32,1,128]{2,1,0:T(1,128)}), s32[32,1,128]{2,1,0:T(1,128)S(1)}, u32[]{:S(2)}, u32[]{:S(2)}) %all-to-all-start) | async-done | bytes 16416 | tf_op jit(solution)/shard_map/all_to_all | solution.py:338
  39.3 1.4 and.199
  40.6 1.3 broadcast_compare_fusion
  42.6 0.8 eq.164
  43.4 0.8 and.202
  44.1 0.8 shift_right_arithmetic.90
  44.9 1.8 %and_reduce_fusion.3 = (pred[8,64]{1,0:T(8,128)(4,1)S(1)}, pred[8,64]{1,0:T(8,128)(4,1)S(1)}, pred[8,64]{1,0:T(8,128)(4,1)S(1)}, pred[8,64]{1,0:T(8,128)(4,1)S(1...) fusion(pred[8,40]{1,0:T(8,128)(4,1)} %get-tuple-element.126, pred[8,40]{1,0:T(8,128)(4,1)S(1)} %eq.164, ...), kind=kLoop, calls=%fused_computation.15 | loop fusion | flops 243712 | bytes 47168 | tf_op jit(solution)/shard_map/reduce_or | solution.py:91
  46.9 1.1 multiply_reduce_fusion
  48.7 0.8 select_reduce_fusion
  50.0 1.2 select_n.255
  51.9 0.9 select_reduce_fusion.3
  53.9 0.9 select_reduce_fusion.1
  57.6 3.3 %pick_tiles.1 = (f32[32,2,8,128]{3,2,1,0:T(8,128)S(1)}, f32[32,2,8,128]{3,2,1,0:T(8,128)S(1)}) custom-call(s32[67]{0:T(128)S(1)} %pad_add_fusion.6.ids_ref, f32[2,2,8,2048]{3,2,1,0:T(8,128)S(1)} %get-tuple-element.108.refs_0_, f32[2,2,8,2048]{3,2,1,0:T(8,128)} %collective-permute-done.3.refs_1_, f32[2,2,8,2048]{3,2,1,0:T(8,128)} %collective-permute-done.4.refs_2_, ...), custom_call_target="tpu_custom_call" | custom-call | tf_op jit(solution)/shard_map/pick_tiles/pallas_call | solution.py:194
  60.8 3.0 %collective-permute-start.6 = (f32[32,2,8,128]{3,2,1,0:T(8,128)S(1)}, f32[32,2,8,128]{3,2,1,0:T(8,128)S(1)}, u32[]{:S(2)}, u32[]{:S(2)}) collective-permute-start(f32[32,2,8,128]{3,2,1,0:T(8,128)S(1)} %get-tuple-element.72), channel_id=1, source_target_pairs={{4,8},{12,16},{20,24},{8,4},{16,12},{24,20},{5,9},{13,17},{21,25},... | collective-permute-start | bytes 786440 | tf_op jit(solution)/shard_map/ppermute | solution.py:59
  63.9 1.4 collective-permute-start.7
  65.5 1.7 split_green.6
  67.2 2.2 %split_green.5 = (bf16[10,128,256]{2,1,0:T(8,128)(2,1)S(1)}, bf16[10,128,256]{2,1,0:T(8,128)(2,1)S(1)}) custom-call(f32[10,2,128,128]{3,2,1,0:T(8,128)} %collective-permute-done.green_ref), custom_call_target="tpu_custom_call" | custom-call | tf_op jit(solution)/shard_map/split_green/pallas_call | solution.py:157
  69.5 2.2 %split_green.7 = (bf16[10,128,256]{2,1,0:T(8,128)(2,1)S(1)}, bf16[10,128,256]{2,1,0:T(8,128)(2,1)S(1)}) custom-call(f32[10,2,128,128]{3,2,1,0:T(8,128)} %collective-permute-done.2.green_ref), custom_call_target="tpu_custom_call" | custom-call | tf_op jit(solution)/shard_map/split_green/pallas_call | solution.py:157
  71.7 0.8 copy-done.14
  72.5 5.0 %collective-permute-done.7.refs_9_ = f32[32,2,8,128]{3,2,1,0:T(8,128)S(1)} collective-permute-done((f32[32,2,8,128]{3,2,1,0:T(8,128)S(1)}, f32[32,2,8,128]{3,2,1,0:T(8,128)S(1)}, u32[]{:S(2)}, u32[]{:S(2)}) %collective-permute-start.7) | collective-permute-done | bytes 262176 | tf_op jit(solution)/shard_map/ppermute | solution.py:59
  77.5 2.0 %tick_first.1 = (f32[32,2,8,128]{3,2,1,0:T(8,128)S(1)}, f32[32,2,8,128]{3,2,1,0:T(8,128)S(1)}, f32[40,2,8,128]{3,2,1,0:T(8,128)S(1)}) custom-call(s32[3,40]{1,0:T(4,128)S(1)} %pad_add_fusion.5.idx_ref, bf16[10,128,256]{2,1,0:T(8,128)(2,1)S(1)} %get-tuple-element.64.refs_0_, bf16[10,128,256]{2,1,0:T(8,128)(2,1)S(1)} %get-tuple-element.65.refs_1_, ...), custom_call_target="tpu_custom_call" | custom-call | tf_op jit(solution)/shard_map/tick_first/pallas_call | solution.py:274
  79.5 3.0 %collective-permute-start.8 = (f32[32,2,8,128]{3,2,1,0:T(8,128)S(1)}, f32[32,2,8,128]{3,2,1,0:T(8,128)S(1)}, u32[]{:S(2)}, u32[]{:S(2)}) collective-permute-start(f32[32,2,8,128]{3,2,1,0:T(8,128)S(1)} %get-tuple-element.75), channel_id=1, source_target_pairs={{4,8},{12,16},{20,24},{8,4},{16,12},{24,20},{5,9},{13,17},{21,25},... | collective-permute-start | bytes 786440 | tf_op jit(solution)/shard_map/ppermute | solution.py:59
  82.5 1.4 collective-permute-start.9
  84.0 5.8 %collective-permute-done.8.refs_9_ = f32[32,2,8,128]{3,2,1,0:T(8,128)S(1)} collective-permute-done((f32[32,2,8,128]{3,2,1,0:T(8,128)S(1)}, f32[32,2,8,128]{3,2,1,0:T(8,128)S(1)}, u32[]{:S(2)}, u32[]{:S(2)}) %collective-permute-start.8) | collective-permute-done | bytes 262176 | tf_op jit(solution)/shard_map/ppermute | solution.py:59
  89.8 6.4 %collective-permute-done.9.refs_10_ = f32[32,2,8,128]{3,2,1,0:T(8,128)S(1)} collective-permute-done((f32[32,2,8,128]{3,2,1,0:T(8,128)S(1)}, f32[32,2,8,128]{3,2,1,0:T(8,128)S(1)}, u32[]{:S(2)}, u32[]{:S(2)}) %collective-permute-start.9) | collective-permute-done | bytes 262176 | tf_op jit(solution)/shard_map/ppermute | solution.py:59
  96.2 2.0 %tick_middle.3 = (f32[32,2,8,128]{3,2,1,0:T(8,128)S(1)}, f32[32,2,8,128]{3,2,1,0:T(8,128)S(1)}) custom-call(s32[3,40]{1,0:T(4,128)S(1)} %pad_add_fusion.5.idx_ref, bf16[10,128,256]{2,1,0:T(8,128)(2,1)S(1)} %get-tuple-element.64.refs_0_, bf16[10,128,256]{2,1,0:T(8,128)(2,1)S(1)} %get-tuple-element.65.refs_1_, ...), custom_call_target="tpu_custom_call" | custom-call | tf_op jit(solution)/shard_map/tick_middle/pallas_call | solution.py:274
  98.1 3.0 %collective-permute-start.10 = (f32[32,2,8,128]{3,2,1,0:T(8,128)S(1)}, f32[32,2,8,128]{3,2,1,0:T(8,128)S(1)}, u32[]{:S(2)}, u32[]{:S(2)}) collective-permute-start(f32[32,2,8,128]{3,2,1,0:T(8,128)S(1)} %get-tuple-element.77), channel_id=1, source_target_pairs={{4,8},{12,16},{20,24},{8,4},{16,12},{24,20},{5,9},{13,17},{21,25},... | collective-permute-start | bytes 786440 | tf_op jit(solution)/shard_map/ppermute | solution.py:59
  101.2 1.4 collective-permute-start.11
  102.6 5.8 %collective-permute-done.10.refs_9_ = f32[32,2,8,128]{3,2,1,0:T(8,128)S(1)} collective-permute-done((f32[32,2,8,128]{3,2,1,0:T(8,128)S(1)}, f32[32,2,8,128]{3,2,1,0:T(8,128)S(1)}, u32[]{:S(2)}, u32[]{:S(2)}) %collective-permute-start.10) | collective-permute-done | bytes 262176 | tf_op jit(solution)/shard_map/ppermute | solution.py:59
  108.4 6.4 %collective-permute-done.11.refs_10_ = f32[32,2,8,128]{3,2,1,0:T(8,128)S(1)} collective-permute-done((f32[32,2,8,128]{3,2,1,0:T(8,128)S(1)}, f32[32,2,8,128]{3,2,1,0:T(8,128)S(1)}, u32[]{:S(2)}, u32[]{:S(2)}) %collective-permute-start.11) | collective-permute-done | bytes 262176 | tf_op jit(solution)/shard_map/ppermute | solution.py:59
  114.8 2.0 %tick_middle.4 = (f32[32,2,8,128]{3,2,1,0:T(8,128)S(1)}, f32[32,2,8,128]{3,2,1,0:T(8,128)S(1)}) custom-call(s32[3,40]{1,0:T(4,128)S(1)} %pad_add_fusion.5.idx_ref, bf16[10,128,256]{2,1,0:T(8,128)(2,1)S(1)} %get-tuple-element.64.refs_0_, bf16[10,128,256]{2,1,0:T(8,128)(2,1)S(1)} %get-tuple-element.65.refs_1_, ...), custom_call_target="tpu_custom_call" | custom-call | tf_op jit(solution)/shard_map/tick_middle/pallas_call | solution.py:274
  116.8 3.0 %collective-permute-start.12 = (f32[32,2,8,128]{3,2,1,0:T(8,128)S(1)}, f32[32,2,8,128]{3,2,1,0:T(8,128)S(1)}, u32[]{:S(2)}, u32[]{:S(2)}) collective-permute-start(f32[32,2,8,128]{3,2,1,0:T(8,128)S(1)} %get-tuple-element.79), channel_id=1, source_target_pairs={{4,8},{12,16},{20,24},{8,4},{16,12},{24,20},{5,9},{13,17},{21,25},... | collective-permute-start | bytes 786440 | tf_op jit(solution)/shard_map/ppermute | solution.py:59
  119.8 1.4 collective-permute-start.13
  121.2 5.7 %collective-permute-done.12.refs_9_ = f32[32,2,8,128]{3,2,1,0:T(8,128)S(1)} collective-permute-done((f32[32,2,8,128]{3,2,1,0:T(8,128)S(1)}, f32[32,2,8,128]{3,2,1,0:T(8,128)S(1)}, u32[]{:S(2)}, u32[]{:S(2)}) %collective-permute-start.12) | collective-permute-done | bytes 262176 | tf_op jit(solution)/shard_map/ppermute | solution.py:59
  127.0 6.4 %collective-permute-done.13.refs_10_ = f32[32,2,8,128]{3,2,1,0:T(8,128)S(1)} collective-permute-done((f32[32,2,8,128]{3,2,1,0:T(8,128)S(1)}, f32[32,2,8,128]{3,2,1,0:T(8,128)S(1)}, u32[]{:S(2)}, u32[]{:S(2)}) %collective-permute-start.13) | collective-permute-done | bytes 262176 | tf_op jit(solution)/shard_map/ppermute | solution.py:59
  133.4 2.8 %tick_middle.5 = (f32[32,2,8,128]{3,2,1,0:T(8,128)}, f32[32,2,8,128]{3,2,1,0:T(8,128)}) custom-call(s32[3,40]{1,0:T(4,128)S(1)} %pad_add_fusion.5.idx_ref, bf16[10,128,256]{2,1,0:T(8,128)(2,1)S(1)} %get-tuple-element.64.refs_0_, bf16[10,128,256]{2,1,0:T(8,128)(2,1)S(1)} %get-tuple-element.65.refs_1_, bf16[10,128,256]{2,1,0:T(8,128)(2,1)S(1)} %get-tuple-element.66.refs_2_, ...), custom_call_target="tpu_custom_call" | custom-call | tf_op jit(solution)/shard_map/tick_middle/pallas_call | solution.py:274
  136.2 3.0 %collective-permute-start.14 = (f32[32,2,8,128]{3,2,1,0:T(8,128)}, f32[32,2,8,128]{3,2,1,0:T(8,128)S(1)}, u32[]{:S(2)}, u32[]{:S(2)}) collective-permute-start(f32[32,2,8,128]{3,2,1,0:T(8,128)} %get-tuple-element.81), channel_id=1, source_target_pairs={{4,8},{12,16},{20,24},{8,4},{16,12},{24,20},{5,9},{13,17},{21,25},... | collective-permute-start | bytes 786440 | tf_op jit(solution)/shard_map/ppermute | solution.py:59
  139.2 1.4 collective-permute-start.15
  140.8 5.8 %collective-permute-done.14.refs_9_ = f32[32,2,8,128]{3,2,1,0:T(8,128)S(1)} collective-permute-done((f32[32,2,8,128]{3,2,1,0:T(8,128)}, f32[32,2,8,128]{3,2,1,0:T(8,128)S(1)}, u32[]{:S(2)}, u32[]{:S(2)}) %collective-permute-start.14) | collective-permute-done | bytes 262176 | tf_op jit(solution)/shard_map/ppermute | solution.py:59
  146.6 6.5 %collective-permute-done.15.refs_10_ = f32[32,2,8,128]{3,2,1,0:T(8,128)} collective-permute-done((f32[32,2,8,128]{3,2,1,0:T(8,128)}, f32[32,2,8,128]{3,2,1,0:T(8,128)}, u32[]{:S(2)}, u32[]{:S(2)}) %collective-permute-start.15) | collective-permute-done | bytes 262176 | tf_op jit(solution)/shard_map/ppermute | solution.py:59
  153.1 1.1 copy-done.3
  154.2 1.1 copy-done.5
  155.3 1.1 copy-done.7
  156.4 1.1 copy-done.9
  157.5 1.1 copy-done.11
  158.6 1.1 copy-done.13
  159.7 1.0 copy-done.16
  160.6 2.6 %tick_last.1 = (f32[10,2,8,128]{3,2,1,0:T(8,128)S(1)}, f32[10,2,8,128]{3,2,1,0:T(8,128)}, f32[10,2,8,128]{3,2,1,0:T(8,128)}, f32[10,2,8,128]{3,2,1,0:T(8,128)}) custom-call(s32[3,40]{1,0:T(4,128)S(1)} %pad_add_fusion.5.idx_ref, bf16[10,128,256]{2,1,0:T(8,128)(2,1)S(1)} %get-tuple-element.64.refs_0_, bf16[10,128,256]{2,1,0:T(8,128)(2,1)S(1)} %copy-done.9, ...), custom_call_target="tpu_custom_call" | custom-call | tf_op jit(solution)/shard_map/tick_last/pallas_call | solution.py:274
  164.4 1.3 collective-permute-start.17
  166.2 2.4 %collective-permute-done.17.refs_2_ = f32[10,2,8,128]{3,2,1,0:T(8,128)S(1)} collective-permute-done((f32[10,2,8,128]{3,2,1,0:T(8,128)}, f32[10,2,8,128]{3,2,1,0:T(8,128)S(1)}, u32[]{:S(2)}, u32[]{:S(2)}) %collective-permute-start.17) | collective-permute-done | bytes 81952 | tf_op jit(solution)/shard_map/ppermute | solution.py:28
  168.6 1.9 %collective-permute-done.18.refs_3_ = f32[10,2,8,128]{3,2,1,0:T(8,128)S(1)} collective-permute-done((f32[10,2,8,128]{3,2,1,0:T(8,128)}, f32[10,2,8,128]{3,2,1,0:T(8,128)S(1)}, u32[]{:S(2)}, u32[]{:S(2)}) %collective-permute-start.18) | collective-permute-done | bytes 81952 | tf_op jit(solution)/shard_map/ppermute | solution.py:28
  170.5 1.2 copy-done.17
  171.7 0.9 copy-done.19
  172.6 1.8 %finish.1 = f32[2,2,32,2048]{3,2,1,0:T(8,128)} custom-call(s32[3,16]{1,0:T(4,128)S(1)} %scatter.14.idx_ref, f32[2,2,32,2048]{3,2,1,0:T(8,128)S(1)} %bitcast.93, f32[10,2,8,128]{3,2,1,0:T(8,128)S(1)} %copy-done.19, f32[10,2,8,128]{3,2,1,0:T(8,128)S(1)} %collective-permute-done.16.refs_1_, f32[10,2,8,128]{3,2,1,0:T(8,128)S(1)} %collective-permute-done.17.refs_2_, ...), custom_call_target="tpu_custom_call" | custom-call | tf_op jit(solution)/shard_map/finish/pallas_call | solution.py:301
  (102 shorter events, 13.0 us)
Async XLA Ops:
  0.0 2.0 %copy-start = (f32[1,20,2,128,128]{4,3,2,1,0:T(8,128)S(1)}, f32[1,20,2,128,128]{4,3,2,1,0:T(8,128)}, u32[]{:S(2)}) copy-start(f32[1,20,2,128,128]{4,3,2,1,0:T(8,128)} %param.11) | copy-start | bytes 7864324
  1.9 6.2 %copy-start.20 = (s32[10]{0:T(128)}, s32[10]{0:T(128)S(1)}, u32[]{:S(2)}) copy-start(s32[10]{0:T(128)S(1)} %get-tuple-element.99) | copy-start | bytes 124
  6.2 61.0 %collective-permute-start = (f32[10,2,128,128]{3,2,1,0:T(8,128)}, f32[10,2,128,128]{3,2,1,0:T(8,128)}, u32[]{:S(2)}, u32[]{:S(2)}) collective-permute-start(f32[10,2,128,128]{3,2,1,0:T(8,128)} %broadcast_select_fusion.green_ref), channel_id=1, source_target_pairs={{0,1},{1,0},{2,3},{3,2},{4,5},{5,4},{6,7},{7,6},{8,9},{9,8},{10,11... | collective-permute-start | bytes 3932168 | tf_op jit(solution)/shard_map/ppermute | solution.py:28
  6.9 46.6 %collective-permute-start.1 = (f32[10,2,128,128]{3,2,1,0:T(8,128)}, f32[10,2,128,128]{3,2,1,0:T(8,128)}, u32[]{:S(2)}, u32[]{:S(2)}) collective-permute-start(f32[10,2,128,128]{3,2,1,0:T(8,128)} %broadcast_select_fusion.green_ref), channel_id=1, source_target_pairs={{0,2},{1,3},{2,0},{3,1},{4,6},{5,7},{6,4},{7,5},{8,10},{9,11},{10,... | collective-permute-start | bytes 3932168 | tf_op jit(solution)/shard_map/ppermute | solution.py:28
  8.7 29.8 %all-to-all-start = ((s32[32,1,128]{2,1,0:T(1,128)}), s32[32,1,128]{2,1,0:T(1,128)S(1)}, u32[]{:S(2)}, u32[]{:S(2)}) async-start(s32[32,1,128]{2,1,0:T(1,128)} %add.173), calls=%async_computation | async-start | bytes 32768 | tf_op jit(solution)/shard_map/all_to_all | solution.py:338
  15.9 41.7 %collective-permute-start.3 = (f32[2,2,8,2048]{3,2,1,0:T(8,128)}, f32[2,2,8,2048]{3,2,1,0:T(8,128)}, u32[]{:S(2)}, u32[]{:S(2)}) collective-permute-start(f32[2,2,8,2048]{3,2,1,0:T(8,128)} %get-tuple-element.107), channel_id=1, source_target_pairs={{0,1},{1,0},{2,3},{3,2},{4,5},{5,4},{6,7},{7,6},{8,9},{9,8},{10,11... | collective-permute-start | bytes 786440 | tf_op jit(solution)/shard_map/ppermute | solution.py:28
  16.3 41.3 %collective-permute-start.4 = (f32[2,2,8,2048]{3,2,1,0:T(8,128)}, f32[2,2,8,2048]{3,2,1,0:T(8,128)}, u32[]{:S(2)}, u32[]{:S(2)}) collective-permute-start(f32[2,2,8,2048]{3,2,1,0:T(8,128)} %get-tuple-element.109), channel_id=1, source_target_pairs={{0,2},{1,3},{2,0},{3,1},{4,6},{5,7},{6,4},{7,5},{8,10},{9,11},{10,... | collective-permute-start | bytes 786440 | tf_op jit(solution)/shard_map/ppermute | solution.py:28
  17.4 40.1 %collective-permute-start.5 = (f32[2,2,8,2048]{3,2,1,0:T(8,128)}, f32[2,2,8,2048]{3,2,1,0:T(8,128)}, u32[]{:S(2)}, u32[]{:S(2)}) collective-permute-start(f32[2,2,8,2048]{3,2,1,0:T(8,128)} %get-tuple-element.106), channel_id=1, source_target_pairs={{0,3},{1,2},{2,1},{3,0},{4,7},{5,6},{6,5},{7,4},{8,11},{9,10},{10,... | collective-permute-start | bytes 786440 | tf_op jit(solution)/shard_map/ppermute | solution.py:28
  20.9 0.9 copy-start.1
  53.5 16.0 %collective-permute-start.2 = (f32[10,2,128,128]{3,2,1,0:T(8,128)}, f32[10,2,128,128]{3,2,1,0:T(8,128)}, u32[]{:S(2)}, u32[]{:S(2)}) collective-permute-start(f32[10,2,128,128]{3,2,1,0:T(8,128)} %collective-permute-done.1.green_ref), channel_id=1, source_target_pairs={{0,1},{1,0},{2,3},{3,2},{4,5},{5,4},{6,7},{7,6},{8,9},{9,8},{10,11... | collective-permute-start | bytes 3932168 | tf_op jit(solution)/shard_map/ppermute | solution.py:28
  60.8 11.7 %collective-permute-start.6 = (f32[32,2,8,128]{3,2,1,0:T(8,128)S(1)}, f32[32,2,8,128]{3,2,1,0:T(8,128)S(1)}, u32[]{:S(2)}, u32[]{:S(2)}) collective-permute-start(f32[32,2,8,128]{3,2,1,0:T(8,128)S(1)} %get-tuple-element.72), channel_id=1, source_target_pairs={{4,8},{12,16},{20,24},{8,4},{16,12},{24,20},{5,9},{13,17},{21,25},... | collective-permute-start | bytes 786440 | tf_op jit(solution)/shard_map/ppermute | solution.py:59
  63.9 13.6 %collective-permute-start.7 = (f32[32,2,8,128]{3,2,1,0:T(8,128)S(1)}, f32[32,2,8,128]{3,2,1,0:T(8,128)S(1)}, u32[]{:S(2)}, u32[]{:S(2)}) collective-permute-start(f32[32,2,8,128]{3,2,1,0:T(8,128)S(1)} %get-tuple-element.73), channel_id=1, source_target_pairs={{0,4},{8,12},{16,20},{24,28},{4,0},{12,8},{20,16},{28,24},{1,5},{9... | collective-permute-start | bytes 786440 | tf_op jit(solution)/shard_map/ppermute | solution.py:59
  67.2 66.2 %copy-start.4 = (bf16[10,128,256]{2,1,0:T(8,128)(2,1)}, bf16[10,128,256]{2,1,0:T(8,128)(2,1)S(1)}, u32[]{:S(2)}) copy-start(bf16[10,128,256]{2,1,0:T(8,128)(2,1)S(1)} %get-tuple-element.66.refs_2_) | copy-start | bytes 1966084
  67.2 66.2 %copy-start.6 = (bf16[10,128,256]{2,1,0:T(8,128)(2,1)}, bf16[10,128,256]{2,1,0:T(8,128)(2,1)S(1)}, u32[]{:S(2)}) copy-start(bf16[10,128,256]{2,1,0:T(8,128)(2,1)S(1)} %get-tuple-element.70.refs_6_) | copy-start | bytes 1966084
  67.2 10.3 %copy-start.2 = (bf16[10,128,256]{2,1,0:T(8,128)(2,1)S(1)}, bf16[10,128,256]{2,1,0:T(8,128)(2,1)}, u32[]{:S(2)}) copy-start(bf16[10,128,256]{2,1,0:T(8,128)(2,1)} %copy-done.1) | copy-start | bytes 1966084
  69.5 64.0 %copy-start.8 = (bf16[10,128,256]{2,1,0:T(8,128)(2,1)}, bf16[10,128,256]{2,1,0:T(8,128)(2,1)S(1)}, u32[]{:S(2)}) copy-start(bf16[10,128,256]{2,1,0:T(8,128)(2,1)S(1)} %get-tuple-element.65.refs_1_) | copy-start | bytes 1966084
  69.5 63.9 %copy-start.10 = (bf16[10,128,256]{2,1,0:T(8,128)(2,1)}, bf16[10,128,256]{2,1,0:T(8,128)(2,1)S(1)}, u32[]{:S(2)}) copy-start(bf16[10,128,256]{2,1,0:T(8,128)(2,1)S(1)} %get-tuple-element.69.refs_5_) | copy-start | bytes 1966084
  71.7 0.8 copy-start.14
  72.5 60.9 %copy-start.12 = (bf16[10,128,256]{2,1,0:T(8,128)(2,1)}, bf16[10,128,256]{2,1,0:T(8,128)(2,1)S(1)}, u32[]{:S(2)}) copy-start(bf16[10,128,256]{2,1,0:T(8,128)(2,1)S(1)} %get-tuple-element.67.refs_3_) | copy-start | bytes 1966084
  79.5 53.9 %copy-start.15 = (f32[40,2,8,128]{3,2,1,0:T(8,128)}, f32[40,2,8,128]{3,2,1,0:T(8,128)S(1)}, u32[]{:S(2)}) copy-start(f32[40,2,8,128]{3,2,1,0:T(8,128)S(1)} %get-tuple-element.74.refs_8_) | copy-start | bytes 983044
  79.5 10.2 %collective-permute-start.8 = (f32[32,2,8,128]{3,2,1,0:T(8,128)S(1)}, f32[32,2,8,128]{3,2,1,0:T(8,128)S(1)}, u32[]{:S(2)}, u32[]{:S(2)}) collective-permute-start(f32[32,2,8,128]{3,2,1,0:T(8,128)S(1)} %get-tuple-element.75), channel_id=1, source_target_pairs={{4,8},{12,16},{20,24},{8,4},{16,12},{24,20},{5,9},{13,17},{21,25},... | collective-permute-start | bytes 786440 | tf_op jit(solution)/shard_map/ppermute | solution.py:59
  82.5 13.6 %collective-permute-start.9 = (f32[32,2,8,128]{3,2,1,0:T(8,128)S(1)}, f32[32,2,8,128]{3,2,1,0:T(8,128)S(1)}, u32[]{:S(2)}, u32[]{:S(2)}) collective-permute-start(f32[32,2,8,128]{3,2,1,0:T(8,128)S(1)} %get-tuple-element.76), channel_id=1, source_target_pairs={{0,4},{8,12},{16,20},{24,28},{4,0},{12,8},{20,16},{28,24},{1,5},{9... | collective-permute-start | bytes 786440 | tf_op jit(solution)/shard_map/ppermute | solution.py:59
  98.1 10.2 %collective-permute-start.10 = (f32[32,2,8,128]{3,2,1,0:T(8,128)S(1)}, f32[32,2,8,128]{3,2,1,0:T(8,128)S(1)}, u32[]{:S(2)}, u32[]{:S(2)}) collective-permute-start(f32[32,2,8,128]{3,2,1,0:T(8,128)S(1)} %get-tuple-element.77), channel_id=1, source_target_pairs={{4,8},{12,16},{20,24},{8,4},{16,12},{24,20},{5,9},{13,17},{21,25},... | collective-permute-start | bytes 786440 | tf_op jit(solution)/shard_map/ppermute | solution.py:59
  101.2 13.6 %collective-permute-start.11 = (f32[32,2,8,128]{3,2,1,0:T(8,128)S(1)}, f32[32,2,8,128]{3,2,1,0:T(8,128)S(1)}, u32[]{:S(2)}, u32[]{:S(2)}) collective-permute-start(f32[32,2,8,128]{3,2,1,0:T(8,128)S(1)} %get-tuple-element.78), channel_id=1, source_target_pairs={{0,4},{8,12},{16,20},{24,28},{4,0},{12,8},{20,16},{28,24},{1,5},{9... | collective-permute-start | bytes 786440 | tf_op jit(solution)/shard_map/ppermute | solution.py:59
  116.8 10.2 %collective-permute-start.12 = (f32[32,2,8,128]{3,2,1,0:T(8,128)S(1)}, f32[32,2,8,128]{3,2,1,0:T(8,128)S(1)}, u32[]{:S(2)}, u32[]{:S(2)}) collective-permute-start(f32[32,2,8,128]{3,2,1,0:T(8,128)S(1)} %get-tuple-element.79), channel_id=1, source_target_pairs={{4,8},{12,16},{20,24},{8,4},{16,12},{24,20},{5,9},{13,17},{21,25},... | collective-permute-start | bytes 786440 | tf_op jit(solution)/shard_map/ppermute | solution.py:59
  119.8 20.9 %copy-start.21 = (s32[10]{0:T(128)S(1)}, s32[10]{0:T(128)}, u32[]{:S(2)}) copy-start(s32[10]{0:T(128)} %copy-done.20) | copy-start | bytes 124
  119.8 13.6 %collective-permute-start.13 = (f32[32,2,8,128]{3,2,1,0:T(8,128)S(1)}, f32[32,2,8,128]{3,2,1,0:T(8,128)S(1)}, u32[]{:S(2)}, u32[]{:S(2)}) collective-permute-start(f32[32,2,8,128]{3,2,1,0:T(8,128)S(1)} %get-tuple-element.80), channel_id=1, source_target_pairs={{0,4},{8,12},{16,20},{24,28},{4,0},{12,8},{20,16},{28,24},{1,5},{9... | collective-permute-start | bytes 786440 | tf_op jit(solution)/shard_map/ppermute | solution.py:59
  136.2 10.4 %collective-permute-start.14 = (f32[32,2,8,128]{3,2,1,0:T(8,128)}, f32[32,2,8,128]{3,2,1,0:T(8,128)S(1)}, u32[]{:S(2)}, u32[]{:S(2)}) collective-permute-start(f32[32,2,8,128]{3,2,1,0:T(8,128)} %get-tuple-element.81), channel_id=1, source_target_pairs={{4,8},{12,16},{20,24},{8,4},{16,12},{24,20},{5,9},{13,17},{21,25},... | collective-permute-start | bytes 786440 | tf_op jit(solution)/shard_map/ppermute | solution.py:59
  139.2 13.9 %collective-permute-start.15 = (f32[32,2,8,128]{3,2,1,0:T(8,128)}, f32[32,2,8,128]{3,2,1,0:T(8,128)}, u32[]{:S(2)}, u32[]{:S(2)}) collective-permute-start(f32[32,2,8,128]{3,2,1,0:T(8,128)} %get-tuple-element.82), channel_id=1, source_target_pairs={{0,4},{8,12},{16,20},{24,28},{4,0},{12,8},{20,16},{28,24},{1,5},{9... | collective-permute-start | bytes 786440 | tf_op jit(solution)/shard_map/ppermute | solution.py:59
  153.1 1.1 copy-start.3
  154.2 1.1 copy-start.5
  155.3 1.1 copy-start.7
  156.4 1.1 copy-start.9
  157.5 1.1 copy-start.11
  158.6 1.1 copy-start.13
  159.7 1.0 copy-start.16
  163.2 0.6 copy-start.18
  163.9 2.3 %collective-permute-start.16 = (f32[10,2,8,128]{3,2,1,0:T(8,128)}, f32[10,2,8,128]{3,2,1,0:T(8,128)S(1)}, u32[]{:S(2)}, u32[]{:S(2)}) collective-permute-start(f32[10,2,8,128]{3,2,1,0:T(8,128)} %get-tuple-element.84), channel_id=1, source_target_pairs={{0,1},{1,0},{2,3},{3,2},{4,5},{5,4},{6,7},{7,6},{8,9},{9,8},{10,11... | collective-permute-start | bytes 245768 | tf_op jit(solution)/shard_map/ppermute | solution.py:28
  164.4 4.3 %collective-permute-start.17 = (f32[10,2,8,128]{3,2,1,0:T(8,128)}, f32[10,2,8,128]{3,2,1,0:T(8,128)S(1)}, u32[]{:S(2)}, u32[]{:S(2)}) collective-permute-start(f32[10,2,8,128]{3,2,1,0:T(8,128)} %get-tuple-element.85), channel_id=1, source_target_pairs={{0,2},{1,3},{2,0},{3,1},{4,6},{5,7},{6,4},{7,5},{8,10},{9,11},{10,... | collective-permute-start | bytes 245768 | tf_op jit(solution)/shard_map/ppermute | solution.py:28
  165.6 4.9 %collective-permute-start.18 = (f32[10,2,8,128]{3,2,1,0:T(8,128)}, f32[10,2,8,128]{3,2,1,0:T(8,128)S(1)}, u32[]{:S(2)}, u32[]{:S(2)}) collective-permute-start(f32[10,2,8,128]{3,2,1,0:T(8,128)} %get-tuple-element.86), channel_id=1, source_target_pairs={{0,3},{1,2},{2,1},{3,0},{4,7},{5,6},{6,5},{7,4},{8,11},{9,10},{10,... | collective-permute-start | bytes 245768 | tf_op jit(solution)/shard_map/ppermute | solution.py:28
  170.5 1.2 copy-start.17
  171.7 0.9 copy-start.19

commit v2 on v0

v2 whole, which is shorter than its diff:
```python
import functools

import jax
import jax.numpy as jnp
from jax import lax
from jax.experimental import pallas as pl
from jax.experimental.pallas import tpu as pltpu
from jax.sharding import PartitionSpec as P

TILE = 128
CAP = 5
TICKS = 6
KINDS = 4
SLOTS = KINDS * CAP
LIVE = 2 * CAP
HALF = LIVE // 2
SIDE = 2 * CAP - 2
STRIDE = 16
SHORT = 12
SHORT_READ = 9
SHIFT = 1024

VMEM = pl.BlockSpec(memory_space=pltpu.VMEM)
SMEM = pl.BlockSpec(memory_space=pltpu.SMEM)
ANY = pl.BlockSpec(memory_space=pl.ANY)
PARAMS = pltpu.CompilerParams(vmem_limit_bytes=24 * 1024 * 1024)


def is_power(count):
    return count & (count - 1) == 0


def swap_tile(block, offset):
    count = lax.axis_size("tile")
    partner = (lambda i: i ^ offset) if is_power(count) else (lambda i: (i + offset) % count)
    return lax.ppermute(block, "tile", [(i, partner(i)) for i in range(count)])


def source_of(place, offset, count):
    return place ^ offset if is_power(count) else lax.rem(place - offset + count, count)


def target_of(place, offset, count):
    return place ^ offset if is_power(count) else lax.rem(place + offset, count)


def gather_groups(own):
    count = lax.axis_size("tile")
    groups = {0: own}
    if is_power(count):
        bit = count // 2
        while bit:
            for offset in list(groups):
                groups[offset ^ bit] = swap_tile(groups[offset], bit)
            bit //= 2
    else:
        for offset in range(1, count):
            groups[offset] = swap_tile(own, offset)
    return [groups[offset] for offset in range(count)]


def swap_layers(first, second):
    layers = lax.axis_size("layer")
    odd = [(i, i + 1) for i in range(1, layers - 1, 2)]
    even = [(i, i + 1) for i in range(0, layers - 1, 2)]
    both = lambda pairs: pairs + [(b, a) for a, b in pairs]
    return lax.ppermute(first, "layer", both(odd)), lax.ppermute(second, "layer", both(even))


def prepare_kernel(tiles_dev, where_ref, rowcol_ref, counts_ref, green_ref, codes_ref, rows_ref, *refs):
    halves, order_ref, sems = refs[:2], refs[2], refs[3]
    place = where_ref[1]

    def scan(want_live, rank):
        for slot in range(SLOTS):
            live = counts_ref[slot // CAP] > slot % CAP

            @pl.when((live == want_live) & (rank < LIVE))
            def _():
                order_ref[rank] = slot

            rank = rank + (live == want_live).astype(jnp.int32)
        return rank

    live_slots = scan(True, jnp.int32(0))
    scan(False, live_slots)
    copies = []
    for j in range(LIVE):
        copy = pltpu.make_async_copy(green_ref.at[order_ref[j]], halves[j // HALF].at[j % HALF], sems.at[j])
        copy.start()
        copies.append(copy)
    lanes = codes_ref.shape[-1]
    lane = lax.broadcasted_iota(jnp.int32, (1, lanes), 1)
    codes = jnp.zeros((1, lanes), jnp.int32)
    for j in range(LIVE):
        slot = order_ref[j]
        kind = lax.div(slot, CAP)
        alive = j < live_slots
        code = rowcol_ref[slot, 0] * 65536 + rowcol_ref[slot, 1] * 8 + kind * 2 + 1
        code = jnp.where(alive, code, 0)
        codes = jnp.where(lane == place * STRIDE + j, code, codes)
        rows_ref[0, j] = lax.shift_right_logical(kind, 1)
        rows_ref[1, j] = jnp.where(alive, rowcol_ref[slot, 0] - place * tiles_dev, 0)
    codes_ref[...] = jnp.broadcast_to(codes[None], codes_ref.shape)
    for copy in copies:
        copy.wait()


def prepare(where, pairs, live_counts, green, receivers, lanes, tiles_dev):
    half = jax.ShapeDtypeStruct((HALF,) + green.shape[1:], green.dtype)
    return pl.pallas_call(
        functools.partial(prepare_kernel, tiles_dev),
        out_shape=(
            jax.ShapeDtypeStruct((receivers, 1, lanes), jnp.int32),
            jax.ShapeDtypeStruct((2, STRIDE), jnp.int32),
            half,
            half,
        ),
        in_specs=[SMEM, SMEM, SMEM, ANY],
        out_specs=(VMEM, SMEM, VMEM, VMEM),
        scratch_shapes=[pltpu.SMEM((SLOTS,), jnp.int32), pltpu.SemaphoreType.DMA((LIVE,))],
        compiler_params=PARAMS,
        name="prepare",
    )(where, pairs, live_counts, green)


def lists_kernel(layers, devices, tiles_dev, where_ref, table_ref, out_ref):
    lanes = table_ref.shape[-1]
    tiles = tiles_dev * devices
    layer, place = where_ref[0], where_ref[1]
    tile = lax.broadcasted_iota(jnp.int32, (tiles, lanes), 0)
    lane = lax.broadcasted_iota(jnp.int32, (tiles, lanes), 1)

    def codes_of(index):
        total = table_ref[index * devices]
        for device in range(1, devices):
            total = total + table_ref[index * devices + device]
        return total

    def unpack(code):
        kind = (code >> 1) & 3
        return (code & 1) == 1, code >> 16, (code >> 3) & 8191, kind >> 1, (kind ^ (kind >> 1)) & 1

    def hots(code):
        alive, row, col, wdir, rdir = unpack(code)
        return (row == tile) & alive, (col == tile) & alive, wdir, rdir

    def column(hot):
        return jnp.minimum(jnp.sum(jnp.where(hot, 1.0, 0.0), axis=1, keepdims=True), 1.0)

    def columns(code):
        row_hot, col_hot, wdir, rdir = hots(code)
        return [column(h & (side == d)) for h, side in ((row_hot, wdir), (col_hot, rdir)) for d in range(2)]

    def longest(wanted):
        most = jnp.sum(wanted[:tiles_dev], axis=0, keepdims=True)
        for device in range(1, devices):
            most = jnp.maximum(
                most, jnp.sum(wanted[device * tiles_dev : (device + 1) * tiles_dev], axis=0, keepdims=True)
            )
        return most

    def one(index, carry):
        w0, w1, r0, r1, most_sent, most_read = carry
        v0, v1, q0, q1 = columns(codes_of(index))
        most_sent = jnp.maximum(most_sent, jnp.sum(w0 * q0, axis=0, keepdims=True))
        most_sent = jnp.maximum(most_sent, jnp.sum(v1 * r1, axis=0, keepdims=True))
        most_read = jnp.maximum(most_read, longest(q0))
        most_read = jnp.maximum(most_read, longest(r1))
        return v0, v1, q0, q1, most_sent, most_read

    none = jnp.zeros((1, 1), jnp.float32)
    start = (*columns(codes_of(0)), none, none)
    most_sent, most_read = lax.fori_loop(1, layers, one, start)[4:]

    has_above = layer > 0
    has_below = layer < layers - 1
    mine = codes_of(layer)
    above = jnp.where(has_above, codes_of(jnp.maximum(layer - 1, 0)), 0)
    below = jnp.where(has_below, codes_of(jnp.minimum(layer + 1, layers - 1)), 0)
    w0, w1, r0, r1 = columns(mine)
    r0 = jnp.where(has_above, r0, 0.0)
    r1 = jnp.where(has_below, r1, 0.0)
    above_w0, _, _, want_up = columns(above)
    _, below_w1, want_down, _ = columns(below)
    chosen = [w0 * want_down, w1 * want_up, above_w0 * r0, below_w1 * r1, want_down, want_up, r0, r1]
    matrix = jnp.zeros((tiles, lanes), jnp.float32)
    for j, values in enumerate(chosen):
        matrix = jnp.where(lane == j, values, matrix)
    matrix = matrix.astype(jnp.bfloat16)
    at = lax.broadcasted_iota(jnp.int32, (tiles, tiles), 0)
    other = lax.broadcasted_iota(jnp.int32, (tiles, tiles), 1)

    def group_of(index):
        total = jnp.zeros_like(index)
        for device in range(1, devices):
            total = total + jnp.where(index >= device * tiles_dev, 1, 0)
        return total

    before = other < at
    inside = before & (group_of(other) == group_of(at))
    as_mask = lambda mask: jnp.where(mask, 1.0, 0.0).astype(jnp.bfloat16)
    position = jnp.dot(as_mask(before), matrix, preferred_element_type=jnp.float32)
    position_in = jnp.dot(as_mask(inside), matrix, preferred_element_type=jnp.float32)

    def entry(j, table):
        return chosen[j] * (table[:, j : j + 1] + 1.0)

    row_hot, col_hot, wdir, rdir = hots(mine)

    def look(hot, side, down, up):
        values = jnp.where(hot, jnp.where(side == 0, down, up), 0.0)
        return jnp.sum(values, axis=0, keepdims=True).astype(jnp.int32) - 1

    odd = layer & 1
    send = look(row_hot, wdir, entry(0, position), entry(1, position))
    recv = look(col_hot, rdir, entry(2, position), entry(3, position))
    src = look(col_hot, rdir, entry(6, position_in), entry(7, position_in))
    _, _, col, _, _ = unpack(mine)
    send_buf = jnp.where(odd == 1, wdir, 1 - wdir)
    recv_buf = jnp.where(odd == 1, 1 - rdir, rdir)
    group = group_of(col)
    if is_power(devices):
        offset = group ^ place
    else:
        offset = jnp.where(group > place, place + devices - group, place - group)
    send = jnp.where(send < 0, -1, send_buf * SHIFT + send)
    recv = jnp.where(recv < 0, -1, recv_buf * SHIFT + recv)
    src = jnp.where(src < 0, -1, (offset * 2 + recv_buf) * SHIFT + src)

    own = jnp.where(group_of(tile) == place, 1.0, 0.0)

    def ids(j):
        found = jnp.where(entry(j, position_in) == (lane + 1).astype(jnp.float32), own * tile.astype(jnp.float32), 0.0)
        return jnp.sum(found, axis=0, keepdims=True).astype(jnp.int32)

    down_ids, up_ids = ids(4), ids(5)
    first = jnp.where(odd == 1, down_ids, up_ids)
    second = jnp.where(odd == 1, up_ids, down_ids)
    lane_row = lane[:1]
    facts = jnp.where(lane_row == 0, most_sent.astype(jnp.int32), most_read.astype(jnp.int32))
    facts = jnp.where(lane_row == 2, odd, facts)
    facts = jnp.where(lane_row == 3, place, facts)
    for j, values in enumerate((send, recv, src, first, second, facts)):
        out_ref[j : j + 1] = values
    out_ref[6:] = jnp.zeros((out_ref.shape[0] - 6, lanes), jnp.int32)


def build_lists(where, table, layers, devices, tiles_dev):
    return pl.pallas_call(
        functools.partial(lists_kernel, layers, devices, tiles_dev),
        out_shape=jax.ShapeDtypeStruct((8, table.shape[-1]), jnp.int32),
        in_specs=[SMEM, VMEM],
        out_specs=VMEM,
        compiler_params=PARAMS,
        name="build_lists",
    )(where, table)


def split_kernel(green_ref, high_ref, low_ref):
    for slot in range(green_ref.shape[0]):
        for part in range(2):
            block = green_ref[slot, part].T
            high = block.astype(jnp.bfloat16)
            low = (block - high.astype(jnp.float32)).astype(jnp.bfloat16)
            high_ref[slot, :, part * TILE : (part + 1) * TILE] = high
            low_ref[slot, :, part * TILE : (part + 1) * TILE] = low


def split_green(packed):
    shape = jax.ShapeDtypeStruct((packed.shape[0], TILE, 2 * TILE), jnp.bfloat16)
    return pl.pallas_call(
        split_kernel,
        out_shape=(shape, shape),
        in_specs=[VMEM],
        out_specs=(VMEM, VMEM),
        compiler_params=PARAMS,
        name="split_green",
    )(packed)


def pick_kernel(devices, lists_ref, sources_ref, *out_refs):
    sub, tiles_dev = sources_ref.shape[2] // devices, sources_ref.shape[3] // TILE
    odd, place = lists_ref[5, 2], lists_ref[5, 3]
    for half, out_ref in enumerate(out_refs):
        direction = jnp.where(odd == 1, half, 1 - half)

        def one(j, carry):
            local = jnp.maximum(lists_ref[3 + half, j] - place * tiles_dev, 0)
            start = pl.multiple_of(local * TILE, TILE)
            for offset in range(devices):
                shot = pl.multiple_of(target_of(place, offset, devices) * sub, sub)
                for part in range(2):
                    out_ref[offset, j, part] = sources_ref[direction, part, pl.ds(shot, sub), pl.ds(start, TILE)]
            return carry

        lax.fori_loop(0, out_ref.shape[1], one, 0, unroll=True)


def pick_tiles(lists, sources, devices, cap_read):
    sub = sources.shape[2] // devices
    shape = jax.ShapeDtypeStruct((devices, cap_read, 2, sub, TILE), jnp.float32)
    return pl.pallas_call(
        functools.partial(pick_kernel, devices),
        out_shape=(shape, shape),
        in_specs=[SMEM, VMEM],
        out_specs=(VMEM, VMEM),
        compiler_params=PARAMS,
        name="pick_tiles",
    )(lists, sources)


def block_term(x, high, low):
    parts, sub, _ = x.shape
    rows = parts * sub
    flat = x.reshape(rows, TILE)
    top = flat.astype(jnp.bfloat16)
    rest = (flat - top.astype(jnp.float32)).astype(jnp.bfloat16)
    main = jnp.dot(jnp.concatenate([top, rest], axis=0), high, preferred_element_type=jnp.float32)
    prod = main[:rows] + main[rows:] + jnp.dot(top, low, preferred_element_type=jnp.float32)
    real = prod[:sub, :TILE] - prod[sub:, TILE:]
    imag = prod[:sub, TILE:] + prod[sub:, :TILE]
    return real, imag


def tick_kernel(stage, devices, lists_ref, *refs):
    refs = list(refs)
    highs = [refs.pop(0) for _ in range(2 * devices)]
    lows = [refs.pop(0) for _ in range(2 * devices)]
    place = lists_ref[5, 3]

    def position(row, lane, cap, empty):
        value = lists_ref[row, lane]
        found = lax.shift_right_logical(value, 10) * cap + (value & (SHIFT - 1))
        return jnp.where(value < 0, empty, found)

    if stage == "first":
        came = [refs.pop(0) for _ in range(devices)]
        out_a, out_b, x_out, got, acc = refs
        buffers = [ref.at[half] for ref in came for half in range(2)]
    else:
        xs, came_a, came_b = refs.pop(0), refs.pop(0), refs.pop(0)
        got = refs.pop()
        buffers = [came_a, came_b]
        if stage == "middle":
            out_a, out_b, acc = refs
        else:
            outs = refs
    got_cap = buffers[0].shape[0]
    got_empty = len(buffers) * got_cap
    for j, ref in enumerate(buffers):
        got[j * got_cap : (j + 1) * got_cap] = ref[...]
    got[got_empty] = jnp.zeros(got.shape[1:], jnp.float32)
    if stage != "last":
        cap = out_a.shape[0]
        acc[...] = jnp.zeros_like(acc)
    for group in range(devices):
        base = source_of(place, group, devices) * STRIDE
        for j in range(LIVE):
            slot = group * LIVE + j
            half, row = j // HALF, j % HALF
            high, low = highs[half * devices + group][row], lows[half * devices + group][row]
            if stage == "first":
                x = got[position(2, base + j, got_cap, got_empty)]
                x_out[slot] = x
            else:
                x = xs[slot] + got[position(1, base + j, got_cap, got_empty)]
            real, imag = block_term(x, high, low)
            if stage == "last":
                outs[group][j, 0] = real
                outs[group][j, 1] = imag
            else:
                at = position(0, base + j, cap, 2 * cap)
                acc[at, 0] += real
                acc[at, 1] += imag
    if stage != "last":
        out_a[...] = acc[:cap]
        out_b[...] = acc[cap : 2 * cap]


def tick(stage, devices, cap, lists, blocks, *data):
    sub = data[0].shape[-2]
    tile_shape = lambda count: jax.ShapeDtypeStruct((count, 2, sub, TILE), jnp.float32)
    room = lambda count: pltpu.VMEM((count, 2, sub, TILE), jnp.float32)
    if stage == "first":
        got = 2 * devices * data[0].shape[1] + 1
    else:
        got = 2 * cap + 1
    if stage == "last":
        out_shape = tuple(tile_shape(LIVE) for _ in range(devices))
        scratch = [room(got)]
    else:
        out_shape = (tile_shape(cap), tile_shape(cap))
        if stage == "first":
            out_shape += (tile_shape(devices * LIVE),)
            scratch = [room(got), room(2 * cap + 1)]
        else:
            scratch = [room(2 * cap + 1), room(got)]
    operands = (*blocks, *data)
    return pl.pallas_call(
        functools.partial(tick_kernel, stage, devices),
        out_shape=out_shape,
        in_specs=[SMEM] + [VMEM] * len(operands),
        out_specs=tuple(VMEM for _ in out_shape),
        scratch_shapes=scratch,
        compiler_params=PARAMS,
        name="tick_" + stage,
    )(lists, *operands)


def finish_kernel(where_ref, rows_ref, sources_ref, *refs):
    out_ref = refs[-1]
    terms = refs[:-1]
    out_ref[...] = sources_ref[...]
    devices = len(terms)
    sub = terms[0].shape[2]
    place = where_ref[1]
    for j in range(LIVE):
        direction = rows_ref[0, j]
        start = pl.multiple_of(rows_ref[1, j] * TILE, TILE)
        for offset, term in enumerate(terms):
            shot = pl.multiple_of(target_of(place, offset, devices) * sub, sub)
            for part in range(2):
                at = (direction, part, pl.ds(shot, sub), pl.ds(start, TILE))
                out_ref[at] += term[j, part]


def finish(where, rows, sources, terms):
    return pl.pallas_call(
        finish_kernel,
        out_shape=jax.ShapeDtypeStruct(sources.shape, sources.dtype),
        in_specs=[SMEM, SMEM] + [VMEM] * (1 + len(terms)),
        out_specs=VMEM,
        compiler_params=PARAMS,
        name="finish",
    )(where, rows, sources, *terms)


def sweeps(cap, cap_read, lists, sources, early, late):
    devices = lax.axis_size("tile")
    picked = pick_tiles(lists, sources, devices, cap_read)
    first, second = swap_layers(*picked)
    late = gather_groups(late)
    came = [jnp.stack([first[0], second[0]])]
    for offset in range(1, devices):
        came.append(swap_tile(jnp.stack([first[offset], second[offset]]), offset))
    highs, lows = zip(*[split_green(group) for group in early + late])
    blocks = highs + lows
    out_a, out_b, xs = tick("first", devices, cap, lists, blocks, *came)
    for _ in range(TICKS - 3):
        out_a, out_b = tick("middle", devices, cap, lists, blocks, xs, *swap_layers(out_a, out_b))
    terms = tick("last", devices, cap, lists, blocks, xs, *swap_layers(out_a, out_b))
    back = [terms[0]]
    for offset in range(1, devices):
        back.append(swap_tile(terms[offset], offset if is_power(devices) else devices - offset))
    return tuple(back)


def body(sources, green, rowcol, counts):
    devices = lax.axis_size("tile")
    layers = lax.axis_size("layer")
    tiles_dev = sources.shape[-1] // TILE
    local = sources[0]
    lanes = -(-devices * STRIDE // 128) * 128
    where = jnp.stack([lax.axis_index("layer"), lax.axis_index("tile")]).astype(jnp.int32)

    codes, rows, early, late = prepare(
        where, rowcol[0], counts[0], green[0], layers * devices, lanes, tiles_dev
    )
    early = gather_groups(early)
    table = lax.all_to_all(codes, ("layer", "tile"), 0, 0, tiled=True)
    lists = build_lists(where, table, layers, devices, tiles_dev)
    long_lists = (SIDE * devices, tiles_dev)
    short_lists = (min(SHORT, long_lists[0]), min(SHORT_READ, long_lists[1]))
    fits = (lists[5, 0] <= short_lists[0]) & (lists[5, 1] <= short_lists[1])
    terms = lax.cond(
        fits,
        functools.partial(sweeps, *short_lists),
        functools.partial(sweeps, *long_lists),
        lists,
        local,
        early,
        late,
    )
    return finish(where, rows, local, terms)[None]


def solution(mesh):
    return jax.shard_map(
        body,
        mesh=mesh,
        in_specs=(
            P("layer", None, None, None, "tile"),
            P("layer", "tile", None, None, None),
            P("layer", "tile", None),
            P("layer", "tile"),
        ),
        out_specs=P("layer", None, None, None, "tile"),
        check_vma=False,
    )
```

time: 246 us -> 122 us (0.50)
  waiting for transfers between devices: 113 us -> 58.6 us
  starting transfers between devices: 55.3 us -> 29.4 us
  local copies, waits for them, and re-layouts: 29.6 us -> 3.79 us
  other arithmetic: 23.8 us -> 0.13 us
  matrix products: 23.1 us -> 0 us
  Pallas kernels: 0 us -> 17.3 us
  blocking collectives: 0 us -> 11.1 us
    ppermute x20 -> x22, waiting for transfers between devices: 113 us -> 58.6 us  [the longest x12 26.7 us: swap_tile(): return lax.ppermute(block, 'tile', [(i, partner(i)) for i in range(count)])]
    ppermute x20 -> x22, starting transfers between devices: 55.3 us -> 29.4 us  [the longest x5 15.5 us: swap_layers(): lax.ppermute(first, 'layer', both(odd))]
    dot_general x10 -> x0, matrix products: 23.1 us -> none  [the longest x5 14.8 us: complex_term(): prod = jnp.einsum(pattern, picked, blocks, precision=lax.Precision.HIGHEST)]
    pallas_call x0 -> x17, Pallas kernels: none -> 17.3 us  [the longest x5 7.27 us: tick(): pl.pallas_call(functools.partial(tick_kernel, stage, devices), out_shape=...]
    gather x11 -> x0, local copies, waits for them, and re-layouts: 15 us -> none  [the longest x6 10.7 us: live_update(): picked = tiled[anchor, :, :, col_local[order]]]
    add x12 -> x0, other arithmetic: 11.9 us -> none  [the longest x5 9.25 us: body(): waves = local_sources + update.reshape(2, 2, shots, width)]
    reshape x5 -> x0, local copies, waits for them, and re-layouts: 11.9 us -> none  [body(): waves = local_sources + update.reshape(2, 2, shots, width)]
    all_to_all x0 -> x1, blocking collectives: none -> 11.1 us  [body(): table = lax.all_to_all(codes, ('layer', 'tile'), 0, 0, tiled=True)]
  transfers between devices with their start and end apart: 20 -> 22, of which waited for: 19 -> 16; matrix products, arithmetic and copies ran while one was open for 4% -> 1% of each run, Pallas kernels for 0% -> 4%
where the time goes in v2:
time: 122 us
  waiting for transfers between devices  58.6 us (48%)
  starting transfers between devices  29.4 us (24%)
  Pallas kernels  17.3 us (14%)
  blocking collectives  11.1 us (9%)
  local copies, waits for them, and re-layouts  3.79 us (3%)
  between operations  1.33 us (1%)
    ppermute x12, waiting for transfers between devices, swap_tile(): return lax.ppermute(block, 'tile', [(i, partner(i)) for i in range(count)])  26.7 us
    ppermute x5, waiting for transfers between devices, swap_layers(): lax.ppermute(first, 'layer', both(odd))  18.4 us
    ppermute x5, starting transfers between devices, swap_layers(): lax.ppermute(first, 'layer', both(odd))  15.5 us
    ppermute x5, waiting for transfers between devices, swap_layers(): lax.ppermute(second, 'layer', both(even))  13.6 us
    ppermute x12, starting transfers between devices, swap_tile(): return lax.ppermute(block, 'tile', [(i, partner(i)) for i in range(count)])  12 us
    all_to_all x1, blocking collectives, body(): table = lax.all_to_all(codes, ('layer', 'tile'), 0, 0, tiled=True)  11.1 us
    pallas_call x5, Pallas kernels, tick(): pl.pallas_call(functools.partial(tick_kernel, stage, devices), out_shape=...  7.27 us
    pallas_call x1, Pallas kernels, prepare(): pl.pallas_call(functools.partial(prepare_kernel, tiles_dev), out_shape=(j...  3.34 us
  transfers between devices with their start and end apart: 22, of which 16 were waited for; matrix products, arithmetic and copies ran while one was open for 1% of the time, Pallas kernels for 4%

profile of v2, /device:TPU:9, one launch (start us, length us, event | category | flops | bytes accessed | tf_op | source)
XLA Modules:
  0.0 122.0 jit_solution(2545021621522650986)
XLA Ops:
  0.0 0.8 copy.5.rowcol_ref
  0.8 0.1 pad_add_fusion.where_ref
  0.8 1.7 %copy-done = f32[1,20,2,128,128]{4,3,2,1,0:T(8,128)S(1)} copy-done((f32[1,20,2,128,128]{4,3,2,1,0:T(8,128)S(1)}, f32[1,20,2,128,128]{4,3,2,1,0:T(8,128)}, u32[]{:S(2)}) %copy-start) | copy-done | bytes 2621464
  2.6 0.7 copy-done.1
  3.2 3.3 %prepare.1 = (s32[32,1,128]{2,1,0:T(1,128)S(1)}, s32[2,16]{1,0:T(2,128)S(1)}, f32[5,2,128,128]{3,2,1,0:T(8,128)S(1)}, f32[5,2,128,128]{3,2,1,0:T(8,128)S(1)}) custom-call(s32[2]{0:T(128)S(1)} %pad_add_fusion.where_ref, s32[20,2]{1,0:T(8,128)S(1)} %copy.5.rowcol_ref, s32[4]{0:T(128)S(1)} %bitcast.9, f32[20,2,128,128]{3,2,1,0:T(8,128)S(1)} %bitcast.8), custom_call_target="tpu_custom_call" | custom-call | tf_op jit(solution)/shard_map/prepare/pallas_call | solution.py:111
  6.6 1.3 %collective-permute-start.39 = (f32[5,2,128,128]{3,2,1,0:T(8,128)S(1)}, f32[5,2,128,128]{3,2,1,0:T(8,128)S(1)}, u32[]{:S(2)}, u32[]{:S(2)}) collective-permute-start(f32[5,2,128,128]{3,2,1,0:T(8,128)S(1)} %get-tuple-element.119), channel_id=1, source_target_pairs={{0,2},{1,3},{2,0},{3,1},{4,6},{5,7},{6,4},{7,5},{8,10},{9,11},{10,... | collective-permute-start | bytes 1966088 | tf_op jit(solution)/shard_map/ppermute | solution.py:36
  7.9 1.0 collective-permute-start.38
  8.9 13.4 %collective-permute-done.39 = f32[5,2,128,128]{3,2,1,0:T(8,128)S(1)} collective-permute-done((f32[5,2,128,128]{3,2,1,0:T(8,128)S(1)}, f32[5,2,128,128]{3,2,1,0:T(8,128)S(1)}, u32[]{:S(2)}, u32[]{:S(2)}) %collective-permute-start.39) | collective-permute-done | bytes 655392 | tf_op jit(solution)/shard_map/ppermute | solution.py:36
  22.3 1.5 %collective-permute-start.40 = (f32[5,2,128,128]{3,2,1,0:T(8,128)S(1)}, f32[5,2,128,128]{3,2,1,0:T(8,128)S(1)}, u32[]{:S(2)}, u32[]{:S(2)}) collective-permute-start(f32[5,2,128,128]{3,2,1,0:T(8,128)S(1)} %collective-permute-done.39), channel_id=1, source_target_pairs={{0,1},{1,0},{2,3},{3,2},{4,5},{5,4},{6,7},{7,6},{8,9},{9,8},{10,11... | collective-permute-start | bytes 1966088 | tf_op jit(solution)/shard_map/ppermute | solution.py:36
  23.8 11.1 %all_to_all.5.table_ref = s32[32,1,128]{2,1,0:T(1,128)S(1)} all-to-all(s32[32,1,128]{2,1,0:T(1,128)S(1)} %get-tuple-element.118), channel_id=1, replica_groups=mesh['layer'=8,'tile'=4] {'layer','tile'}, dimensions={0} | all-to-all | bytes 32768 | tf_op jit(solution)/shard_map/all_to_all | solution.py:471
  34.9 1.9 %build_lists.1 = s32[8,128]{1,0:T(8,128)S(1)} custom-call(s32[2]{0:T(128)S(1)} %pad_add_fusion.where_ref, s32[32,1,128]{2,1,0:T(1,128)S(1)} %all_to_all.5.table_ref), custom_call_target="tpu_custom_call" | custom-call | tf_op jit(solution)/shard_map/build_lists/pallas_call | solution.py:250
  36.9 0.6 fusion.4
  38.8 0.0 collective-permute-done.38
  38.8 81.0 %conditional.1 = (f32[10,2,8,128]{3,2,1,0:T(8,128)S(1)}, f32[10,2,8,128]{3,2,1,0:T(8,128)}, f32[10,2,8,128]{3,2,1,0:T(8,128)}, f32[10,2,8,128]{3,2,1,0:T(8,128)}) conditional(s32[]{:T(128)} %bitcast.6, (f32[5,2,128,128]{3,2,1,0:T(8,128)S(1)}, f32[5,2,128,128]{3,2,1,0:T(8,128)S(1)}, f32[5,2,128,128]{3,2,1,0:T(8,128)S(1)}, ...), branch_computations={%region_0.0_spmd, %region_1.0_spmd} | conditional | flops 262144 | bytes 28771096 | solution.py:476
  38.8 0.5 collective-permute-start.20
  39.3 0.7 pick_tiles.3
  40.0 3.3 %collective-permute-start.22 = (f32[4,9,2,8,128]{4,3,2,1,0:T(8,128)S(1)}, f32[4,9,2,8,128]{4,3,2,1,0:T(8,128)S(1)}, u32[]{:S(2)}, u32[]{:S(2)}) collective-permute-start(f32[4,9,2,8,128]{4,3,2,1,0:T(8,128)S(1)} %get-tuple-element.94), channel_id=1, source_target_pairs={{4,8},{12,16},{20,24},{8,4},{16,12},{24,20},{5,9},{13,17},{21,25},... | collective-permute-start | bytes 884744 | tf_op jit(solution)/shard_map/cond/branch_1_fun/ppermute | solution.py:67
  43.2 0.4 collective-permute-start.23
  43.6 1.5 %collective-permute-start.19 = (f32[5,2,128,128]{3,2,1,0:T(8,128)S(1)}, f32[5,2,128,128]{3,2,1,0:T(8,128)S(1)}, u32[]{:S(2)}, u32[]{:S(2)}) collective-permute-start(f32[5,2,128,128]{3,2,1,0:T(8,128)S(1)} %get-tuple-element.80.green_ref), channel_id=1, source_target_pairs={{0,1},{1,0},{2,3},{3,2},{4,5},{5,4},{6,7},{7,6},{8,9},{9,8},{10,11... | collective-permute-start | bytes 1966088 | tf_op jit(solution)/shard_map/cond/branch_1_fun/ppermute | solution.py:36
  45.1 5.3 %collective-permute-done.22 = f32[4,9,2,8,128]{4,3,2,1,0:T(8,128)S(1)} collective-permute-done((f32[4,9,2,8,128]{4,3,2,1,0:T(8,128)S(1)}, f32[4,9,2,8,128]{4,3,2,1,0:T(8,128)S(1)}, u32[]{:S(2)}, u32[]{:S(2)}) %collective-permute-start.22) | collective-permute-done | bytes 294944 | tf_op jit(solution)/shard_map/cond/branch_1_fun/ppermute | solution.py:67
  50.4 3.9 %collective-permute-done.20.green_ref = f32[5,2,128,128]{3,2,1,0:T(8,128)S(1)} collective-permute-done((f32[5,2,128,128]{3,2,1,0:T(8,128)S(1)}, f32[5,2,128,128]{3,2,1,0:T(8,128)S(1)}, u32[]{:S(2)}, u32[]{:S(2)}) %collective-permute-start.20) | collective-permute-done | bytes 655392 | tf_op jit(solution)/shard_map/cond/branch_1_fun/ppermute | solution.py:36
  54.4 1.7 %collective-permute-start.21 = (f32[5,2,128,128]{3,2,1,0:T(8,128)S(1)}, f32[5,2,128,128]{3,2,1,0:T(8,128)S(1)}, u32[]{:S(2)}, u32[]{:S(2)}) collective-permute-start(f32[5,2,128,128]{3,2,1,0:T(8,128)S(1)} %collective-permute-done.20.green_ref), channel_id=1, source_target_pairs={{0,1},{1,0},{2,3},{3,2},{4,5},{5,4},{6,7},{7,6},{8,9},{9,8},{10,11... | collective-permute-start | bytes 1966088 | tf_op jit(solution)/shard_map/cond/branch_1_fun/ppermute | solution.py:36
  56.0 2.0 %collective-permute-done.23 = f32[4,9,2,8,128]{4,3,2,1,0:T(8,128)S(1)} collective-permute-done((f32[4,9,2,8,128]{4,3,2,1,0:T(8,128)S(1)}, f32[4,9,2,8,128]{4,3,2,1,0:T(8,128)S(1)}, u32[]{:S(2)}, u32[]{:S(2)}) %collective-permute-start.23) | collective-permute-done | bytes 294944 | tf_op jit(solution)/shard_map/cond/branch_1_fun/ppermute | solution.py:67
  58.1 0.6 collective-permute-start.24
  58.6 1.1 collective-permute-start.25
  59.8 0.6 collective-permute-start.26
  60.4 0.2 split_green.28
  60.7 0.2 split_green.24
  60.9 0.2 split_green.25
  61.2 0.2 split_green.26
  61.4 0.2 split_green.27
  61.7 0.2 split_green.30
  61.9 0.2 split_green.29
  62.2 0.0 collective-permute-done.21.green_ref
  62.2 0.2 split_green.31
  62.5 1.7 %collective-permute-done.25.refs_18_ = f32[2,9,2,8,128]{4,3,2,1,0:T(8,128)S(1)} collective-permute-done((f32[2,9,2,8,128]{4,3,2,1,0:T(8,128)S(1)}, f32[2,9,2,8,128]{4,3,2,1,0:T(8,128)S(1)}, u32[]{:S(2)}, u32[]{:S(2)}) %collective-permute-start.25) | collective-permute-done | bytes 147488 | tf_op jit(solution)/shard_map/cond/branch_1_fun/ppermute | solution.py:36
  64.2 3.3 %collective-permute-done.26.refs_19_ = f32[2,9,2,8,128]{4,3,2,1,0:T(8,128)S(1)} collective-permute-done((f32[2,9,2,8,128]{4,3,2,1,0:T(8,128)S(1)}, f32[2,9,2,8,128]{4,3,2,1,0:T(8,128)S(1)}, u32[]{:S(2)}, u32[]{:S(2)}) %collective-permute-start.26) | collective-permute-done | bytes 147488 | tf_op jit(solution)/shard_map/cond/branch_1_fun/ppermute | solution.py:36
  67.4 1.5 %tick_first.3 = (f32[12,2,8,128]{3,2,1,0:T(8,128)S(1)}, f32[12,2,8,128]{3,2,1,0:T(8,128)S(1)}, f32[40,2,8,128]{3,2,1,0:T(8,128)S(1)}) custom-call(s32[8,128]{1,0:T(8,128)S(1)} %get-tuple-element.71.lists_ref, bf16[5,128,256]{2,1,0:T(8,128)(2,1)S(1)} %get-tuple-element.73.refs_0_, bf16[5,128,256]{2,1,0:T(8,128)(2,1)S(1)} %get-tuple-element.75.refs_1_, ...), custom_call_target="tpu_custom_call" | custom-call | tf_op jit(solution)/shard_map/cond/branch_1_fun/tick_first/pallas_call | solution.py:400
  68.9 3.1 %collective-permute-start.27 = (f32[12,2,8,128]{3,2,1,0:T(8,128)S(1)}, f32[12,2,8,128]{3,2,1,0:T(8,128)S(1)}, u32[]{:S(2)}, u32[]{:S(2)}) collective-permute-start(f32[12,2,8,128]{3,2,1,0:T(8,128)S(1)} %get-tuple-element.97), channel_id=1, source_target_pairs={{4,8},{12,16},{20,24},{8,4},{16,12},{24,20},{5,9},{13,17},{21,25},... | collective-permute-start | bytes 294920 | tf_op jit(solution)/shard_map/cond/branch_1_fun/ppermute | solution.py:67
  72.0 0.4 collective-permute-start.28
  72.4 3.4 %collective-permute-done.27.refs_17_ = f32[12,2,8,128]{3,2,1,0:T(8,128)S(1)} collective-permute-done((f32[12,2,8,128]{3,2,1,0:T(8,128)S(1)}, f32[12,2,8,128]{3,2,1,0:T(8,128)S(1)}, u32[]{:S(2)}, u32[]{:S(2)}) %collective-permute-start.27) | collective-permute-done | bytes 98336 | tf_op jit(solution)/shard_map/cond/branch_1_fun/ppermute | solution.py:67
  75.8 2.7 %collective-permute-done.28.refs_18_ = f32[12,2,8,128]{3,2,1,0:T(8,128)S(1)} collective-permute-done((f32[12,2,8,128]{3,2,1,0:T(8,128)S(1)}, f32[12,2,8,128]{3,2,1,0:T(8,128)S(1)}, u32[]{:S(2)}, u32[]{:S(2)}) %collective-permute-start.28) | collective-permute-done | bytes 98336 | tf_op jit(solution)/shard_map/cond/branch_1_fun/ppermute | solution.py:67
  78.6 1.5 %tick_middle.9 = (f32[12,2,8,128]{3,2,1,0:T(8,128)S(1)}, f32[12,2,8,128]{3,2,1,0:T(8,128)S(1)}) custom-call(s32[8,128]{1,0:T(8,128)S(1)} %get-tuple-element.71.lists_ref, bf16[5,128,256]{2,1,0:T(8,128)(2,1)S(1)} %get-tuple-element.73.refs_0_, bf16[5,128,256]{2,1,0:T(8,128)(2,1)S(1)} %get-tuple-element.75.refs_1_, ...), custom_call_target="tpu_custom_call" | custom-call | tf_op jit(solution)/shard_map/cond/branch_1_fun/tick_middle/pallas_call | solution.py:400
  80.0 3.1 %collective-permute-start.29 = (f32[12,2,8,128]{3,2,1,0:T(8,128)S(1)}, f32[12,2,8,128]{3,2,1,0:T(8,128)S(1)}, u32[]{:S(2)}, u32[]{:S(2)}) collective-permute-start(f32[12,2,8,128]{3,2,1,0:T(8,128)S(1)} %get-tuple-element.99), channel_id=1, source_target_pairs={{4,8},{12,16},{20,24},{8,4},{16,12},{24,20},{5,9},{13,17},{21,25},... | collective-permute-start | bytes 294920 | tf_op jit(solution)/shard_map/cond/branch_1_fun/ppermute | solution.py:67
  83.1 0.4 collective-permute-start.30
  83.5 3.2 %collective-permute-done.29.refs_17_ = f32[12,2,8,128]{3,2,1,0:T(8,128)S(1)} collective-permute-done((f32[12,2,8,128]{3,2,1,0:T(8,128)S(1)}, f32[12,2,8,128]{3,2,1,0:T(8,128)S(1)}, u32[]{:S(2)}, u32[]{:S(2)}) %collective-permute-start.29) | collective-permute-done | bytes 98336 | tf_op jit(solution)/shard_map/cond/branch_1_fun/ppermute | solution.py:67
  86.7 2.9 %collective-permute-done.30.refs_18_ = f32[12,2,8,128]{3,2,1,0:T(8,128)S(1)} collective-permute-done((f32[12,2,8,128]{3,2,1,0:T(8,128)S(1)}, f32[12,2,8,128]{3,2,1,0:T(8,128)S(1)}, u32[]{:S(2)}, u32[]{:S(2)}) %collective-permute-start.30) | collective-permute-done | bytes 98336 | tf_op jit(solution)/shard_map/cond/branch_1_fun/ppermute | solution.py:67
  89.6 1.5 %tick_middle.10 = (f32[12,2,8,128]{3,2,1,0:T(8,128)S(1)}, f32[12,2,8,128]{3,2,1,0:T(8,128)S(1)}) custom-call(s32[8,128]{1,0:T(8,128)S(1)} %get-tuple-element.71.lists_ref, bf16[5,128,256]{2,1,0:T(8,128)(2,1)S(1)} %get-tuple-element.73.refs_0_, bf16[5,128,256]{2,1,0:T(8,128)(2,1)S(1)} %get-tuple-element.75.refs_1_, ...), custom_call_target="tpu_custom_call" | custom-call | tf_op jit(solution)/shard_map/cond/branch_1_fun/tick_middle/pallas_call | solution.py:400
  91.1 3.1 %collective-permute-start.31 = (f32[12,2,8,128]{3,2,1,0:T(8,128)S(1)}, f32[12,2,8,128]{3,2,1,0:T(8,128)S(1)}, u32[]{:S(2)}, u32[]{:S(2)}) collective-permute-start(f32[12,2,8,128]{3,2,1,0:T(8,128)S(1)} %get-tuple-element.101), channel_id=1, source_target_pairs={{4,8},{12,16},{20,24},{8,4},{16,12},{24,20},{5,9},{13,17},{21,25},... | collective-permute-start | bytes 294920 | tf_op jit(solution)/shard_map/cond/branch_1_fun/ppermute | solution.py:67
  94.2 0.4 collective-permute-start.32
  94.6 3.2 %collective-permute-done.31.refs_17_ = f32[12,2,8,128]{3,2,1,0:T(8,128)S(1)} collective-permute-done((f32[12,2,8,128]{3,2,1,0:T(8,128)S(1)}, f32[12,2,8,128]{3,2,1,0:T(8,128)S(1)}, u32[]{:S(2)}, u32[]{:S(2)}) %collective-permute-start.31) | collective-permute-done | bytes 98336 | tf_op jit(solution)/shard_map/cond/branch_1_fun/ppermute | solution.py:67
  97.8 2.9 %collective-permute-done.32.refs_18_ = f32[12,2,8,128]{3,2,1,0:T(8,128)S(1)} collective-permute-done((f32[12,2,8,128]{3,2,1,0:T(8,128)S(1)}, f32[12,2,8,128]{3,2,1,0:T(8,128)S(1)}, u32[]{:S(2)}, u32[]{:S(2)}) %collective-permute-start.32) | collective-permute-done | bytes 98336 | tf_op jit(solution)/shard_map/cond/branch_1_fun/ppermute | solution.py:67
  100.7 1.5 %tick_middle.11 = (f32[12,2,8,128]{3,2,1,0:T(8,128)S(1)}, f32[12,2,8,128]{3,2,1,0:T(8,128)S(1)}) custom-call(s32[8,128]{1,0:T(8,128)S(1)} %get-tuple-element.71.lists_ref, bf16[5,128,256]{2,1,0:T(8,128)(2,1)S(1)} %get-tuple-element.73.refs_0_, bf16[5,128,256]{2,1,0:T(8,128)(2,1)S(1)} %get-tuple-element.75.refs_1_, ...), custom_call_target="tpu_custom_call" | custom-call | tf_op jit(solution)/shard_map/cond/branch_1_fun/tick_middle/pallas_call | solution.py:400
  102.2 3.1 %collective-permute-start.33 = (f32[12,2,8,128]{3,2,1,0:T(8,128)S(1)}, f32[12,2,8,128]{3,2,1,0:T(8,128)S(1)}, u32[]{:S(2)}, u32[]{:S(2)}) collective-permute-start(f32[12,2,8,128]{3,2,1,0:T(8,128)S(1)} %get-tuple-element.103), channel_id=1, source_target_pairs={{4,8},{12,16},{20,24},{8,4},{16,12},{24,20},{5,9},{13,17},{21,25},... | collective-permute-start | bytes 294920 | tf_op jit(solution)/shard_map/cond/branch_1_fun/ppermute | solution.py:67
  105.3 0.4 collective-permute-start.34
  105.7 3.2 %collective-permute-done.33.refs_17_ = f32[12,2,8,128]{3,2,1,0:T(8,128)S(1)} collective-permute-done((f32[12,2,8,128]{3,2,1,0:T(8,128)S(1)}, f32[12,2,8,128]{3,2,1,0:T(8,128)S(1)}, u32[]{:S(2)}, u32[]{:S(2)}) %collective-permute-start.33) | collective-permute-done | bytes 98336 | tf_op jit(solution)/shard_map/cond/branch_1_fun/ppermute | solution.py:67
  108.9 2.9 %collective-permute-done.34.refs_18_ = f32[12,2,8,128]{3,2,1,0:T(8,128)S(1)} collective-permute-done((f32[12,2,8,128]{3,2,1,0:T(8,128)S(1)}, f32[12,2,8,128]{3,2,1,0:T(8,128)S(1)}, u32[]{:S(2)}, u32[]{:S(2)}) %collective-permute-start.34) | collective-permute-done | bytes 98336 | tf_op jit(solution)/shard_map/cond/branch_1_fun/ppermute | solution.py:67
  111.8 1.4 %tick_last.3 = (f32[10,2,8,128]{3,2,1,0:T(8,128)S(1)}, f32[10,2,8,128]{3,2,1,0:T(8,128)S(1)}, f32[10,2,8,128]{3,2,1,0:T(8,128)S(1)}, f32[10,2,8,128]{3,2,1,0:T(8,128)S(1)}) custom-call(s32[8,128]{1,0:T(8,128)S(1)} %get-tuple-element.71.lists_ref, bf16[5,128,256]{2,1,0:T(8,128)(2,1)S(1)} %get-tuple-element.73.refs_0_, ...), custom_call_target="tpu_custom_call" | custom-call | tf_op jit(solution)/shard_map/cond/branch_1_fun/tick_last/pallas_call | solution.py:400
  113.2 0.5 collective-permute-start.35
  113.7 1.1 collective-permute-start.36
  114.8 0.6 collective-permute-start.37
  115.5 2.4 %collective-permute-done.36 = f32[10,2,8,128]{3,2,1,0:T(8,128)} collective-permute-done((f32[10,2,8,128]{3,2,1,0:T(8,128)S(1)}, f32[10,2,8,128]{3,2,1,0:T(8,128)}, u32[]{:S(2)}, u32[]{:S(2)}) %collective-permute-start.36) | collective-permute-done | bytes 81952 | tf_op jit(solution)/shard_map/cond/branch_1_fun/ppermute | solution.py:36
  117.9 1.9 %collective-permute-done.37 = f32[10,2,8,128]{3,2,1,0:T(8,128)} collective-permute-done((f32[10,2,8,128]{3,2,1,0:T(8,128)S(1)}, f32[10,2,8,128]{3,2,1,0:T(8,128)}, u32[]{:S(2)}, u32[]{:S(2)}) %collective-permute-start.37) | collective-permute-done | bytes 81952 | tf_op jit(solution)/shard_map/cond/branch_1_fun/ppermute | solution.py:36
  119.8 2.2 %finish.1 = f32[2,2,32,2048]{3,2,1,0:T(8,128)} custom-call(s32[2]{0:T(128)S(1)} %pad_add_fusion.where_ref, s32[2,16]{1,0:T(2,128)S(1)} %get-tuple-element.117.rows_ref, f32[2,2,32,2048]{3,2,1,0:T(8,128)S(1)} %bitcast.12, f32[10,2,8,128]{3,2,1,0:T(8,128)S(1)} %get-tuple-element.121.refs_0_, f32[10,2,8,128]{3,2,1,0:T(8,128)} %get-tuple-element.122.refs_1_, ...), custom_call_target="tpu_custom_call" | custom-call | tf_op jit(solution)/shard_map/finish/pallas_call | solution.py:429
  (14 shorter events, 0.1 us)
Async XLA Ops:
  0.8 1.7 %copy-start = (f32[1,20,2,128,128]{4,3,2,1,0:T(8,128)S(1)}, f32[1,20,2,128,128]{4,3,2,1,0:T(8,128)}, u32[]{:S(2)}) copy-start(f32[1,20,2,128,128]{4,3,2,1,0:T(8,128)} %param.7) | copy-start | bytes 7864324
  2.6 0.7 copy-start.1
  3.2 35.5 %copy-start.2 = (f32[1,2,2,32,2048]{4,3,2,1,0:T(8,128)S(1)}, f32[1,2,2,32,2048]{4,3,2,1,0:T(8,128)}, u32[]{:S(2)}) copy-start(f32[1,2,2,32,2048]{4,3,2,1,0:T(8,128)} %param.6) | copy-start | bytes 3145732
  6.6 15.7 %collective-permute-start.39 = (f32[5,2,128,128]{3,2,1,0:T(8,128)S(1)}, f32[5,2,128,128]{3,2,1,0:T(8,128)S(1)}, u32[]{:S(2)}, u32[]{:S(2)}) collective-permute-start(f32[5,2,128,128]{3,2,1,0:T(8,128)S(1)} %get-tuple-element.119), channel_id=1, source_target_pairs={{0,2},{1,3},{2,0},{3,1},{4,6},{5,7},{6,4},{7,5},{8,10},{9,11},{10,... | collective-permute-start | bytes 1966088 | tf_op jit(solution)/shard_map/ppermute | solution.py:36
  7.9 30.9 %collective-permute-start.38 = (f32[5,2,128,128]{3,2,1,0:T(8,128)S(1)}, f32[5,2,128,128]{3,2,1,0:T(8,128)S(1)}, u32[]{:S(2)}, u32[]{:S(2)}) collective-permute-start(f32[5,2,128,128]{3,2,1,0:T(8,128)S(1)} %get-tuple-element.119), channel_id=1, source_target_pairs={{0,1},{1,0},{2,3},{3,2},{4,5},{5,4},{6,7},{7,6},{8,9},{9,8},{10,11... | collective-permute-start | bytes 1966088 | tf_op jit(solution)/shard_map/ppermute | solution.py:36
  22.3 16.5 %collective-permute-start.40 = (f32[5,2,128,128]{3,2,1,0:T(8,128)S(1)}, f32[5,2,128,128]{3,2,1,0:T(8,128)S(1)}, u32[]{:S(2)}, u32[]{:S(2)}) collective-permute-start(f32[5,2,128,128]{3,2,1,0:T(8,128)S(1)} %collective-permute-done.39), channel_id=1, source_target_pairs={{0,1},{1,0},{2,3},{3,2},{4,5},{5,4},{6,7},{7,6},{8,9},{9,8},{10,11... | collective-permute-start | bytes 1966088 | tf_op jit(solution)/shard_map/ppermute | solution.py:36
  38.8 15.6 %collective-permute-start.20 = (f32[5,2,128,128]{3,2,1,0:T(8,128)S(1)}, f32[5,2,128,128]{3,2,1,0:T(8,128)S(1)}, u32[]{:S(2)}, u32[]{:S(2)}) collective-permute-start(f32[5,2,128,128]{3,2,1,0:T(8,128)S(1)} %get-tuple-element.80.green_ref), channel_id=1, source_target_pairs={{0,2},{1,3},{2,0},{3,1},{4,6},{5,7},{6,4},{7,5},{8,10},{9,11},{10,... | collective-permute-start | bytes 1966088 | tf_op jit(solution)/shard_map/cond/branch_1_fun/ppermute | solution.py:36
  40.0 10.4 %collective-permute-start.22 = (f32[4,9,2,8,128]{4,3,2,1,0:T(8,128)S(1)}, f32[4,9,2,8,128]{4,3,2,1,0:T(8,128)S(1)}, u32[]{:S(2)}, u32[]{:S(2)}) collective-permute-start(f32[4,9,2,8,128]{4,3,2,1,0:T(8,128)S(1)} %get-tuple-element.94), channel_id=1, source_target_pairs={{4,8},{12,16},{20,24},{8,4},{16,12},{24,20},{5,9},{13,17},{21,25},... | collective-permute-start | bytes 884744 | tf_op jit(solution)/shard_map/cond/branch_1_fun/ppermute | solution.py:67
  43.2 14.8 %collective-permute-start.23 = (f32[4,9,2,8,128]{4,3,2,1,0:T(8,128)S(1)}, f32[4,9,2,8,128]{4,3,2,1,0:T(8,128)S(1)}, u32[]{:S(2)}, u32[]{:S(2)}) collective-permute-start(f32[4,9,2,8,128]{4,3,2,1,0:T(8,128)S(1)} %get-tuple-element.95), channel_id=1, source_target_pairs={{0,4},{8,12},{16,20},{24,28},{4,0},{12,8},{20,16},{28,24},{1,5},{9... | collective-permute-start | bytes 884744 | tf_op jit(solution)/shard_map/cond/branch_1_fun/ppermute | solution.py:67
  43.6 18.3 %collective-permute-start.19 = (f32[5,2,128,128]{3,2,1,0:T(8,128)S(1)}, f32[5,2,128,128]{3,2,1,0:T(8,128)S(1)}, u32[]{:S(2)}, u32[]{:S(2)}) collective-permute-start(f32[5,2,128,128]{3,2,1,0:T(8,128)S(1)} %get-tuple-element.80.green_ref), channel_id=1, source_target_pairs={{0,1},{1,0},{2,3},{3,2},{4,5},{5,4},{6,7},{7,6},{8,9},{9,8},{10,11... | collective-permute-start | bytes 1966088 | tf_op jit(solution)/shard_map/cond/branch_1_fun/ppermute | solution.py:36
  54.4 7.8 %collective-permute-start.21 = (f32[5,2,128,128]{3,2,1,0:T(8,128)S(1)}, f32[5,2,128,128]{3,2,1,0:T(8,128)S(1)}, u32[]{:S(2)}, u32[]{:S(2)}) collective-permute-start(f32[5,2,128,128]{3,2,1,0:T(8,128)S(1)} %collective-permute-done.20.green_ref), channel_id=1, source_target_pairs={{0,1},{1,0},{2,3},{3,2},{4,5},{5,4},{6,7},{7,6},{8,9},{9,8},{10,11... | collective-permute-start | bytes 1966088 | tf_op jit(solution)/shard_map/cond/branch_1_fun/ppermute | solution.py:36
  58.1 4.4 %collective-permute-start.24 = (f32[2,9,2,8,128]{4,3,2,1,0:T(8,128)S(1)}, f32[2,9,2,8,128]{4,3,2,1,0:T(8,128)S(1)}, u32[]{:S(2)}, u32[]{:S(2)}) collective-permute-start(f32[2,9,2,8,128]{4,3,2,1,0:T(8,128)S(1)} %pad_maximum_fusion.5), channel_id=1, source_target_pairs={{0,1},{1,0},{2,3},{3,2},{4,5},{5,4},{6,7},{7,6},{8,9},{9,8},{10,11... | collective-permute-start | bytes 442376 | tf_op jit(solution)/shard_map/cond/branch_1_fun/ppermute | solution.py:36
  58.6 5.5 %collective-permute-start.25 = (f32[2,9,2,8,128]{4,3,2,1,0:T(8,128)S(1)}, f32[2,9,2,8,128]{4,3,2,1,0:T(8,128)S(1)}, u32[]{:S(2)}, u32[]{:S(2)}) collective-permute-start(f32[2,9,2,8,128]{4,3,2,1,0:T(8,128)S(1)} %pad_maximum_fusion.6), channel_id=1, source_target_pairs={{0,2},{1,3},{2,0},{3,1},{4,6},{5,7},{6,4},{7,5},{8,10},{9,11},{10,... | collective-permute-start | bytes 442376 | tf_op jit(solution)/shard_map/cond/branch_1_fun/ppermute | solution.py:36
  59.8 7.6 %collective-permute-start.26 = (f32[2,9,2,8,128]{4,3,2,1,0:T(8,128)S(1)}, f32[2,9,2,8,128]{4,3,2,1,0:T(8,128)S(1)}, u32[]{:S(2)}, u32[]{:S(2)}) collective-permute-start(f32[2,9,2,8,128]{4,3,2,1,0:T(8,128)S(1)} %pad_maximum_fusion.7), channel_id=1, source_target_pairs={{0,3},{1,2},{2,1},{3,0},{4,7},{5,6},{6,5},{7,4},{8,11},{9,10},{10,... | collective-permute-start | bytes 442376 | tf_op jit(solution)/shard_map/cond/branch_1_fun/ppermute | solution.py:36
  68.9 6.9 %collective-permute-start.27 = (f32[12,2,8,128]{3,2,1,0:T(8,128)S(1)}, f32[12,2,8,128]{3,2,1,0:T(8,128)S(1)}, u32[]{:S(2)}, u32[]{:S(2)}) collective-permute-start(f32[12,2,8,128]{3,2,1,0:T(8,128)S(1)} %get-tuple-element.97), channel_id=1, source_target_pairs={{4,8},{12,16},{20,24},{8,4},{16,12},{24,20},{5,9},{13,17},{21,25},... | collective-permute-start | bytes 294920 | tf_op jit(solution)/shard_map/cond/branch_1_fun/ppermute | solution.py:67
  72.0 6.5 %collective-permute-start.28 = (f32[12,2,8,128]{3,2,1,0:T(8,128)S(1)}, f32[12,2,8,128]{3,2,1,0:T(8,128)S(1)}, u32[]{:S(2)}, u32[]{:S(2)}) collective-permute-start(f32[12,2,8,128]{3,2,1,0:T(8,128)S(1)} %get-tuple-element.98), channel_id=1, source_target_pairs={{0,4},{8,12},{16,20},{24,28},{4,0},{12,8},{20,16},{28,24},{1,5},{9... | collective-permute-start | bytes 294920 | tf_op jit(solution)/shard_map/cond/branch_1_fun/ppermute | solution.py:67
  80.0 6.7 %collective-permute-start.29 = (f32[12,2,8,128]{3,2,1,0:T(8,128)S(1)}, f32[12,2,8,128]{3,2,1,0:T(8,128)S(1)}, u32[]{:S(2)}, u32[]{:S(2)}) collective-permute-start(f32[12,2,8,128]{3,2,1,0:T(8,128)S(1)} %get-tuple-element.99), channel_id=1, source_target_pairs={{4,8},{12,16},{20,24},{8,4},{16,12},{24,20},{5,9},{13,17},{21,25},... | collective-permute-start | bytes 294920 | tf_op jit(solution)/shard_map/cond/branch_1_fun/ppermute | solution.py:67
  83.1 6.5 %collective-permute-start.30 = (f32[12,2,8,128]{3,2,1,0:T(8,128)S(1)}, f32[12,2,8,128]{3,2,1,0:T(8,128)S(1)}, u32[]{:S(2)}, u32[]{:S(2)}) collective-permute-start(f32[12,2,8,128]{3,2,1,0:T(8,128)S(1)} %get-tuple-element.100), channel_id=1, source_target_pairs={{0,4},{8,12},{16,20},{24,28},{4,0},{12,8},{20,16},{28,24},{1,5},{9... | collective-permute-start | bytes 294920 | tf_op jit(solution)/shard_map/cond/branch_1_fun/ppermute | solution.py:67
  91.1 6.7 %collective-permute-start.31 = (f32[12,2,8,128]{3,2,1,0:T(8,128)S(1)}, f32[12,2,8,128]{3,2,1,0:T(8,128)S(1)}, u32[]{:S(2)}, u32[]{:S(2)}) collective-permute-start(f32[12,2,8,128]{3,2,1,0:T(8,128)S(1)} %get-tuple-element.101), channel_id=1, source_target_pairs={{4,8},{12,16},{20,24},{8,4},{16,12},{24,20},{5,9},{13,17},{21,25},... | collective-permute-start | bytes 294920 | tf_op jit(solution)/shard_map/cond/branch_1_fun/ppermute | solution.py:67
  94.2 6.5 %collective-permute-start.32 = (f32[12,2,8,128]{3,2,1,0:T(8,128)S(1)}, f32[12,2,8,128]{3,2,1,0:T(8,128)S(1)}, u32[]{:S(2)}, u32[]{:S(2)}) collective-permute-start(f32[12,2,8,128]{3,2,1,0:T(8,128)S(1)} %get-tuple-element.102), channel_id=1, source_target_pairs={{0,4},{8,12},{16,20},{24,28},{4,0},{12,8},{20,16},{28,24},{1,5},{9... | collective-permute-start | bytes 294920 | tf_op jit(solution)/shard_map/cond/branch_1_fun/ppermute | solution.py:67
  102.2 6.7 %collective-permute-start.33 = (f32[12,2,8,128]{3,2,1,0:T(8,128)S(1)}, f32[12,2,8,128]{3,2,1,0:T(8,128)S(1)}, u32[]{:S(2)}, u32[]{:S(2)}) collective-permute-start(f32[12,2,8,128]{3,2,1,0:T(8,128)S(1)} %get-tuple-element.103), channel_id=1, source_target_pairs={{4,8},{12,16},{20,24},{8,4},{16,12},{24,20},{5,9},{13,17},{21,25},... | collective-permute-start | bytes 294920 | tf_op jit(solution)/shard_map/cond/branch_1_fun/ppermute | solution.py:67
  105.3 6.5 %collective-permute-start.34 = (f32[12,2,8,128]{3,2,1,0:T(8,128)S(1)}, f32[12,2,8,128]{3,2,1,0:T(8,128)S(1)}, u32[]{:S(2)}, u32[]{:S(2)}) collective-permute-start(f32[12,2,8,128]{3,2,1,0:T(8,128)S(1)} %get-tuple-element.104), channel_id=1, source_target_pairs={{0,4},{8,12},{16,20},{24,28},{4,0},{12,8},{20,16},{28,24},{1,5},{9... | collective-permute-start | bytes 294920 | tf_op jit(solution)/shard_map/cond/branch_1_fun/ppermute | solution.py:67
  113.2 2.2 %collective-permute-start.35 = (f32[10,2,8,128]{3,2,1,0:T(8,128)S(1)}, f32[10,2,8,128]{3,2,1,0:T(8,128)}, u32[]{:S(2)}, u32[]{:S(2)}) collective-permute-start(f32[10,2,8,128]{3,2,1,0:T(8,128)S(1)} %get-tuple-element.106), channel_id=1, source_target_pairs={{0,1},{1,0},{2,3},{3,2},{4,5},{5,4},{6,7},{7,6},{8,9},{9,8},{10,11... | collective-permute-start | bytes 245768 | tf_op jit(solution)/shard_map/cond/branch_1_fun/ppermute | solution.py:36
  113.7 4.1 %collective-permute-start.36 = (f32[10,2,8,128]{3,2,1,0:T(8,128)S(1)}, f32[10,2,8,128]{3,2,1,0:T(8,128)}, u32[]{:S(2)}, u32[]{:S(2)}) collective-permute-start(f32[10,2,8,128]{3,2,1,0:T(8,128)S(1)} %get-tuple-element.107), channel_id=1, source_target_pairs={{0,2},{1,3},{2,0},{3,1},{4,6},{5,7},{6,4},{7,5},{8,10},{9,11},{10,... | collective-permute-start | bytes 245768 | tf_op jit(solution)/shard_map/cond/branch_1_fun/ppermute | solution.py:36
  114.8 5.0 %collective-permute-start.37 = (f32[10,2,8,128]{3,2,1,0:T(8,128)S(1)}, f32[10,2,8,128]{3,2,1,0:T(8,128)}, u32[]{:S(2)}, u32[]{:S(2)}) collective-permute-start(f32[10,2,8,128]{3,2,1,0:T(8,128)S(1)} %get-tuple-element.108), channel_id=1, source_target_pairs={{0,3},{1,2},{2,1},{3,0},{4,7},{5,6},{6,5},{7,4},{8,11},{9,10},{10,... | collective-permute-start | bytes 245768 | tf_op jit(solution)/shard_map/cond/branch_1_fun/ppermute | solution.py:36

commit v3 on v2

v3 whole, which is shorter than its diff:
```python
import functools

import jax
import jax.numpy as jnp
from jax import lax
from jax.experimental import pallas as pl
from jax.experimental.pallas import tpu as pltpu
from jax.sharding import PartitionSpec as P

TILE = 128
CAP = 5
TICKS = 6
KINDS = 4
SLOTS = KINDS * CAP
LIVE = 2 * CAP
SIDE = 2 * CAP - 2
STRIDE = 16
SHORT = 12
SHIFT = 1024

VMEM = pl.BlockSpec(memory_space=pltpu.VMEM)
SMEM = pl.BlockSpec(memory_space=pltpu.SMEM)
HBM = pl.BlockSpec(memory_space=pltpu.HBM)
PARAMS = pltpu.CompilerParams(vmem_limit_bytes=24 * 1024 * 1024)


def is_power(count):
    return count & (count - 1) == 0


def swap_tile(block, offset):
    count = lax.axis_size("tile")
    partner = (lambda i: i ^ offset) if is_power(count) else (lambda i: (i + offset) % count)
    return lax.ppermute(block, "tile", [(i, partner(i)) for i in range(count)])


def source_of(place, offset, count):
    return place ^ offset if is_power(count) else (place - offset + count) % count


def target_of(place, offset, count):
    return place ^ offset if is_power(count) else (place + offset) % count


def direct_groups(own):
    count = lax.axis_size("tile")
    if is_power(count):
        offsets = [1 << bit for bit in reversed(range(count.bit_length() - 1))]
    else:
        offsets = range(1, count)
    return {0: own, **{offset: swap_tile(own, offset) for offset in offsets}}


def all_groups(groups):
    groups = dict(groups)
    count = lax.axis_size("tile")
    for offset in sorted(range(count), key=lambda k: bin(k).count("1")):
        if offset not in groups:
            groups[offset] = swap_tile(groups[offset & (offset - 1)], offset & -offset)
    return [groups[offset] for offset in range(count)]


def swap_layers(first, second):
    layers = lax.axis_size("layer")

    def swap(block, start):
        pairs = [(i, i + 1) for i in range(start, layers - 1, 2)]
        return lax.ppermute(block, "layer", pairs + [(b, a) for a, b in pairs])

    return swap(first, 1), swap(second, 0)


def codes_kernel(tiles_dev, where_ref, rowcol_ref, counts_ref, codes_ref, rows_ref, order_ref):
    place = where_ref[1]

    def scan(want_live, rank):
        for slot in range(SLOTS):
            live = counts_ref[slot // CAP] > slot % CAP

            @pl.when((live == want_live) & (rank < LIVE))
            def _():
                order_ref[rank] = slot

            rank = rank + (live == want_live).astype(jnp.int32)
        return rank

    live_slots = scan(True, jnp.int32(0))
    scan(False, live_slots)
    lanes = codes_ref.shape[-1]
    lane = lax.broadcasted_iota(jnp.int32, (1, lanes), 1)
    codes = jnp.zeros((1, lanes), jnp.int32)
    for j in range(LIVE):
        slot = order_ref[j]
        kind = lax.div(slot, CAP)
        alive = j < live_slots
        code = rowcol_ref[slot, 0] * 65536 + rowcol_ref[slot, 1] * 8 + kind * 2 + 1
        code = jnp.where(alive, code, 0)
        codes = jnp.where(lane == place * STRIDE + j, code, codes)
        rows_ref[0, j] = lax.shift_right_logical(kind, 1)
        rows_ref[1, j] = jnp.where(alive, rowcol_ref[slot, 0] - place * tiles_dev, 0)
    codes_ref[...] = jnp.broadcast_to(codes[None], codes_ref.shape)


def slot_codes(where, pairs, live_counts, receivers, lanes, tiles_dev):
    return pl.pallas_call(
        functools.partial(codes_kernel, tiles_dev),
        out_shape=(
            jax.ShapeDtypeStruct((receivers, 1, lanes), jnp.int32),
            jax.ShapeDtypeStruct((2, STRIDE), jnp.int32),
            jax.ShapeDtypeStruct((STRIDE,), jnp.int32),
        ),
        in_specs=[SMEM, SMEM, SMEM],
        out_specs=(VMEM, SMEM, SMEM),
        compiler_params=PARAMS,
        name="slot_codes",
    )(where, pairs, live_counts)


def pack_kernel(order_ref, green_ref, packed_ref, sems):
    copies = []
    for j in range(LIVE):
        copy = pltpu.make_async_copy(green_ref.at[order_ref[j]], packed_ref.at[j], sems.at[j])
        copy.start()
        copies.append(copy)
    for copy in copies:
        copy.wait()


def pack_green(order, green):
    return pl.pallas_call(
        pack_kernel,
        out_shape=jax.ShapeDtypeStruct((LIVE,) + green.shape[1:], green.dtype),
        in_specs=[SMEM, HBM],
        out_specs=VMEM,
        scratch_shapes=[pltpu.SemaphoreType.DMA((LIVE,))],
        compiler_params=PARAMS,
        name="pack_green",
    )(order, green)


def lists_kernel(layers, devices, tiles_dev, where_ref, table_ref, out_ref):
    lanes = table_ref.shape[-1]
    tiles = tiles_dev * devices
    layer, place = where_ref[0], where_ref[1]
    tile = lax.broadcasted_iota(jnp.int32, (tiles, lanes), 0)
    lane = lax.broadcasted_iota(jnp.int32, (tiles, lanes), 1)

    def codes_of(index):
        total = table_ref[index * devices]
        for device in range(1, devices):
            total = total + table_ref[index * devices + device]
        return total

    def unpack(code):
        kind = (code >> 1) & 3
        return (code & 1) == 1, code >> 16, (code >> 3) & 8191, kind >> 1, (kind ^ (kind >> 1)) & 1

    def hots(code):
        alive, row, col, wdir, rdir = unpack(code)
        return (row == tile) & alive, (col == tile) & alive, wdir, rdir

    def column(hot):
        return jnp.minimum(jnp.sum(jnp.where(hot, 1.0, 0.0), axis=1, keepdims=True), 1.0)

    def columns(code):
        row_hot, col_hot, wdir, rdir = hots(code)
        return [column(h & (side == d)) for h, side in ((row_hot, wdir), (col_hot, rdir)) for d in range(2)]

    def one(index, carry):
        w0, w1, r0, r1, most_sent = carry
        v0, v1, q0, q1 = columns(codes_of(index))
        most_sent = jnp.maximum(most_sent, jnp.sum(w0 * q0, axis=0, keepdims=True))
        most_sent = jnp.maximum(most_sent, jnp.sum(v1 * r1, axis=0, keepdims=True))
        return v0, v1, q0, q1, most_sent

    none = jnp.zeros((1, 1), jnp.float32)
    start = (*columns(codes_of(0)), none)
    most_sent = lax.fori_loop(1, layers, one, start)[4]

    has_above = layer > 0
    has_below = layer < layers - 1
    mine = codes_of(layer)
    above = jnp.where(has_above, codes_of(jnp.maximum(layer - 1, 0)), 0)
    below = jnp.where(has_below, codes_of(jnp.minimum(layer + 1, layers - 1)), 0)
    w0, w1, r0, r1 = columns(mine)
    r0 = jnp.where(has_above, r0, 0.0)
    r1 = jnp.where(has_below, r1, 0.0)
    above_w0, _, _, want_up = columns(above)
    _, below_w1, want_down, _ = columns(below)
    chosen = [w0 * want_down, w1 * want_up, above_w0 * r0, below_w1 * r1]
    matrix = jnp.zeros((tiles, lanes), jnp.float32)
    for j, values in enumerate(chosen):
        matrix = jnp.where(lane == j, values, matrix)
    matrix = matrix.astype(jnp.bfloat16)
    at = lax.broadcasted_iota(jnp.int32, (tiles, tiles), 0)
    other = lax.broadcasted_iota(jnp.int32, (tiles, tiles), 1)

    def group_of(index):
        total = jnp.zeros_like(index)
        for device in range(1, devices):
            total = total + jnp.where(index >= device * tiles_dev, 1, 0)
        return total

    before = other < at
    before = jnp.where(before, 1.0, 0.0).astype(jnp.bfloat16)
    position = jnp.dot(before, matrix, preferred_element_type=jnp.float32)

    def entry(j):
        return chosen[j] * (position[:, j : j + 1] + 1.0)

    row_hot, col_hot, wdir, rdir = hots(mine)

    def look(hot, side, down, up):
        values = jnp.where(hot, jnp.where(side == 0, down, up), 0.0)
        return jnp.sum(values, axis=0, keepdims=True).astype(jnp.int32) - 1

    odd = layer & 1
    send = look(row_hot, wdir, entry(0), entry(1))
    recv = look(col_hot, rdir, entry(2), entry(3))
    alive, _, col, _, _ = unpack(mine)
    send_buf = jnp.where(odd == 1, wdir, 1 - wdir)
    recv_buf = jnp.where(odd == 1, 1 - rdir, rdir)
    group = group_of(col)
    if is_power(devices):
        offset = group ^ place
    else:
        offset = jnp.where(group > place, place + devices - group, place - group)
    send = jnp.where(send < 0, -1, send_buf * SHIFT + send)
    recv = jnp.where(recv < 0, -1, recv_buf * SHIFT + recv)
    src = jnp.where(alive, (offset * 2 + recv_buf) * SHIFT + col - group * tiles_dev, -1)

    lane_row = lane[:1]
    facts = jnp.where(lane_row == 0, most_sent.astype(jnp.int32), place)
    for j, values in enumerate((send, recv, src, facts)):
        out_ref[j : j + 1] = values
    out_ref[4:] = jnp.zeros((out_ref.shape[0] - 4, lanes), jnp.int32)


def build_lists(where, table, layers, devices, tiles_dev):
    return pl.pallas_call(
        functools.partial(lists_kernel, layers, devices, tiles_dev),
        out_shape=jax.ShapeDtypeStruct((8, table.shape[-1]), jnp.int32),
        in_specs=[SMEM, VMEM],
        out_specs=VMEM,
        compiler_params=PARAMS,
        name="build_lists",
    )(where, table)


def split_kernel(green_ref, high_ref, low_ref):
    for slot in range(green_ref.shape[0]):
        for part in range(2):
            block = green_ref[slot, part].T
            high = block.astype(jnp.bfloat16)
            low = (block - high.astype(jnp.float32)).astype(jnp.bfloat16)
            high_ref[slot, :, part * TILE : (part + 1) * TILE] = high
            low_ref[slot, :, part * TILE : (part + 1) * TILE] = low


def split_green(packed):
    shape = jax.ShapeDtypeStruct((packed.shape[0], TILE, 2 * TILE), jnp.bfloat16)
    return pl.pallas_call(
        split_kernel,
        out_shape=(shape, shape),
        in_specs=[VMEM],
        out_specs=(VMEM, VMEM),
        compiler_params=PARAMS,
        name="split_green",
    )(packed)


def block_term(x, high, low):
    parts, sub, _ = x.shape
    rows = parts * sub
    flat = x.reshape(rows, TILE)
    top = flat.astype(jnp.bfloat16)
    rest = (flat - top.astype(jnp.float32)).astype(jnp.bfloat16)
    main = jnp.dot(jnp.concatenate([top, rest], axis=0), high, preferred_element_type=jnp.float32)
    prod = main[:rows] + main[rows:] + jnp.dot(top, low, preferred_element_type=jnp.float32)
    real = prod[:sub, :TILE] - prod[sub:, TILE:]
    imag = prod[:sub, TILE:] + prod[sub:, :TILE]
    return real, imag


def tick_kernel(stage, devices, lists_ref, *refs):
    refs = list(refs)
    highs = [refs.pop(0) for _ in range(devices)]
    lows = [refs.pop(0) for _ in range(devices)]
    place = lists_ref[3, 1]

    def position(row, lane, cap, empty):
        value = lists_ref[row, lane]
        found = lax.shift_right_logical(value, 10) * cap + (value & (SHIFT - 1))
        return jnp.where(value < 0, empty, found)

    if stage == "first":
        came = [refs.pop(0) for _ in range(devices)]
        out_a, out_b, x_out, traces, acc = refs
        for j, ref in enumerate(came):
            traces[2 * j : 2 * j + 2] = ref[...]
    else:
        xs, came_a, came_b = refs.pop(0), refs.pop(0), refs.pop(0)
        got = refs.pop()
        if stage == "middle":
            out_a, out_b, acc = refs
        else:
            outs = refs
        got_cap = came_a.shape[0]
        got_empty = 2 * got_cap
        got[:got_cap] = came_a[...]
        got[got_cap:got_empty] = came_b[...]
        got[got_empty] = jnp.zeros(got.shape[1:], jnp.float32)
    if stage != "last":
        cap = out_a.shape[0]
        acc[...] = jnp.zeros_like(acc)
    for group in range(devices):
        base = source_of(place, group, devices) * STRIDE
        for j in range(LIVE):
            slot = group * LIVE + j
            high, low = highs[group][j], lows[group][j]
            if stage == "first":
                value = lists_ref[2, base + j]
                piece = jnp.maximum(lax.shift_right_arithmetic(value, 10), 0)
                start = pl.multiple_of(jnp.where(value < 0, 0, value & (SHIFT - 1)) * TILE, TILE)
                x = traces[piece, :, :, pl.ds(start, TILE)]
                x = jnp.where(value < 0, jnp.zeros_like(x), x)
                x_out[slot] = x
            else:
                x = xs[slot] + got[position(1, base + j, got_cap, got_empty)]
            real, imag = block_term(x, high, low)
            if stage == "last":
                outs[group][j, 0] = real
                outs[group][j, 1] = imag
            else:
                at = position(0, base + j, cap, 2 * cap)
                acc[at, 0] += real
                acc[at, 1] += imag
    if stage != "last":
        out_a[...] = acc[:cap]
        out_b[...] = acc[cap : 2 * cap]


def tick(stage, devices, cap, lists, blocks, *data):
    sub = data[-1].shape[-2]
    tile_shape = lambda count: jax.ShapeDtypeStruct((count, 2, sub, TILE), jnp.float32)
    room = lambda count: pltpu.VMEM((count, 2, sub, TILE), jnp.float32)
    if stage == "first":
        out_shape = (tile_shape(cap), tile_shape(cap), tile_shape(devices * LIVE))
        scratch = [pltpu.VMEM((2 * devices,) + data[0].shape[1:], jnp.float32), room(2 * cap + 1)]
    elif stage == "middle":
        out_shape = (tile_shape(cap), tile_shape(cap))
        scratch = [room(2 * cap + 1), room(2 * cap + 1)]
    else:
        out_shape = tuple(tile_shape(LIVE) for _ in range(devices))
        scratch = [room(2 * cap + 1)]
    operands = (*blocks, *data)
    return pl.pallas_call(
        functools.partial(tick_kernel, stage, devices),
        out_shape=out_shape,
        in_specs=[SMEM] + [VMEM] * len(operands),
        out_specs=tuple(VMEM for _ in out_shape),
        scratch_shapes=scratch,
        compiler_params=PARAMS,
        name="tick_" + stage,
    )(lists, *operands)


def finish_kernel(where_ref, rows_ref, sources_ref, *refs):
    out_ref = refs[-1]
    terms = refs[:-1]
    out_ref[...] = sources_ref[...]
    devices = len(terms)
    sub = terms[0].shape[2]
    place = where_ref[1]
    for j in range(LIVE):
        direction = rows_ref[0, j]
        start = pl.multiple_of(rows_ref[1, j] * TILE, TILE)
        for offset, term in enumerate(terms):
            shot = pl.multiple_of(target_of(place, offset, devices) * sub, sub)
            for part in range(2):
                at = (direction, part, pl.ds(shot, sub), pl.ds(start, TILE))
                out_ref[at] += term[j, part]


def finish(where, rows, sources, terms):
    return pl.pallas_call(
        finish_kernel,
        out_shape=jax.ShapeDtypeStruct(sources.shape, sources.dtype),
        in_specs=[SMEM, SMEM] + [VMEM] * (1 + len(terms)),
        out_specs=VMEM,
        compiler_params=PARAMS,
        name="finish",
    )(where, rows, sources, *terms)


def sweeps(cap, lists, came, blocks):
    devices = lax.axis_size("tile")
    out_a, out_b, xs = tick("first", devices, cap, lists, blocks, *came)
    for _ in range(TICKS - 3):
        out_a, out_b = tick("middle", devices, cap, lists, blocks, xs, *swap_layers(out_a, out_b))
    terms = tick("last", devices, cap, lists, blocks, xs, *swap_layers(out_a, out_b))
    back = [terms[0]]
    for offset in range(1, devices):
        back.append(swap_tile(terms[offset], offset if is_power(devices) else devices - offset))
    return tuple(back)


def body(sources, green, rowcol, counts):
    devices = lax.axis_size("tile")
    layers = lax.axis_size("layer")
    tiles_dev = sources.shape[-1] // TILE
    local = sources[0]
    lanes = -(-devices * STRIDE // 128) * 128
    where = jnp.stack([lax.axis_index("layer"), lax.axis_index("tile")]).astype(jnp.int32)

    codes, rows, order = slot_codes(where, rowcol[0], counts[0], layers * devices, lanes, tiles_dev)
    groups = direct_groups(pack_green(order, green[0]))
    layer, place = lax.axis_index("layer"), lax.axis_index("tile")
    near = swap_layers(
        lax.dynamic_index_in_dim(local, 1 - layer % 2, keepdims=False),
        lax.dynamic_index_in_dim(local, layer % 2, keepdims=False),
    )
    table = lax.all_to_all(codes, ("layer", "tile"), 0, 0, tiled=True)
    near, groups, table = lax.optimization_barrier((near, groups, table))
    sub = local.shape[2] // devices

    def shots_of(offset):
        shot = target_of(place, offset, devices) * sub
        return jnp.stack([lax.dynamic_slice_in_dim(block, shot, sub, axis=1) for block in near])

    came = [shots_of(0)] + [swap_tile(shots_of(offset), offset) for offset in range(1, devices)]
    groups = all_groups(groups)
    lists = build_lists(where, table, layers, devices, tiles_dev)
    highs, lows = zip(*[split_green(group) for group in groups])
    cap = SIDE * devices
    short = min(SHORT, cap)
    terms = lax.cond(
        lists[3, 0] <= short,
        functools.partial(sweeps, short),
        functools.partial(sweeps, cap),
        lists,
        came,
        highs + lows,
    )
    return finish(where, rows, local, terms)[None]


def solution(mesh):
    return jax.shard_map(
        body,
        mesh=mesh,
        in_specs=(
            P("layer", None, None, None, "tile"),
            P("layer", "tile", None, None, None),
            P("layer", "tile", None),
            P("layer", "tile"),
        ),
        out_specs=P("layer", None, None, None, "tile"),
        check_vma=False,
    )
```

time: 122 us -> 108 us (0.89)
  waiting for transfers between devices: 58.6 us -> 27.8 us
  blocking collectives: 11.1 us -> 25.5 us
  Pallas kernels: 17.3 us -> 20.9 us
    ppermute x12 -> x9, waiting for transfers between devices: 26.7 us -> 7.14 us  [swap_tile(): return lax.ppermute(block, 'tile', [(i, partner(i)) for i in range(count)])]
    all_to_all x1, blocking collectives: 11.1 us -> 25.5 us  [body(): table = lax.all_to_all(codes, ('layer', 'tile'), 0, 0, tiled=True)]
    ppermute x10, waiting for transfers between devices: 31.9 us -> 20.7 us  [swap(): return lax.ppermute(block, 'layer', pairs + [(b, a) for a, b in pairs])]
    ppermute x12 -> x9, starting transfers between devices: 12 us -> 7.32 us  [swap_tile(): return lax.ppermute(block, 'tile', [(i, partner(i)) for i in range(count)])]
    pallas_call x8 -> x4, Pallas kernels: 1.9 us -> 5.57 us  [split_green(): pl.pallas_call(split_kernel, out_shape=(shape, shape), in_specs=[VMEM], o...]
    ppermute x10, starting transfers between devices: 17.4 us -> 21.1 us  [swap(): return lax.ppermute(block, 'layer', pairs + [(b, a) for a, b in pairs])]
  transfers between devices with their start and end apart: 22 -> 19, of which waited for: 16 -> 11; matrix products, arithmetic and copies ran while one was open for 1% -> 1% of each run, Pallas kernels for 4% -> 7%
where the time goes in v3:
time: 108 us; the launch traced here: 107 us
  starting transfers between devices  28.4 us (26%)
  waiting for transfers between devices  27.8 us (26%)
  blocking collectives  25.5 us (24%)
  Pallas kernels  20.9 us (19%)
  local copies, waits for them, and re-layouts  3.82 us (4%)
    all_to_all x1, blocking collectives, body(): table = lax.all_to_all(codes, ('layer', 'tile'), 0, 0, tiled=True)  25.5 us
    ppermute x10, starting transfers between devices, swap(): return lax.ppermute(block, 'layer', pairs + [(b, a) for a, b in pairs])  21.1 us
    ppermute x10, waiting for transfers between devices, swap(): return lax.ppermute(block, 'layer', pairs + [(b, a) for a, b in pairs])  20.7 us
    pallas_call x5, Pallas kernels, tick(): pl.pallas_call(functools.partial(tick_kernel, stage, devices), out_shape=...  7.33 us
    ppermute x9, starting transfers between devices, swap_tile(): return lax.ppermute(block, 'tile', [(i, partner(i)) for i in range(count)])  7.32 us
    ppermute x9, waiting for transfers between devices, swap_tile(): return lax.ppermute(block, 'tile', [(i, partner(i)) for i in range(count)])  7.14 us
    pallas_call x4, Pallas kernels, split_green(): pl.pallas_call(split_kernel, out_shape=(shape, shape), in_specs=[VMEM], o...  5.57 us
    unnamed x6, local copies, waits for them, and re-layouts  2.39 us
  transfers between devices with their start and end apart: 19, of which 11 were waited for; matrix products, arithmetic and copies ran while one was open for 1% of the time, Pallas kernels for 7%

profile of v3, /device:TPU:9, one launch (start us, length us, event | category | flops | bytes accessed | tf_op | source)
XLA Modules:
  0.0 107.4 jit_solution(8515278973724403276)
XLA Ops:
  0.0 0.8 copy.5.rowcol_ref
  0.8 0.1 pad_add_fusion.where_ref
  0.8 0.0 copy-start.2
  0.8 0.7 copy-done.2
  1.5 1.5 %slot_codes.1 = (s32[32,1,128]{2,1,0:T(1,128)S(1)}, s32[2,16]{1,0:T(2,128)S(1)}, s32[16]{0:T(128)S(1)}) custom-call(s32[2]{0:T(128)S(1)} %pad_add_fusion.where_ref, s32[20,2]{1,0:T(8,128)S(1)} %copy.5.rowcol_ref, s32[4]{0:T(128)S(1)} %bitcast.30), custom_call_target="tpu_custom_call" | custom-call | tf_op jit(solution)/shard_map/slot_codes/pallas_call | solution.py:105
  3.0 0.0 copy-start.1
  3.0 1.7 %copy-done.1 = f32[1,20,2,128,128]{4,3,2,1,0:T(8,128)S(1)} copy-done((f32[1,20,2,128,128]{4,3,2,1,0:T(8,128)S(1)}, f32[1,20,2,128,128]{4,3,2,1,0:T(8,128)}, u32[]{:S(2)}) %copy-start.1) | copy-done | bytes 2621464
  4.8 0.0 copy-start
  4.8 2.4 %pack_green.1.green_ref = f32[10,2,128,128]{3,2,1,0:T(8,128)S(1)} custom-call(s32[16]{0:T(128)S(1)} %get-tuple-element.131.order_ref, f32[20,2,128,128]{3,2,1,0:T(8,128)S(1)} %bitcast.29), custom_call_target="tpu_custom_call" | custom-call | tf_op jit(solution)/shard_map/pack_green/pallas_call | solution.py:130
  7.2 1.3 %collective-permute-start.25 = (f32[10,2,128,128]{3,2,1,0:T(8,128)S(1)}, f32[10,2,128,128]{3,2,1,0:T(8,128)}, u32[]{:S(2)}, u32[]{:S(2)}) collective-permute-start(f32[10,2,128,128]{3,2,1,0:T(8,128)S(1)} %pack_green.1.green_ref), channel_id=1, source_target_pairs={{0,2},{1,3},{2,0},{3,1},{4,6},{5,7},{6,4},{7,5},{8,10},{9,11},{10,... | collective-permute-start | bytes 3932168 | tf_op jit(solution)/shard_map/ppermute | solution.py:34
  8.5 1.0 collective-permute-start.24
  9.4 0.0 copy-done
  9.4 0.1 dynamic-slice_bitcast_fusion
  9.5 1.3 %collective-permute-start.23 = (f32[2,32,2048]{2,1,0:T(8,128)S(1)}, f32[2,32,2048]{2,1,0:T(8,128)S(1)}, u32[]{:S(2)}, u32[]{:S(2)}) collective-permute-start(f32[2,32,2048]{2,1,0:T(8,128)S(1)} %get-tuple-element.151), channel_id=1, source_target_pairs={{0,4},{8,12},{16,20},{24,28},{4,0},{12,8},{20,16},{28,24},{1,5},{9... | collective-permute-start | bytes 1572872 | tf_op jit(solution)/shard_map/ppermute | solution.py:68
  10.8 2.0 %collective-permute-start.22 = (f32[2,32,2048]{2,1,0:T(8,128)S(1)}, f32[2,32,2048]{2,1,0:T(8,128)S(1)}, u32[]{:S(2)}, u32[]{:S(2)}) collective-permute-start(f32[2,32,2048]{2,1,0:T(8,128)S(1)} %get-tuple-element.152), channel_id=1, source_target_pairs={{4,8},{12,16},{20,24},{8,4},{16,12},{24,20},{5,9},{13,17},{21,25},... | collective-permute-start | bytes 1572872 | tf_op jit(solution)/shard_map/ppermute | solution.py:68
  12.8 25.5 %all_to_all.5.table_ref = s32[32,1,128]{2,1,0:T(1,128)S(1)} all-to-all(s32[32,1,128]{2,1,0:T(1,128)S(1)} %get-tuple-element.132), channel_id=1, replica_groups=mesh['layer'=8,'tile'=4] {'layer','tile'}, dimensions={0} | all-to-all | bytes 32768 | tf_op jit(solution)/shard_map/all_to_all | solution.py:423
  38.3 0.0 collective-permute-done.23
  38.3 0.0 collective-permute-done.22
  38.3 0.0 collective-permute-done.25.green_ref
  38.3 0.0 collective-permute-done.24.green_ref
  38.3 0.5 collective-permute-start.26
  38.8 0.1 dynamic-slice_bitcast_fusion.2
  38.9 0.2 collective-permute-start.27
  39.1 1.3 %collective-permute-start.28 = (f32[2,2,8,2048]{3,2,1,0:T(8,128)S(1)}, f32[2,2,8,2048]{3,2,1,0:T(8,128)S(1)}, u32[]{:S(2)}, u32[]{:S(2)}) collective-permute-start(f32[2,2,8,2048]{3,2,1,0:T(8,128)S(1)} %pad_maximum_fusion.2), channel_id=1, source_target_pairs={{0,2},{1,3},{2,0},{3,1},{4,6},{5,7},{6,4},{7,5},{8,10},{9,11},{10,... | collective-permute-start | bytes 786440 | tf_op jit(solution)/shard_map/ppermute | solution.py:34
  40.4 0.9 collective-permute-start.29
  41.3 1.7 %split_green.6 = (bf16[10,128,256]{2,1,0:T(8,128)(2,1)S(1)}, bf16[10,128,256]{2,1,0:T(8,128)(2,1)S(1)}) custom-call(f32[10,2,128,128]{3,2,1,0:T(8,128)} %collective-permute-done.25.green_ref), custom_call_target="tpu_custom_call" | custom-call | tf_op jit(solution)/shard_map/split_green/pallas_call | solution.py:262
  43.0 1.9 %build_lists.1 = s32[8,128]{1,0:T(8,128)S(1)} custom-call(s32[2]{0:T(128)S(1)} %pad_add_fusion.where_ref, s32[32,1,128]{2,1,0:T(1,128)S(1)} %all_to_all.5.table_ref), custom_call_target="tpu_custom_call" | custom-call | tf_op jit(solution)/shard_map/build_lists/pallas_call | solution.py:240
  44.9 0.5 slice.3
  46.0 0.4 split_green.4
  46.5 1.7 %split_green.5 = (bf16[10,128,256]{2,1,0:T(8,128)(2,1)S(1)}, bf16[10,128,256]{2,1,0:T(8,128)(2,1)S(1)}) custom-call(f32[10,2,128,128]{3,2,1,0:T(8,128)} %collective-permute-done.24.green_ref), custom_call_target="tpu_custom_call" | custom-call | tf_op jit(solution)/shard_map/split_green/pallas_call | solution.py:262
  48.2 0.0 collective-permute-done.26.green_ref
  48.2 1.7 %split_green.7 = (bf16[10,128,256]{2,1,0:T(8,128)(2,1)S(1)}, bf16[10,128,256]{2,1,0:T(8,128)(2,1)S(1)}) custom-call(f32[10,2,128,128]{3,2,1,0:T(8,128)} %collective-permute-done.26.green_ref), custom_call_target="tpu_custom_call" | custom-call | tf_op jit(solution)/shard_map/split_green/pallas_call | solution.py:262
  50.0 0.0 collective-permute-done.27
  50.0 0.0 collective-permute-done.28
  50.0 2.8 %collective-permute-done.29 = f32[2,2,8,2048]{3,2,1,0:T(8,128)S(1)} collective-permute-done((f32[2,2,8,2048]{3,2,1,0:T(8,128)S(1)}, f32[2,2,8,2048]{3,2,1,0:T(8,128)S(1)}, u32[]{:S(2)}, u32[]{:S(2)}) %collective-permute-start.29) | collective-permute-done | bytes 262176 | tf_op jit(solution)/shard_map/ppermute | solution.py:34
  52.8 52.5 %conditional.1 = (f32[10,2,8,128]{3,2,1,0:T(8,128)S(1)}, f32[10,2,8,128]{3,2,1,0:T(8,128)}, f32[10,2,8,128]{3,2,1,0:T(8,128)}, f32[10,2,8,128]{3,2,1,0:T(8,128)}) conditional(s32[]{:T(128)} %bitcast.8, (s32[8,128]{1,0:T(8,128)S(1)}, bf16[10,128,256]{2,1,0:T(8,128)(2,1)S(1)}, bf16[10,128,256]{2,1,0:T(8,128)(2,1)S(1)}, ...), branch_computations={%region_0.1_spmd, %region_1.2_spmd} | conditional | bytes 9372120 | solution.py:437
  52.8 1.5 %tick_first.3 = (f32[12,2,8,128]{3,2,1,0:T(8,128)S(1)}, f32[12,2,8,128]{3,2,1,0:T(8,128)S(1)}, f32[40,2,8,128]{3,2,1,0:T(8,128)S(1)}) custom-call(s32[8,128]{1,0:T(8,128)S(1)} %get-tuple-element.83.lists_ref, bf16[10,128,256]{2,1,0:T(8,128)(2,1)S(1)} %get-tuple-element.84.refs_0_, bf16[10,128,256]{2,1,0:T(8,128)(2,1)S(1)} %get-tuple-element.85.refs_1_, ...), custom_call_target="tpu_custom_call" | custom-call | tf_op jit(solution)/shard_map/cond/branch_1_fun/tick_first/pallas_call | solution.py:357
  54.3 3.0 %collective-permute-start.11 = (f32[12,2,8,128]{3,2,1,0:T(8,128)S(1)}, f32[12,2,8,128]{3,2,1,0:T(8,128)S(1)}, u32[]{:S(2)}, u32[]{:S(2)}) collective-permute-start(f32[12,2,8,128]{3,2,1,0:T(8,128)S(1)} %get-tuple-element.97), channel_id=1, source_target_pairs={{4,8},{12,16},{20,24},{8,4},{16,12},{24,20},{5,9},{13,17},{21,25},... | collective-permute-start | bytes 294920 | tf_op jit(solution)/shard_map/cond/branch_1_fun/ppermute | solution.py:68
  57.3 1.4 %collective-permute-start.12 = (f32[12,2,8,128]{3,2,1,0:T(8,128)S(1)}, f32[12,2,8,128]{3,2,1,0:T(8,128)S(1)}, u32[]{:S(2)}, u32[]{:S(2)}) collective-permute-start(f32[12,2,8,128]{3,2,1,0:T(8,128)S(1)} %get-tuple-element.98), channel_id=1, source_target_pairs={{0,4},{8,12},{16,20},{24,28},{4,0},{12,8},{20,16},{28,24},{1,5},{9... | collective-permute-start | bytes 294920 | tf_op jit(solution)/shard_map/cond/branch_1_fun/ppermute | solution.py:68
  58.7 2.9 %collective-permute-done.11.refs_9_ = f32[12,2,8,128]{3,2,1,0:T(8,128)S(1)} collective-permute-done((f32[12,2,8,128]{3,2,1,0:T(8,128)S(1)}, f32[12,2,8,128]{3,2,1,0:T(8,128)S(1)}, u32[]{:S(2)}, u32[]{:S(2)}) %collective-permute-start.11) | collective-permute-done | bytes 98336 | tf_op jit(solution)/shard_map/cond/branch_1_fun/ppermute | solution.py:68
  61.6 2.3 %collective-permute-done.12.refs_10_ = f32[12,2,8,128]{3,2,1,0:T(8,128)S(1)} collective-permute-done((f32[12,2,8,128]{3,2,1,0:T(8,128)S(1)}, f32[12,2,8,128]{3,2,1,0:T(8,128)S(1)}, u32[]{:S(2)}, u32[]{:S(2)}) %collective-permute-start.12) | collective-permute-done | bytes 98336 | tf_op jit(solution)/shard_map/cond/branch_1_fun/ppermute | solution.py:68
  63.9 1.5 %tick_middle.9 = (f32[12,2,8,128]{3,2,1,0:T(8,128)S(1)}, f32[12,2,8,128]{3,2,1,0:T(8,128)S(1)}) custom-call(s32[8,128]{1,0:T(8,128)S(1)} %get-tuple-element.83.lists_ref, bf16[10,128,256]{2,1,0:T(8,128)(2,1)S(1)} %get-tuple-element.84.refs_0_, bf16[10,128,256]{2,1,0:T(8,128)(2,1)S(1)} %get-tuple-element.85.refs_1_, ...), custom_call_target="tpu_custom_call" | custom-call | tf_op jit(solution)/shard_map/cond/branch_1_fun/tick_middle/pallas_call | solution.py:357
  65.4 3.0 %collective-permute-start.13 = (f32[12,2,8,128]{3,2,1,0:T(8,128)S(1)}, f32[12,2,8,128]{3,2,1,0:T(8,128)S(1)}, u32[]{:S(2)}, u32[]{:S(2)}) collective-permute-start(f32[12,2,8,128]{3,2,1,0:T(8,128)S(1)} %get-tuple-element.99), channel_id=1, source_target_pairs={{4,8},{12,16},{20,24},{8,4},{16,12},{24,20},{5,9},{13,17},{21,25},... | collective-permute-start | bytes 294920 | tf_op jit(solution)/shard_map/cond/branch_1_fun/ppermute | solution.py:68
  68.4 1.4 %collective-permute-start.14 = (f32[12,2,8,128]{3,2,1,0:T(8,128)S(1)}, f32[12,2,8,128]{3,2,1,0:T(8,128)S(1)}, u32[]{:S(2)}, u32[]{:S(2)}) collective-permute-start(f32[12,2,8,128]{3,2,1,0:T(8,128)S(1)} %get-tuple-element.100), channel_id=1, source_target_pairs={{0,4},{8,12},{16,20},{24,28},{4,0},{12,8},{20,16},{28,24},{1,5},{9... | collective-permute-start | bytes 294920 | tf_op jit(solution)/shard_map/cond/branch_1_fun/ppermute | solution.py:68
  69.9 2.2 %collective-permute-done.13.refs_9_ = f32[12,2,8,128]{3,2,1,0:T(8,128)S(1)} collective-permute-done((f32[12,2,8,128]{3,2,1,0:T(8,128)S(1)}, f32[12,2,8,128]{3,2,1,0:T(8,128)S(1)}, u32[]{:S(2)}, u32[]{:S(2)}) %collective-permute-start.13) | collective-permute-done | bytes 98336 | tf_op jit(solution)/shard_map/cond/branch_1_fun/ppermute | solution.py:68
  72.1 2.9 %collective-permute-done.14.refs_10_ = f32[12,2,8,128]{3,2,1,0:T(8,128)S(1)} collective-permute-done((f32[12,2,8,128]{3,2,1,0:T(8,128)S(1)}, f32[12,2,8,128]{3,2,1,0:T(8,128)S(1)}, u32[]{:S(2)}, u32[]{:S(2)}) %collective-permute-start.14) | collective-permute-done | bytes 98336 | tf_op jit(solution)/shard_map/cond/branch_1_fun/ppermute | solution.py:68
  75.0 1.5 %tick_middle.10 = (f32[12,2,8,128]{3,2,1,0:T(8,128)S(1)}, f32[12,2,8,128]{3,2,1,0:T(8,128)S(1)}) custom-call(s32[8,128]{1,0:T(8,128)S(1)} %get-tuple-element.83.lists_ref, bf16[10,128,256]{2,1,0:T(8,128)(2,1)S(1)} %get-tuple-element.84.refs_0_, bf16[10,128,256]{2,1,0:T(8,128)(2,1)S(1)} %get-tuple-element.85.refs_1_, ...), custom_call_target="tpu_custom_call" | custom-call | tf_op jit(solution)/shard_map/cond/branch_1_fun/tick_middle/pallas_call | solution.py:357
  76.5 3.0 %collective-permute-start.15 = (f32[12,2,8,128]{3,2,1,0:T(8,128)S(1)}, f32[12,2,8,128]{3,2,1,0:T(8,128)S(1)}, u32[]{:S(2)}, u32[]{:S(2)}) collective-permute-start(f32[12,2,8,128]{3,2,1,0:T(8,128)S(1)} %get-tuple-element.101), channel_id=1, source_target_pairs={{4,8},{12,16},{20,24},{8,4},{16,12},{24,20},{5,9},{13,17},{21,25},... | collective-permute-start | bytes 294920 | tf_op jit(solution)/shard_map/cond/branch_1_fun/ppermute | solution.py:68
  79.5 1.4 %collective-permute-start.16 = (f32[12,2,8,128]{3,2,1,0:T(8,128)S(1)}, f32[12,2,8,128]{3,2,1,0:T(8,128)S(1)}, u32[]{:S(2)}, u32[]{:S(2)}) collective-permute-start(f32[12,2,8,128]{3,2,1,0:T(8,128)S(1)} %get-tuple-element.102), channel_id=1, source_target_pairs={{0,4},{8,12},{16,20},{24,28},{4,0},{12,8},{20,16},{28,24},{1,5},{9... | collective-permute-start | bytes 294920 | tf_op jit(solution)/shard_map/cond/branch_1_fun/ppermute | solution.py:68
  81.0 2.2 %collective-permute-done.15.refs_9_ = f32[12,2,8,128]{3,2,1,0:T(8,128)S(1)} collective-permute-done((f32[12,2,8,128]{3,2,1,0:T(8,128)S(1)}, f32[12,2,8,128]{3,2,1,0:T(8,128)S(1)}, u32[]{:S(2)}, u32[]{:S(2)}) %collective-permute-start.15) | collective-permute-done | bytes 98336 | tf_op jit(solution)/shard_map/cond/branch_1_fun/ppermute | solution.py:68
  83.2 3.0 %collective-permute-done.16.refs_10_ = f32[12,2,8,128]{3,2,1,0:T(8,128)S(1)} collective-permute-done((f32[12,2,8,128]{3,2,1,0:T(8,128)S(1)}, f32[12,2,8,128]{3,2,1,0:T(8,128)S(1)}, u32[]{:S(2)}, u32[]{:S(2)}) %collective-permute-start.16) | collective-permute-done | bytes 98336 | tf_op jit(solution)/shard_map/cond/branch_1_fun/ppermute | solution.py:68
  86.1 1.5 %tick_middle.11 = (f32[12,2,8,128]{3,2,1,0:T(8,128)S(1)}, f32[12,2,8,128]{3,2,1,0:T(8,128)S(1)}) custom-call(s32[8,128]{1,0:T(8,128)S(1)} %get-tuple-element.83.lists_ref, bf16[10,128,256]{2,1,0:T(8,128)(2,1)S(1)} %get-tuple-element.84.refs_0_, bf16[10,128,256]{2,1,0:T(8,128)(2,1)S(1)} %get-tuple-element.85.refs_1_, ...), custom_call_target="tpu_custom_call" | custom-call | tf_op jit(solution)/shard_map/cond/branch_1_fun/tick_middle/pallas_call | solution.py:357
  87.6 3.0 %collective-permute-start.17 = (f32[12,2,8,128]{3,2,1,0:T(8,128)S(1)}, f32[12,2,8,128]{3,2,1,0:T(8,128)S(1)}, u32[]{:S(2)}, u32[]{:S(2)}) collective-permute-start(f32[12,2,8,128]{3,2,1,0:T(8,128)S(1)} %get-tuple-element.103), channel_id=1, source_target_pairs={{4,8},{12,16},{20,24},{8,4},{16,12},{24,20},{5,9},{13,17},{21,25},... | collective-permute-start | bytes 294920 | tf_op jit(solution)/shard_map/cond/branch_1_fun/ppermute | solution.py:68
  90.6 1.4 %collective-permute-start.18 = (f32[12,2,8,128]{3,2,1,0:T(8,128)S(1)}, f32[12,2,8,128]{3,2,1,0:T(8,128)S(1)}, u32[]{:S(2)}, u32[]{:S(2)}) collective-permute-start(f32[12,2,8,128]{3,2,1,0:T(8,128)S(1)} %get-tuple-element.104), channel_id=1, source_target_pairs={{0,4},{8,12},{16,20},{24,28},{4,0},{12,8},{20,16},{28,24},{1,5},{9... | collective-permute-start | bytes 294920 | tf_op jit(solution)/shard_map/cond/branch_1_fun/ppermute | solution.py:68
  92.1 2.2 %collective-permute-done.17.refs_9_ = f32[12,2,8,128]{3,2,1,0:T(8,128)S(1)} collective-permute-done((f32[12,2,8,128]{3,2,1,0:T(8,128)S(1)}, f32[12,2,8,128]{3,2,1,0:T(8,128)S(1)}, u32[]{:S(2)}, u32[]{:S(2)}) %collective-permute-start.17) | collective-permute-done | bytes 98336 | tf_op jit(solution)/shard_map/cond/branch_1_fun/ppermute | solution.py:68
  94.3 3.0 %collective-permute-done.18.refs_10_ = f32[12,2,8,128]{3,2,1,0:T(8,128)S(1)} collective-permute-done((f32[12,2,8,128]{3,2,1,0:T(8,128)S(1)}, f32[12,2,8,128]{3,2,1,0:T(8,128)S(1)}, u32[]{:S(2)}, u32[]{:S(2)}) %collective-permute-start.18) | collective-permute-done | bytes 98336 | tf_op jit(solution)/shard_map/cond/branch_1_fun/ppermute | solution.py:68
  97.2 1.4 %tick_last.3 = (f32[10,2,8,128]{3,2,1,0:T(8,128)S(1)}, f32[10,2,8,128]{3,2,1,0:T(8,128)S(1)}, f32[10,2,8,128]{3,2,1,0:T(8,128)S(1)}, f32[10,2,8,128]{3,2,1,0:T(8,128)S(1)}) custom-call(s32[8,128]{1,0:T(8,128)S(1)} %get-tuple-element.83.lists_ref, bf16[10,128,256]{2,1,0:T(8,128)(2,1)S(1)} %get-tuple-element.84.refs_0_, ...), custom_call_target="tpu_custom_call" | custom-call | tf_op jit(solution)/shard_map/cond/branch_1_fun/tick_last/pallas_call | solution.py:357
  98.6 0.5 collective-permute-start.19
  99.2 1.3 %collective-permute-start.20 = (f32[10,2,8,128]{3,2,1,0:T(8,128)S(1)}, f32[10,2,8,128]{3,2,1,0:T(8,128)}, u32[]{:S(2)}, u32[]{:S(2)}) collective-permute-start(f32[10,2,8,128]{3,2,1,0:T(8,128)S(1)} %get-tuple-element.107), channel_id=1, source_target_pairs={{0,2},{1,3},{2,0},{3,1},{4,6},{5,7},{6,4},{7,5},{8,10},{9,11},{10,... | collective-permute-start | bytes 245768 | tf_op jit(solution)/shard_map/cond/branch_1_fun/ppermute | solution.py:34
  100.4 0.5 collective-permute-start.21
  100.9 0.0 collective-permute-done.19
  100.9 2.4 %collective-permute-done.20 = f32[10,2,8,128]{3,2,1,0:T(8,128)} collective-permute-done((f32[10,2,8,128]{3,2,1,0:T(8,128)S(1)}, f32[10,2,8,128]{3,2,1,0:T(8,128)}, u32[]{:S(2)}, u32[]{:S(2)}) %collective-permute-start.20) | collective-permute-done | bytes 81952 | tf_op jit(solution)/shard_map/cond/branch_1_fun/ppermute | solution.py:34
  103.3 1.9 %collective-permute-done.21 = f32[10,2,8,128]{3,2,1,0:T(8,128)} collective-permute-done((f32[10,2,8,128]{3,2,1,0:T(8,128)S(1)}, f32[10,2,8,128]{3,2,1,0:T(8,128)}, u32[]{:S(2)}, u32[]{:S(2)}) %collective-permute-start.21) | collective-permute-done | bytes 81952 | tf_op jit(solution)/shard_map/cond/branch_1_fun/ppermute | solution.py:34
  105.2 2.2 %finish.1 = f32[2,2,32,2048]{3,2,1,0:T(8,128)} custom-call(s32[2]{0:T(128)S(1)} %pad_add_fusion.where_ref, s32[2,16]{1,0:T(2,128)S(1)} %get-tuple-element.130.rows_ref, f32[2,2,32,2048]{3,2,1,0:T(8,128)S(1)} %bitcast.28, f32[10,2,8,128]{3,2,1,0:T(8,128)S(1)} %get-tuple-element.147.refs_0_, f32[10,2,8,128]{3,2,1,0:T(8,128)} %get-tuple-element.148.refs_1_, ...), custom_call_target="tpu_custom_call" | custom-call | tf_op jit(solution)/shard_map/finish/pallas_call | solution.py:386
  (4 shorter events, 0.1 us)
Async XLA Ops:
  0.8 0.7 copy-start.2
  3.0 1.7 %copy-start.1 = (f32[1,20,2,128,128]{4,3,2,1,0:T(8,128)S(1)}, f32[1,20,2,128,128]{4,3,2,1,0:T(8,128)}, u32[]{:S(2)}) copy-start(f32[1,20,2,128,128]{4,3,2,1,0:T(8,128)} %param.7) | copy-start | bytes 7864324
  4.8 4.6 %copy-start = (f32[1,2,2,32,2048]{4,3,2,1,0:T(8,128)S(1)}, f32[1,2,2,32,2048]{4,3,2,1,0:T(8,128)}, u32[]{:S(2)}) copy-start(f32[1,2,2,32,2048]{4,3,2,1,0:T(8,128)} %param.6) | copy-start | bytes 3145732
  7.2 31.1 %collective-permute-start.25 = (f32[10,2,128,128]{3,2,1,0:T(8,128)S(1)}, f32[10,2,128,128]{3,2,1,0:T(8,128)}, u32[]{:S(2)}, u32[]{:S(2)}) collective-permute-start(f32[10,2,128,128]{3,2,1,0:T(8,128)S(1)} %pack_green.1.green_ref), channel_id=1, source_target_pairs={{0,2},{1,3},{2,0},{3,1},{4,6},{5,7},{6,4},{7,5},{8,10},{9,11},{10,... | collective-permute-start | bytes 3932168 | tf_op jit(solution)/shard_map/ppermute | solution.py:34
  8.5 29.8 %collective-permute-start.24 = (f32[10,2,128,128]{3,2,1,0:T(8,128)S(1)}, f32[10,2,128,128]{3,2,1,0:T(8,128)}, u32[]{:S(2)}, u32[]{:S(2)}) collective-permute-start(f32[10,2,128,128]{3,2,1,0:T(8,128)S(1)} %pack_green.1.green_ref), channel_id=1, source_target_pairs={{0,1},{1,0},{2,3},{3,2},{4,5},{5,4},{6,7},{7,6},{8,9},{9,8},{10,11... | collective-permute-start | bytes 3932168 | tf_op jit(solution)/shard_map/ppermute | solution.py:34
  9.5 28.8 %collective-permute-start.23 = (f32[2,32,2048]{2,1,0:T(8,128)S(1)}, f32[2,32,2048]{2,1,0:T(8,128)S(1)}, u32[]{:S(2)}, u32[]{:S(2)}) collective-permute-start(f32[2,32,2048]{2,1,0:T(8,128)S(1)} %get-tuple-element.151), channel_id=1, source_target_pairs={{0,4},{8,12},{16,20},{24,28},{4,0},{12,8},{20,16},{28,24},{1,5},{9... | collective-permute-start | bytes 1572872 | tf_op jit(solution)/shard_map/ppermute | solution.py:68
  10.8 27.5 %collective-permute-start.22 = (f32[2,32,2048]{2,1,0:T(8,128)S(1)}, f32[2,32,2048]{2,1,0:T(8,128)S(1)}, u32[]{:S(2)}, u32[]{:S(2)}) collective-permute-start(f32[2,32,2048]{2,1,0:T(8,128)S(1)} %get-tuple-element.152), channel_id=1, source_target_pairs={{4,8},{12,16},{20,24},{8,4},{16,12},{24,20},{5,9},{13,17},{21,25},... | collective-permute-start | bytes 1572872 | tf_op jit(solution)/shard_map/ppermute | solution.py:68
  38.3 9.9 %collective-permute-start.26 = (f32[10,2,128,128]{3,2,1,0:T(8,128)}, f32[10,2,128,128]{3,2,1,0:T(8,128)}, u32[]{:S(2)}, u32[]{:S(2)}) collective-permute-start(f32[10,2,128,128]{3,2,1,0:T(8,128)} %collective-permute-done.25.green_ref), channel_id=1, source_target_pairs={{0,1},{1,0},{2,3},{3,2},{4,5},{5,4},{6,7},{7,6},{8,9},{9,8},{10,11... | collective-permute-start | bytes 3932168 | tf_op jit(solution)/shard_map/ppermute | solution.py:34
  38.9 11.1 %collective-permute-start.27 = (f32[2,2,8,2048]{3,2,1,0:T(8,128)S(1)}, f32[2,2,8,2048]{3,2,1,0:T(8,128)S(1)}, u32[]{:S(2)}, u32[]{:S(2)}) collective-permute-start(f32[2,2,8,2048]{3,2,1,0:T(8,128)S(1)} %pad_maximum_fusion.1), channel_id=1, source_target_pairs={{0,1},{1,0},{2,3},{3,2},{4,5},{5,4},{6,7},{7,6},{8,9},{9,8},{10,11... | collective-permute-start | bytes 786440 | tf_op jit(solution)/shard_map/ppermute | solution.py:34
  39.1 10.9 %collective-permute-start.28 = (f32[2,2,8,2048]{3,2,1,0:T(8,128)S(1)}, f32[2,2,8,2048]{3,2,1,0:T(8,128)S(1)}, u32[]{:S(2)}, u32[]{:S(2)}) collective-permute-start(f32[2,2,8,2048]{3,2,1,0:T(8,128)S(1)} %pad_maximum_fusion.2), channel_id=1, source_target_pairs={{0,2},{1,3},{2,0},{3,1},{4,6},{5,7},{6,4},{7,5},{8,10},{9,11},{10,... | collective-permute-start | bytes 786440 | tf_op jit(solution)/shard_map/ppermute | solution.py:34
  40.4 12.4 %collective-permute-start.29 = (f32[2,2,8,2048]{3,2,1,0:T(8,128)S(1)}, f32[2,2,8,2048]{3,2,1,0:T(8,128)S(1)}, u32[]{:S(2)}, u32[]{:S(2)}) collective-permute-start(f32[2,2,8,2048]{3,2,1,0:T(8,128)S(1)} %pad_maximum_fusion.3), channel_id=1, source_target_pairs={{0,3},{1,2},{2,1},{3,0},{4,7},{5,6},{6,5},{7,4},{8,11},{9,10},{10,... | collective-permute-start | bytes 786440 | tf_op jit(solution)/shard_map/ppermute | solution.py:34
  54.3 7.3 %collective-permute-start.11 = (f32[12,2,8,128]{3,2,1,0:T(8,128)S(1)}, f32[12,2,8,128]{3,2,1,0:T(8,128)S(1)}, u32[]{:S(2)}, u32[]{:S(2)}) collective-permute-start(f32[12,2,8,128]{3,2,1,0:T(8,128)S(1)} %get-tuple-element.97), channel_id=1, source_target_pairs={{4,8},{12,16},{20,24},{8,4},{16,12},{24,20},{5,9},{13,17},{21,25},... | collective-permute-start | bytes 294920 | tf_op jit(solution)/shard_map/cond/branch_1_fun/ppermute | solution.py:68
  57.3 6.6 %collective-permute-start.12 = (f32[12,2,8,128]{3,2,1,0:T(8,128)S(1)}, f32[12,2,8,128]{3,2,1,0:T(8,128)S(1)}, u32[]{:S(2)}, u32[]{:S(2)}) collective-permute-start(f32[12,2,8,128]{3,2,1,0:T(8,128)S(1)} %get-tuple-element.98), channel_id=1, source_target_pairs={{0,4},{8,12},{16,20},{24,28},{4,0},{12,8},{20,16},{28,24},{1,5},{9... | collective-permute-start | bytes 294920 | tf_op jit(solution)/shard_map/cond/branch_1_fun/ppermute | solution.py:68
  65.4 6.7 %collective-permute-start.13 = (f32[12,2,8,128]{3,2,1,0:T(8,128)S(1)}, f32[12,2,8,128]{3,2,1,0:T(8,128)S(1)}, u32[]{:S(2)}, u32[]{:S(2)}) collective-permute-start(f32[12,2,8,128]{3,2,1,0:T(8,128)S(1)} %get-tuple-element.99), channel_id=1, source_target_pairs={{4,8},{12,16},{20,24},{8,4},{16,12},{24,20},{5,9},{13,17},{21,25},... | collective-permute-start | bytes 294920 | tf_op jit(solution)/shard_map/cond/branch_1_fun/ppermute | solution.py:68
  68.4 6.6 %collective-permute-start.14 = (f32[12,2,8,128]{3,2,1,0:T(8,128)S(1)}, f32[12,2,8,128]{3,2,1,0:T(8,128)S(1)}, u32[]{:S(2)}, u32[]{:S(2)}) collective-permute-start(f32[12,2,8,128]{3,2,1,0:T(8,128)S(1)} %get-tuple-element.100), channel_id=1, source_target_pairs={{0,4},{8,12},{16,20},{24,28},{4,0},{12,8},{20,16},{28,24},{1,5},{9... | collective-permute-start | bytes 294920 | tf_op jit(solution)/shard_map/cond/branch_1_fun/ppermute | solution.py:68
  76.5 6.7 %collective-permute-start.15 = (f32[12,2,8,128]{3,2,1,0:T(8,128)S(1)}, f32[12,2,8,128]{3,2,1,0:T(8,128)S(1)}, u32[]{:S(2)}, u32[]{:S(2)}) collective-permute-start(f32[12,2,8,128]{3,2,1,0:T(8,128)S(1)} %get-tuple-element.101), channel_id=1, source_target_pairs={{4,8},{12,16},{20,24},{8,4},{16,12},{24,20},{5,9},{13,17},{21,25},... | collective-permute-start | bytes 294920 | tf_op jit(solution)/shard_map/cond/branch_1_fun/ppermute | solution.py:68
  79.5 6.6 %collective-permute-start.16 = (f32[12,2,8,128]{3,2,1,0:T(8,128)S(1)}, f32[12,2,8,128]{3,2,1,0:T(8,128)S(1)}, u32[]{:S(2)}, u32[]{:S(2)}) collective-permute-start(f32[12,2,8,128]{3,2,1,0:T(8,128)S(1)} %get-tuple-element.102), channel_id=1, source_target_pairs={{0,4},{8,12},{16,20},{24,28},{4,0},{12,8},{20,16},{28,24},{1,5},{9... | collective-permute-start | bytes 294920 | tf_op jit(solution)/shard_map/cond/branch_1_fun/ppermute | solution.py:68
  87.6 6.7 %collective-permute-start.17 = (f32[12,2,8,128]{3,2,1,0:T(8,128)S(1)}, f32[12,2,8,128]{3,2,1,0:T(8,128)S(1)}, u32[]{:S(2)}, u32[]{:S(2)}) collective-permute-start(f32[12,2,8,128]{3,2,1,0:T(8,128)S(1)} %get-tuple-element.103), channel_id=1, source_target_pairs={{4,8},{12,16},{20,24},{8,4},{16,12},{24,20},{5,9},{13,17},{21,25},... | collective-permute-start | bytes 294920 | tf_op jit(solution)/shard_map/cond/branch_1_fun/ppermute | solution.py:68
  90.6 6.6 %collective-permute-start.18 = (f32[12,2,8,128]{3,2,1,0:T(8,128)S(1)}, f32[12,2,8,128]{3,2,1,0:T(8,128)S(1)}, u32[]{:S(2)}, u32[]{:S(2)}) collective-permute-start(f32[12,2,8,128]{3,2,1,0:T(8,128)S(1)} %get-tuple-element.104), channel_id=1, source_target_pairs={{0,4},{8,12},{16,20},{24,28},{4,0},{12,8},{20,16},{28,24},{1,5},{9... | collective-permute-start | bytes 294920 | tf_op jit(solution)/shard_map/cond/branch_1_fun/ppermute | solution.py:68
  98.6 2.2 %collective-permute-start.19 = (f32[10,2,8,128]{3,2,1,0:T(8,128)S(1)}, f32[10,2,8,128]{3,2,1,0:T(8,128)}, u32[]{:S(2)}, u32[]{:S(2)}) collective-permute-start(f32[10,2,8,128]{3,2,1,0:T(8,128)S(1)} %get-tuple-element.106), channel_id=1, source_target_pairs={{0,1},{1,0},{2,3},{3,2},{4,5},{5,4},{6,7},{7,6},{8,9},{9,8},{10,11... | collective-permute-start | bytes 245768 | tf_op jit(solution)/shard_map/cond/branch_1_fun/ppermute | solution.py:34
  99.2 4.1 %collective-permute-start.20 = (f32[10,2,8,128]{3,2,1,0:T(8,128)S(1)}, f32[10,2,8,128]{3,2,1,0:T(8,128)}, u32[]{:S(2)}, u32[]{:S(2)}) collective-permute-start(f32[10,2,8,128]{3,2,1,0:T(8,128)S(1)} %get-tuple-element.107), channel_id=1, source_target_pairs={{0,2},{1,3},{2,0},{3,1},{4,6},{5,7},{6,4},{7,5},{8,10},{9,11},{10,... | collective-permute-start | bytes 245768 | tf_op jit(solution)/shard_map/cond/branch_1_fun/ppermute | solution.py:34
  100.4 4.8 %collective-permute-start.21 = (f32[10,2,8,128]{3,2,1,0:T(8,128)S(1)}, f32[10,2,8,128]{3,2,1,0:T(8,128)}, u32[]{:S(2)}, u32[]{:S(2)}) collective-permute-start(f32[10,2,8,128]{3,2,1,0:T(8,128)S(1)} %get-tuple-element.108), channel_id=1, source_target_pairs={{0,3},{1,2},{2,1},{3,0},{4,7},{5,6},{6,5},{7,4},{8,11},{9,10},{10,... | collective-permute-start | bytes 245768 | tf_op jit(solution)/shard_map/cond/branch_1_fun/ppermute | solution.py:34

commit v4 on v0

--- a/solution.py
+++ b/solution.py
@@ -1,12 +1,33 @@
+import functools
+
 import jax
 import jax.numpy as jnp
 from jax import lax
+from jax.experimental import pallas as pl
+from jax.experimental.pallas import tpu as pltpu
 from jax.sharding import PartitionSpec as P
 
 TILE = 128
 CAP = 5
 BAND = 4
 TICKS = 6
+KINDS = 4
+SLOTS = KINDS * CAP
+LIVE = 2 * CAP
+STRIDE = 16
+READ = 9
+CROSS = 4
+EXTRA = 4
+ROUNDS = (8, 5, 4, 3)
+SHIFT = 1024
+
+VMEM = pl.BlockSpec(memory_space=pltpu.VMEM)
+SMEM = pl.BlockSpec(memory_space=pltpu.SMEM)
+ANY = pl.BlockSpec(memory_space=pl.ANY)
+PARAMS = pltpu.CompilerParams(vmem_limit_bytes=32 * 1024 * 1024)
+
+SEND, RECV, SOURCE, FOREIGN, OFFER, READS, LEND, COPY_OUT, COPY_IN, CODE, FACTS = 0, 4, 8, 9, 10, 11, 12, 13, 14, 15, 16
+TABLE_ROWS = 24
 
 
 def from_behind(block, axis, distance):
@@ -60,7 +81,7 @@
     return place_terms(terms, target, live[order], tiles_dev)
 
 
-def body(sources, green, rowcol, counts):
+def full_sweeps(sources, green, rowcol, counts):
     width = sources.shape[-1]
     shots = sources.shape[3]
     tiles_dev = width // TILE
@@ -80,7 +101,575 @@
         tiled = widened.reshape(2, 2, shots, tiles_dev + 2 * BAND, TILE)
         update = live_update(tiled, blocks, row_local, col_local, live_counts, tiles_dev)
         waves = local_sources + update.reshape(2, 2, shots, width)
-    return waves[None]
+    return waves
+
+
+def swap_tile(block, offset):
+    return lax.ppermute(block, "tile", [(i, i ^ offset) for i in range(lax.axis_size("tile"))])
+
+
+def swap_layers(first, second):
+    layers = lax.axis_size("layer")
+
+    def swap(block, start):
+        pairs = [(i, i + 1) for i in range(start, layers - 1, 2)]
+        return lax.ppermute(block, "layer", pairs + [(b, a) for a, b in pairs])
+
+    return swap(first, 1), swap(second, 0)
+
+
+def codes_kernel(tiles_dev, where_ref, rowcol_ref, counts_ref, codes_ref, rows_ref, order_ref):
+    place = where_ref[1]
+
+    def scan(want_live, rank):
+        for slot in range(SLOTS):
+            live = counts_ref[slot // CAP] > slot % CAP
+
+            @pl.when((live == want_live) & (rank < LIVE))
+            def _():
+                order_ref[rank] = slot
+
+            rank = rank + (live == want_live).astype(jnp.int32)
+        return rank
+
+    live_slots = scan(True, jnp.int32(0))
+    scan(False, live_slots)
+    lanes = codes_ref.shape[-1]
+    lane = lax.broadcasted_iota(jnp.int32, (1, lanes), 1)
+    codes = jnp.zeros((1, lanes), jnp.int32)
+    for j in range(LIVE):
+        slot = order_ref[j]
+        kind = lax.div(slot, CAP)
+        alive = j < live_slots
+        code = rowcol_ref[slot, 0] * 65536 + rowcol_ref[slot, 1] * 8 + kind * 2 + 1
+        code = jnp.where(alive, code, 0)
+        codes = jnp.where(lane == place * STRIDE + j, code, codes)
+        rows_ref[0, j] = lax.shift_right_logical(kind, 1)
+        rows_ref[1, j] = jnp.where(alive, rowcol_ref[slot, 0] - place * tiles_dev, 0)
+    codes_ref[...] = jnp.broadcast_to(codes[None], codes_ref.shape)
+
+
+def slot_codes(where, pairs, live_counts, receivers, lanes, tiles_dev):
+    return pl.pallas_call(
+        functools.partial(codes_kernel, tiles_dev),
+        out_shape=(
+            jax.ShapeDtypeStruct((receivers, 1, lanes), jnp.int32),
+            jax.ShapeDtypeStruct((2, STRIDE), jnp.int32),
+            jax.ShapeDtypeStruct((STRIDE,), jnp.int32),
+        ),
+        in_specs=[SMEM, SMEM, SMEM],
+        out_specs=(VMEM, SMEM, SMEM),
+        compiler_params=PARAMS,
+        name="slot_codes",
+    )(where, pairs, live_counts)
+
+
+def pack_kernel(order_ref, green_ref, packed_ref, sems):
+    copies = []
+    for j in range(LIVE):
+        copy = pltpu.make_async_copy(green_ref.at[order_ref[j]], packed_ref.at[j], sems.at[j])
+        copy.start()
+        copies.append(copy)
+    for copy in copies:
+        copy.wait()
+
+
+def pack_green(order, green):
+    return pl.pallas_call(
+        pack_kernel,
+        out_shape=jax.ShapeDtypeStruct((LIVE,) + green.shape[1:], green.dtype),
+        in_specs=[SMEM, ANY],
+        out_specs=VMEM,
+        scratch_shapes=[pltpu.SemaphoreType.DMA((LIVE,))],
+        compiler_params=PARAMS,
+        name="pack_green",
+    )(order, green)
+
+
+def lists_kernel(layers, devices, tiles_dev, where_ref, table_ref, out_ref, writes, reads, active, changed, now, sets, seen):
+    lanes = 128
+    tiles = tiles_dev * devices
+    pad = 2
+    layer, place = where_ref[0], where_ref[1]
+    pair = place >> 1
+    down = lax.broadcasted_iota(jnp.int32, (lanes, lanes), 0)
+    across = lax.broadcasted_iota(jnp.int32, (lanes, lanes), 1)
+    row8 = lax.broadcasted_iota(jnp.int32, (8, lanes), 0)
+    lane8 = lax.broadcasted_iota(jnp.int32, (8, lanes), 1)
+    lane = lane8[:1]
+    low = lane8 < tiles
+    as_mask = lambda mask: jnp.where(mask, 1.0, 0.0).astype(jnp.bfloat16)
+    narrow = lambda values: values.astype(jnp.bfloat16)
+
+    def by_rows(values, matrix):
+        return lax.dot_general(narrow(values), matrix, (((1,), (1,)), ((), ())), preferred_element_type=jnp.float32)
+
+    def by_columns(values, matrix):
+        return jnp.dot(narrow(values), matrix, preferred_element_type=jnp.float32)
+
+    def each(step):
+        if layers <= 8:
+            for index in range(layers):
+                step(index)
+        else:
+            lax.fori_loop(0, layers, lambda index, carry: (step(index), carry)[1], 0)
+
+    def code_of(index):
+        total = table_ref[index * devices]
+        for device in range(1, devices):
+            total = total + table_ref[index * devices + device]
+        return total
+
+    for ref in (changed, now, seen):
+        ref[...] = jnp.zeros_like(ref)
+
+    def unpack(index):
+        code = code_of(index)
+        kind = (code >> 1) & 3
+        alive = (code & 1) == 1
+        wdir, rdir = kind >> 1, (kind ^ (kind >> 1)) & 1
+        target = jnp.where(alive, wdir * tiles + (code >> 16), -1)
+        origin = rdir * tiles + ((code >> 3) & 8191)
+        from_edge = ((rdir == 0) & (index == 0)) | ((rdir == 1) & (index == layers - 1))
+        origin = jnp.where(alive & jnp.logical_not(from_edge), origin, -1)
+        writes[index] = as_mask(down == target)
+        reads[index] = as_mask(down == origin)
+        live = jnp.where(alive, 1.0, 0.0)
+        active[index] = jnp.where(row8 == 0, live, 0.0)
+        device = lane >> 4
+        first = jnp.where((device >> 1) == 0, live, 0.0)
+        second = jnp.where((device >> 1) == 1, live, 0.0)
+        sets[index] = jnp.where(row8 == 0, first, jnp.where(row8 == 1, second, jnp.where(row8 == 2, live, 0.0)))
+
+    each(unpack)
+
+    for step in range(len(ROUNDS) + 1):
+        last = step == len(ROUNDS)
+
+        def spread(index):
+            if not last:
+                hit = jnp.minimum(by_rows(active[index], writes[index]), 1.0)
+                now[index + pad] = hit
+                changed[index + pad] = jnp.where(row8 == step, hit[:1], changed[index + pad])
+            seen[index + pad] = jnp.minimum(by_rows(sets[index], reads[index]), 1.0)
+
+        each(spread)
+        if last:
+            break
+
+        def collect(index):
+            coming = jnp.where(low, now[index + pad - 1], now[index + pad + 1])
+            active[index] = jnp.minimum(by_columns(coming, reads[index]), 1.0)
+            wanted = jnp.where(low, seen[index + pad + 1], seen[index + pad - 1])
+            added = jnp.minimum(by_columns(wanted, writes[index]), 1.0)
+            sets[index] = jnp.maximum(sets[index], added)
+
+        each(collect)
+
+    same_half = (down >= tiles) == (across >= tiles)
+    same_group = (down >> 4) == (across >> 4)
+    half_total, group_total = as_mask(same_half), as_mask(same_group)
+    half_before = as_mask(same_half & (down < across))
+    group_before = as_mask(same_group & (down < across))
+    room = jnp.zeros((8, lanes), jnp.float32)
+    for j, most in enumerate(ROUNDS):
+        room = jnp.where(row8 == j, float(most), room)
+
+    tile_pair = ((lane8 & (tiles - 1)) >> 4) >> 1
+    slot_pair = (lane8 >> 4) >> 1
+
+    def pick(rows, which):
+        return jnp.where(which == 0, rows[0:1], rows[1:2])
+
+    def wanted_by(which, index):
+        ahead, behind = seen[index + pad + 1], seen[index + pad - 1]
+        return jnp.where(low[:1], pick(ahead, which), pick(behind, which))
+
+    now[0] = jnp.full((8, lanes), -1.0, jnp.float32)
+
+    def measure(index):
+        over = now[0]
+        for which in range(2):
+            counts = by_columns(changed[index + pad] * wanted_by(which, index), half_total)
+            over = jnp.maximum(over, jnp.where(row8 < len(ROUNDS), counts - room, -1.0))
+        counts = by_columns(seen[index + pad], group_total)
+        over = jnp.maximum(over, jnp.where(row8 == 2, counts - READ, -1.0))
+        over = jnp.maximum(over, jnp.where((row8 < 2) & (tile_pair != row8), counts - CROSS, -1.0))
+        counts = by_columns(sets[index], group_total)
+        over = jnp.maximum(over, jnp.where((row8 < 2) & (slot_pair != row8) & (slot_pair < 2), counts - EXTRA, -1.0))
+        now[0] = over
+
+    each(measure)
+    over = jnp.max(jnp.max(now[0], axis=1, keepdims=True), axis=0, keepdims=True)
+
+    odd = layer & 1
+    other = 1 - pair
+    code = code_of(layer)
+    kind = (code >> 1) & 3
+    wdir, rdir = kind >> 1, (kind ^ (kind >> 1)) & 1
+
+    def travelling(index):
+        sent = changed[index + pad] * wanted_by(pair, index)
+        return sent * (by_columns(sent, half_before) + 1.0)
+
+    def ranked(flags):
+        return flags * (by_columns(flags, group_before) + 1.0)
+
+    mine = travelling(layer)
+    above = travelling(jnp.maximum(layer - 1, 0))
+    below = travelling(jnp.minimum(layer + 1, layers - 1))
+    coming = jnp.where(low, jnp.where(layer > 0, above, 0.0), jnp.where(layer < layers - 1, below, 0.0))
+    send = by_columns(mine, writes[layer]).astype(jnp.int32) - 1
+    recv = by_columns(coming, reads[layer]).astype(jnp.int32) - 1
+    send = jnp.where((send >= 0) & (wdir == odd), send + SHIFT, send)
+    recv = jnp.where((recv >= 0) & (rdir != odd), recv + SHIFT, recv)
+    here = seen[layer + pad]
+    ahead, behind = seen[layer + pad + 1], seen[layer + pad - 1]
+    foreign = pick(here, pair) * jnp.where(tile_pair[:1] != pair, 1.0, 0.0)
+    lent = pick(here, other)
+    offered = jnp.where(low[:1], ahead[2:3], behind[2:3])
+    flags = jnp.where(row8 == 0, here[2:3], 0.0)
+    flags = jnp.where(row8 == 1, foreign, flags)
+    flags = jnp.where(row8 == 2, offered, flags)
+    flags = jnp.where(row8 == 3, lent, flags)
+    ranks = ranked(flags)
+    sources = by_columns(ranks, reads[layer]).astype(jnp.int32) - 1
+    chosen = sets[layer]
+    flags = jnp.where(row8 == 0, pick(chosen, other), 0.0)
+    flags = jnp.where(row8 == 1, pick(chosen, pair) * jnp.where(slot_pair[:1] != pair, 1.0, 0.0), flags)
+    copies = ranked(flags).astype(jnp.int32)
+    ranks = ranks.astype(jnp.int32)
+    out_ref[...] = jnp.zeros_like(out_ref)
+    rounds = len(ROUNDS)
+    out_ref[SEND : SEND + rounds] = send[:rounds]
+    out_ref[RECV : RECV + rounds] = recv[:rounds]
+    out_ref[SOURCE : SOURCE + 2] = sources[:2]
+    out_ref[OFFER : OFFER + 1] = ranks[2:3]
+    out_ref[READS : READS + 1] = ranks[0:1]
+    out_ref[LEND : LEND + 1] = ranks[3:4]
+    out_ref[COPY_OUT : COPY_OUT + 2] = copies[:2]
+    out_ref[CODE : CODE + 1] = code
+    facts = jnp.where(lane == 0, jnp.where(over > 0.0, 1, 0), jnp.where(lane == 1, layer, place))
+    out_ref[FACTS : FACTS + 1] = facts
+
+
+def build_lists(where, table, layers, devices, tiles_dev):
+    lanes = table.shape[-1]
+    rows = lambda count: pltpu.VMEM((count, 8, lanes), jnp.float32)
+    square = pltpu.VMEM((layers, lanes, lanes), jnp.bfloat16)
+    return pl.pallas_call(
+        functools.partial(lists_kernel, layers, devices, tiles_dev),
+        out_shape=jax.ShapeDtypeStruct((TABLE_ROWS, lanes), jnp.int32),
+        in_specs=[SMEM, VMEM],
+        out_specs=VMEM,
+        scratch_shapes=[square, square, rows(layers), rows(layers + 4), rows(layers + 4), rows(layers), rows(layers + 4)],
+        compiler_params=PARAMS,
+        name="build_lists",
+    )(where, table)
+
+
+def split_kernel(green_ref, high_ref, low_ref):
+    for slot in range(green_ref.shape[0]):
+        for part in range(2):
+            block = green_ref[slot, part].T
+            high = block.astype(jnp.bfloat16)
+            low = (block - high.astype(jnp.float32)).astype(jnp.bfloat16)
+            high_ref[slot, :, part * TILE : (part + 1) * TILE] = high
+            low_ref[slot, :, part * TILE : (part + 1) * TILE] = low
+
+
+def split_green(packed):
+    shape = jax.ShapeDtypeStruct((packed.shape[0], TILE, 2 * TILE), jnp.bfloat16)
+    return pl.pallas_call(
+        split_kernel,
+        out_shape=(shape, shape),
+        in_specs=[VMEM],
+        out_specs=(VMEM, VMEM),
+        compiler_params=PARAMS,
+        name="split_green",
+    )(packed)
+
+
+def pick_kernel(tiles, lists_ref, sources_ref, packed_ref, first_ref, second_ref, copy_ref):
+    odd, place = lists_ref[FACTS, 1] & 1, lists_ref[FACTS, 2]
+    tiles_dev = sources_ref.shape[3] // TILE
+    first_ref[...] = jnp.zeros_like(first_ref)
+    second_ref[...] = jnp.zeros_like(second_ref)
+    for direction in range(2):
+        for tile in range(tiles_dev):
+            rank = lists_ref[OFFER, direction * tiles + place * tiles_dev + tile]
+            found = (rank > 0) & (rank <= READ)
+
+            def copy_to(ref):
+                ref[jnp.clip(rank - 1, 0, READ - 1)] = sources_ref[direction, :, :, tile * TILE : (tile + 1) * TILE]
+
+            pl.when(found & (odd != direction))(functools.partial(copy_to, first_ref))
+            pl.when(found & (odd == direction))(functools.partial(copy_to, second_ref))
+    for j in range(LIVE):
+        rank = lists_ref[COPY_OUT, place * STRIDE + j]
+
+        @pl.when((rank > 0) & (rank <= EXTRA))
+        def _():
+            copy_ref[jnp.clip(rank - 1, 0, EXTRA - 1)] = packed_ref[j]
+
+
+def pick_tiles(lists, sources, packed, tiles):
+    shots = sources.shape[2]
+    shape = jax.ShapeDtypeStruct((READ, 2, shots, TILE), jnp.float32)
+    return pl.pallas_call(
+        functools.partial(pick_kernel, tiles),
+        out_shape=(shape, shape, jax.ShapeDtypeStruct((EXTRA,) + packed.shape[1:], packed.dtype)),
+        in_specs=[SMEM, VMEM, VMEM],
+        out_specs=(VMEM, VMEM, VMEM),
+        compiler_params=PARAMS,
+        name="pick_tiles",
+    )(lists, sources, packed)
+
+
+def share_kernel(tiles, tiles_dev, lists_ref, first_ref, second_ref, core_ref, *cross_refs):
+    odd, place = lists_ref[FACTS, 1] & 1, lists_ref[FACTS, 2]
+    sub = core_ref.shape[3]
+    core = place & 1
+    theirs = pl.multiple_of((1 - core) * sub, sub)
+    core_ref[0] = first_ref[:, :, pl.ds(theirs, sub), :]
+    core_ref[1] = second_ref[:, :, pl.ds(theirs, sub), :]
+    for cross_ref in cross_refs:
+        cross_ref[...] = jnp.zeros_like(cross_ref)
+    for direction in range(2):
+        for tile in range(tiles_dev):
+            lane = direction * tiles + place * tiles_dev + tile
+            rank = lists_ref[LEND, lane]
+            at = jnp.clip(lists_ref[READS, lane] - 1, 0, READ - 1)
+
+            def copy_from(ref):
+                for flip, cross_ref in enumerate(cross_refs):
+                    shot = pl.multiple_of((core ^ flip) * sub, sub)
+                    cross_ref[direction, jnp.clip(rank - 1, 0, CROSS - 1)] = ref[at, :, pl.ds(shot, sub), :]
+
+            found = (rank > 0) & (rank <= CROSS)
+            pl.when(found & (odd == direction))(functools.partial(copy_from, first_ref))
+            pl.when(found & (odd != direction))(functools.partial(copy_from, second_ref))
+
+
+def share_tiles(lists, first, second, tiles, tiles_dev):
+    sub = first.shape[2] // 2
+    piece = jax.ShapeDtypeStruct((2, READ, 2, sub, TILE), jnp.float32)
+    cross = jax.ShapeDtypeStruct((2, CROSS, 2, sub, TILE), jnp.float32)
+    return pl.pallas_call(
+        functools.partial(share_kernel, tiles, tiles_dev),
+        out_shape=(piece, cross, cross),
+        in_specs=[SMEM, VMEM, VMEM],
+        out_specs=(VMEM, VMEM, VMEM),
+        compiler_params=PARAMS,
+        name="share_tiles",
+    )(lists, first, second)
+
+
+def block_term(x, high, low):
+    parts, sub, _ = x.shape
+    rows = parts * sub
+    flat = x.reshape(rows, TILE)
+    top = flat.astype(jnp.bfloat16)
+    rest = (flat - top.astype(jnp.float32)).astype(jnp.bfloat16)
+    main = jnp.dot(jnp.concatenate([top, rest], axis=0), high, preferred_element_type=jnp.float32)
+    prod = main[:rows] + main[rows:] + jnp.dot(top, low, preferred_element_type=jnp.float32)
+    real = prod[:sub, :TILE] - prod[sub:, TILE:]
+    imag = prod[:sub, TILE:] + prod[sub:, :TILE]
+    return real, imag
+
+
+def tick_kernel(step, tiles_dev, lists_ref, *refs):
+    refs = list(refs)
+    highs = [refs.pop(0) for _ in range(4)]
+    lows = [refs.pop(0) for _ in range(4)]
+    first_ref, second_ref = refs.pop(0), refs.pop(0)
+    last = step == len(ROUNDS)
+    if step == 0:
+        core_ref, cross_refs, (total_ref, out_a, out_b, traces, acc) = refs[0], refs[1:3], refs[3:]
+    elif last:
+        _, total_ref = refs
+    else:
+        _, total_ref, out_a, out_b, acc = refs
+    odd, place = lists_ref[FACTS, 1] & 1, lists_ref[FACTS, 2]
+    core = place & 1
+    if step == 0:
+        sub = core_ref.shape[3]
+        shot = pl.multiple_of(core * sub, sub)
+        traces[:READ] = first_ref[:, :, pl.ds(shot, sub), :]
+        traces[READ : 2 * READ] = second_ref[:, :, pl.ds(shot, sub), :]
+        traces[2 * READ : 3 * READ] = core_ref[0]
+        traces[3 * READ : 4 * READ] = core_ref[1]
+        for j, ref in enumerate(cross_refs):
+            for direction in range(2):
+                at = 4 * READ + (2 * j + direction) * CROSS
+                traces[at : at + CROSS] = ref[direction]
+        empty = 4 * READ + 4 * CROSS
+        traces[empty] = jnp.zeros(traces.shape[1:], jnp.float32)
+    if not last:
+        cap = out_a.shape[0]
+        acc[...] = jnp.zeros_like(acc)
+
+    def entering(lane):
+        if step:
+            value = lists_ref[RECV + step - 1, lane]
+            at = value & (SHIFT - 1)
+            return jnp.where(value < SHIFT, first_ref[at], second_ref[at])
+        code = lists_ref[CODE, lane]
+        kind = lax.shift_right_logical(code, 1) & 3
+        rdir = (kind ^ lax.shift_right_logical(kind, 1)) & 1
+        group = lax.div(lax.shift_right_logical(code, 3) & 8191, tiles_dev)
+        relative = group ^ place
+        near = lists_ref[SOURCE, lane]
+        far = lists_ref[FOREIGN, lane]
+        near_at = relative * 2 * READ + jnp.where(rdir == odd, 0, READ) + near
+        far_at = 4 * READ + (2 * (relative - 2) + rdir) * CROSS + far
+        at = jnp.where(relative < 2, jnp.where(near < 0, empty, near_at), jnp.where(far < 0, empty, far_at))
+        return traces[jnp.clip(at, 0, empty)]
+
+    def apply(lane, group, row, slot):
+        real, imag = block_term(entering(lane), highs[group][row], lows[group][row])
+        if slot is not None:
+            if step == 0:
+                total_ref[slot, 0] = real
+                total_ref[slot, 1] = imag
+            else:
+                total_ref[slot, 0] += real
+                total_ref[slot, 1] += imag
+        if not last:
+            value = lists_ref[SEND + step, lane]
+            at = jnp.where(value < SHIFT, value, value - SHIFT + cap)
+            at = jnp.where(value < 0, 2 * cap, at)
+            acc[at, 0] += real
+            acc[at, 1] += imag
+
+    for group in range(2):
+        base = (place ^ group) * STRIDE
+        for j in range(LIVE):
+            step_in = functools.partial(apply, base + j, group, j, group * LIVE + j)
+            if step == 0:
+                step_in()
+            else:
+                pl.when(lists_ref[RECV + step - 1, base + j] >= 0)(step_in)
+    if not last:
+        for group in range(2, 4):
+            base = (place ^ group) * STRIDE
+            for j in range(LIVE):
+                rank = lists_ref[COPY_IN, base + j]
+                wanted = rank > 0
+                if step:
+                    wanted = wanted & (lists_ref[RECV + step - 1, base + j] >= 0)
+                row = jnp.clip(rank - 1, 0, EXTRA - 1)
+                pl.when(wanted)(functools.partial(apply, base + j, group, row, None))
+        out_a[...] = acc[:cap]
+        out_b[...] = acc[cap : 2 * cap]
+
+
+def tick(step, tiles_dev, lists, blocks, first, second, *data):
+    sub = data[0].shape[-2]
+    tile_shape = lambda count: jax.ShapeDtypeStruct((count, 2, sub, TILE), jnp.float32)
+    room = lambda count: pltpu.VMEM((count, 2, sub, TILE), jnp.float32)
+    out_shape = (tile_shape(2 * LIVE),)
+    scratch = []
+    aliases = {}
+    if step == 0:
+        scratch.append(room(4 * READ + 4 * CROSS + 1))
+    else:
+        aliases = {1 + len(blocks) + 2: 0}
+    if step < len(ROUNDS):
+        cap = ROUNDS[step]
+        out_shape += (tile_shape(cap), tile_shape(cap))
+        scratch.append(room(2 * cap + 1))
+    operands = (*blocks, first, second, *data)
+    return pl.pallas_call(
+        functools.partial(tick_kernel, step, tiles_dev),
+        out_shape=out_shape,
+        in_specs=[SMEM] + [VMEM] * len(operands),
+        out_specs=tuple(VMEM for _ in out_shape),
+        scratch_shapes=scratch,
+        input_output_aliases=aliases,
+        compiler_params=PARAMS,
+        name=f"tick_{step}",
+    )(lists, *operands)
+
+
+def finish_kernel(where_ref, rows_ref, sources_ref, total_ref, back_ref, out_ref):
+    out_ref[...] = sources_ref[...]
+    sub = total_ref.shape[2]
+    core = where_ref[1] & 1
+    for j in range(LIVE):
+        direction = rows_ref[0, j]
+        start = pl.multiple_of(rows_ref[1, j] * TILE, TILE)
+        for flip, ref in enumerate((total_ref, back_ref)):
+            shot = pl.multiple_of((core ^ flip) * sub, sub)
+            for part in range(2):
+                out_ref[direction, part, pl.ds(shot, sub), pl.ds(start, TILE)] += ref[j, part]
+
+
+def finish(where, rows, sources, total, back):
+    return pl.pallas_call(
+        finish_kernel,
+        out_shape=jax.ShapeDtypeStruct(sources.shape, sources.dtype),
+        in_specs=[SMEM, SMEM, VMEM, VMEM, VMEM],
+        out_specs=VMEM,
+        compiler_params=PARAMS,
+        name="finish",
+    )(where, rows, sources, total, back)
+
+
+def short_sweeps(where, rows, sources, lists, blocks, near, pieces, *unused):
+    tiles_dev = sources.shape[-1] // TILE
+    total, out_a, out_b = tick(0, tiles_dev, lists, blocks, *near, *pieces)
+    for step in range(1, len(ROUNDS) + 1):
+        got = swap_layers(out_a, out_b)
+        total, *out = tick(step, tiles_dev, lists, blocks, *got, total)
+        if out:
+            out_a, out_b = out
+    back = swap_tile(total[LIVE:], 1)
+    return finish(where, rows, sources, total, back)
+
+
+def long_sweeps(where, rows, sources, lists, blocks, near, pieces, green, rowcol, counts):
+    return full_sweeps(sources[None], green, rowcol, counts)
+
+
+def body(sources, green, rowcol, counts):
+    devices = lax.axis_size("tile")
+    layers = lax.axis_size("layer")
+    tiles_dev = sources.shape[-1] // TILE
+    tiles = tiles_dev * devices
+    if devices != 4 or 2 * tiles != 128 or tiles_dev != STRIDE:
+        return full_sweeps(sources, green, rowcol, counts)[None]
+    local = sources[0]
+    where = jnp.stack([lax.axis_index("layer"), lax.axis_index("tile")]).astype(jnp.int32)
+
+    codes, rows, order = slot_codes(where, rowcol[0], counts[0], layers * devices, 2 * tiles, tiles_dev)
+    packed = pack_green(order, green[0])
+    table = lax.all_to_all(codes, ("layer", "tile"), 0, 0, tiled=True)
+    lists = build_lists(where, table, layers, devices, tiles_dev)
+    first, second, copies = pick_tiles(lists, local, packed, tiles)
+    near = swap_layers(first, second)
+    partner = swap_tile(packed, 1)
+    copies = swap_tile(copies, 2)
+    copies_partner = swap_tile(copies, 1)
+    core, *cross = share_tiles(lists, *near, tiles, tiles_dev)
+    pieces = (swap_tile(core, 1), swap_tile(cross[0], 2), swap_tile(cross[1], 3))
+    highs, lows = zip(*[split_green(group) for group in (packed, partner, copies, copies_partner)])
+    out = lax.cond(
+        lists[FACTS, 0] == 0,
+        short_sweeps,
+        long_sweeps,
+        where,
+        rows,
+        local,
+        lists,
+        highs + lows,
+        near,
+        pieces,
+        green,
+        rowcol,
+        counts,
+    )
+    return out[None]
 
 
 def solution(mesh):

time: 246 us -> 97.9 us (0.40)
  waiting for transfers between devices: 113 us -> 35.6 us
  starting transfers between devices: 55.3 us -> 24.2 us
  local copies, waits for them, and re-layouts: 29.6 us -> 2.31 us
  other arithmetic: 23.8 us -> 0.07 us
  matrix products: 23.1 us -> 0 us
  Pallas kernels: 0 us -> 22.4 us
  blocking collectives: 0 us -> 11.1 us
    ppermute x20 -> x17, waiting for transfers between devices: 113 us -> 35.6 us  [the longest x10 24.5 us: swap(): return lax.ppermute(block, 'layer', pairs + [(b, a) for a, b in pairs])]
    ppermute x20 -> x17, starting transfers between devices: 55.3 us -> 24.2 us  [the longest x10 16.9 us: swap(): return lax.ppermute(block, 'layer', pairs + [(b, a) for a, b in pairs])]
    dot_general x10 -> x0, matrix products: 23.1 us -> none  [the longest x5 14.8 us: complex_term(): prod = jnp.einsum(pattern, picked, blocks, precision=lax.Precision.HIGHEST)]
    pallas_call x0 -> x15, Pallas kernels: none -> 22.4 us  [the longest x5 8.23 us: tick(): pl.pallas_call(functools.partial(tick_kernel, step, tiles_dev), out_shape...]
    gather x11 -> x0, local copies, waits for them, and re-layouts: 15 us -> none  [the longest x6 10.7 us: live_update(): picked = tiled[anchor, :, :, col_local[order]]]
    add x12 -> x0, other arithmetic: 11.9 us -> none  [the longest x5 9.25 us: body(): waves = local_sources + update.reshape(2, 2, shots, width)]
    reshape x5 -> x0, local copies, waits for them, and re-layouts: 11.9 us -> none  [body(): waves = local_sources + update.reshape(2, 2, shots, width)]
    all_to_all x0 -> x1, blocking collectives: none -> 11.1 us  [body(): table = lax.all_to_all(codes, ('layer', 'tile'), 0, 0, tiled=True)]
  transfers between devices with their start and end apart: 20 -> 17, of which waited for: 19 -> 12; matrix products, arithmetic and copies ran while one was open for 4% -> 1% of each run, Pallas kernels for 0% -> 10%
where the time goes in v4:
time: 97.9 us; the launch traced here: 96.8 us
  waiting for transfers between devices  35.6 us (36%)
  starting transfers between devices  24.2 us (25%)
  Pallas kernels  22.4 us (23%)
  blocking collectives  11.1 us (11%)
  local copies, waits for them, and re-layouts  2.31 us (2%)
    ppermute x10, waiting for transfers between devices, swap(): return lax.ppermute(block, 'layer', pairs + [(b, a) for a, b in pairs])  24.5 us
    ppermute x10, starting transfers between devices, swap(): return lax.ppermute(block, 'layer', pairs + [(b, a) for a, b in pairs])  16.9 us
    all_to_all x1, blocking collectives, body(): table = lax.all_to_all(codes, ('layer', 'tile'), 0, 0, tiled=True)  11.1 us
    ppermute x7, waiting for transfers between devices, swap_tile(): lax.ppermute(block, 'tile', [(i, i ^ offset) for i in range(lax.axis_size...  11 us
    pallas_call x5, Pallas kernels, tick(): pl.pallas_call(functools.partial(tick_kernel, step, tiles_dev), out_shape...  8.23 us
    ppermute x7, starting transfers between devices, swap_tile(): lax.ppermute(block, 'tile', [(i, i ^ offset) for i in range(lax.axis_size...  7.28 us
    pallas_call x4, Pallas kernels, split_green(): pl.pallas_call(split_kernel, out_shape=(shape, shape), in_specs=[VMEM], o...  3.94 us
    pallas_call x1, Pallas kernels, build_lists(): pl.pallas_call(functools.partial(lists_kernel, layers, devices, tiles_dev...  2.99 us
  transfers between devices with their start and end apart: 17, of which 12 were waited for; matrix products, arithmetic and copies ran while one was open for 1% of the time, Pallas kernels for 10%

profile of v4, /device:TPU:9, one launch (start us, length us, event | category | flops | bytes accessed | tf_op | source)
XLA Modules:
  0.0 96.8 jit_solution(3202976264933918396)
XLA Ops:
  0.0 0.8 copy.63.rowcol_ref
  0.8 0.1 pad_add_fusion.where_ref
  0.8 1.6 %slot_codes.1 = (s32[32,1,128]{2,1,0:T(1,128)S(1)}, s32[2,16]{1,0:T(2,128)}, s32[16]{0:T(128)S(1)}) custom-call(s32[2]{0:T(128)S(1)} %pad_add_fusion.where_ref, s32[20,2]{1,0:T(8,128)S(1)} %copy.63.rowcol_ref, s32[4]{0:T(128)} %bitcast.296), custom_call_target="tpu_custom_call" | custom-call | tf_op jit(solution)/shard_map/slot_codes/pallas_call | solution.py:153
  2.5 0.0 copy-start
  2.5 2.0 %pack_green.1.green_ref.packed_ref = f32[10,2,128,128]{3,2,1,0:T(8,128)S(1)} custom-call(s32[16]{0:T(128)S(1)} %get-tuple-element.104.order_ref, f32[20,2,128,128]{3,2,1,0:T(8,128)} %bitcast.273), custom_call_target="tpu_custom_call" | custom-call | tf_op jit(solution)/shard_map/pack_green/pallas_call | solution.py:178
  4.5 0.7 collective-permute-start.29
  5.2 11.1 %all_to_all.5.table_ref = s32[32,1,128]{2,1,0:T(1,128)S(1)} all-to-all(s32[32,1,128]{2,1,0:T(1,128)S(1)} %get-tuple-element.103), channel_id=1, replica_groups=mesh['layer'=8,'tile'=4] {'layer','tile'}, dimensions={0} | all-to-all | bytes 32768 | tf_op jit(solution)/shard_map/all_to_all | solution.py:647
  16.4 0.0 copy-done.10
  16.4 3.0 %build_lists.1.lists_ref = s32[24,128]{1,0:T(8,128)S(1)} custom-call(s32[2]{0:T(128)S(1)} %pad_add_fusion.where_ref, s32[32,1,128]{2,1,0:T(1,128)S(1)} %all_to_all.5.table_ref), custom_call_target="tpu_custom_call" | custom-call | tf_op jit(solution)/shard_map/build_lists/pallas_call | solution.py:360
  19.4 0.0 copy-done
  19.4 1.5 %pick_tiles.1 = (f32[9,2,32,128]{3,2,1,0:T(8,128)S(1)}, f32[9,2,32,128]{3,2,1,0:T(8,128)S(1)}, f32[4,2,128,128]{3,2,1,0:T(8,128)S(1)}) custom-call(s32[24,128]{1,0:T(8,128)S(1)} %build_lists.1.lists_ref, f32[2,2,32,2048]{3,2,1,0:T(8,128)S(1)} %bitcast.271, f32[10,2,128,128]{3,2,1,0:T(8,128)S(1)} %pack_green.1.green_ref.packed_ref), custom_call_target="tpu_custom_call" | custom-call | tf_op jit(solution)/shard_map/pick_tiles/pallas_call | solution.py:419
  20.9 0.5 collective-permute-start.30
  21.3 3.0 %collective-permute-start.32 = (f32[9,2,32,128]{3,2,1,0:T(8,128)S(1)}, f32[9,2,32,128]{3,2,1,0:T(8,128)S(1)}, u32[]{:S(2)}, u32[]{:S(2)}) collective-permute-start(f32[9,2,32,128]{3,2,1,0:T(8,128)S(1)} %get-tuple-element.114), channel_id=1, source_target_pairs={{4,8},{12,16},{20,24},{8,4},{16,12},{24,20},{5,9},{13,17},{21,25},... | collective-permute-start | bytes 884744 | tf_op jit(solution)/shard_map/ppermute | solution.py:116
  24.4 0.4 collective-permute-start.33
  24.8 8.8 %collective-permute-done.30.green_ref = f32[4,2,128,128]{3,2,1,0:T(8,128)S(1)} collective-permute-done((f32[4,2,128,128]{3,2,1,0:T(8,128)S(1)}, f32[4,2,128,128]{3,2,1,0:T(8,128)S(1)}, u32[]{:S(2)}, u32[]{:S(2)}) %collective-permute-start.30) | collective-permute-done | bytes 524320 | tf_op jit(solution)/shard_map/ppermute | solution.py:108
  33.6 1.7 %collective-permute-start.31 = (f32[4,2,128,128]{3,2,1,0:T(8,128)S(1)}, f32[4,2,128,128]{3,2,1,0:T(8,128)S(1)}, u32[]{:S(2)}, u32[]{:S(2)}) collective-permute-start(f32[4,2,128,128]{3,2,1,0:T(8,128)S(1)} %collective-permute-done.30.green_ref), channel_id=1, source_target_pairs={{0,1},{1,0},{2,3},{3,2},{4,5},{5,4},{6,7},{7,6},{8,9},{9,8},{10,11... | collective-permute-start | bytes 1572872 | tf_op jit(solution)/shard_map/ppermute | solution.py:108
  35.3 0.0 collective-permute-done.32.first_ref
  35.3 4.1 %collective-permute-done.33.second_ref = f32[9,2,32,128]{3,2,1,0:T(8,128)S(1)} collective-permute-done((f32[9,2,32,128]{3,2,1,0:T(8,128)S(1)}, f32[9,2,32,128]{3,2,1,0:T(8,128)S(1)}, u32[]{:S(2)}, u32[]{:S(2)}) %collective-permute-start.33) | collective-permute-done | bytes 294944 | tf_op jit(solution)/shard_map/ppermute | solution.py:116
  39.4 1.4 %share_tiles.1 = (f32[2,9,2,16,128]{4,3,2,1,0:T(8,128)S(1)}, f32[2,4,2,16,128]{4,3,2,1,0:T(8,128)S(1)}, f32[2,4,2,16,128]{4,3,2,1,0:T(8,128)S(1)}) custom-call(s32[24,128]{1,0:T(8,128)S(1)} %build_lists.1.lists_ref, f32[9,2,32,128]{3,2,1,0:T(8,128)S(1)} %collective-permute-done.32.first_ref, f32[9,2,32,128]{3,2,1,0:T(8,128)S(1)} %collective-permute-done.33.second_ref), custom_call_target="tpu_custom_call" | custom-call | tf_op jit(solution)/shard_map/share_tiles/pallas_call | solution.py:458
  40.8 0.6 collective-permute-start.34
  41.3 1.1 %collective-permute-start.35 = (f32[2,4,2,16,128]{4,3,2,1,0:T(8,128)S(1)}, f32[2,4,2,16,128]{4,3,2,1,0:T(8,128)S(1)}, u32[]{:S(2)}, u32[]{:S(2)}) collective-permute-start(f32[2,4,2,16,128]{4,3,2,1,0:T(8,128)S(1)} %get-tuple-element.117), channel_id=1, source_target_pairs={{0,2},{1,3},{2,0},{3,1},{4,6},{5,7},{6,4},{7,5},{8,10},{9,11},{10,... | collective-permute-start | bytes 393224 | tf_op jit(solution)/shard_map/ppermute | solution.py:108
  42.4 0.6 collective-permute-start.36
  43.0 1.3 %split_green.4 = (bf16[10,128,256]{2,1,0:T(8,128)(2,1)S(1)}, bf16[10,128,256]{2,1,0:T(8,128)(2,1)}) custom-call(f32[10,2,128,128]{3,2,1,0:T(8,128)S(1)} %pack_green.1.green_ref.packed_ref), custom_call_target="tpu_custom_call" | custom-call | tf_op jit(solution)/shard_map/split_green/pallas_call | solution.py:383
  44.3 0.5 slice.201
  45.5 0.0 copy-done.7
  45.5 0.2 split_green.6
  45.7 0.0 collective-permute-done.31.green_ref
  45.7 1.0 %split_green.7 = (bf16[4,128,256]{2,1,0:T(8,128)(2,1)}, bf16[4,128,256]{2,1,0:T(8,128)(2,1)}) custom-call(f32[4,2,128,128]{3,2,1,0:T(8,128)S(1)} %collective-permute-done.31.green_ref), custom_call_target="tpu_custom_call" | custom-call | tf_op jit(solution)/shard_map/split_green/pallas_call | solution.py:383
  46.7 0.0 collective-permute-done.29.green_ref
  46.7 1.5 %split_green.5 = (bf16[10,128,256]{2,1,0:T(8,128)(2,1)}, bf16[10,128,256]{2,1,0:T(8,128)(2,1)}) custom-call(f32[10,2,128,128]{3,2,1,0:T(8,128)S(1)} %collective-permute-done.29.green_ref), custom_call_target="tpu_custom_call" | custom-call | tf_op jit(solution)/shard_map/split_green/pallas_call | solution.py:383
  48.2 0.0 collective-permute-done.35
  48.2 1.2 %collective-permute-done.36 = f32[2,4,2,16,128]{4,3,2,1,0:T(8,128)S(1)} collective-permute-done((f32[2,4,2,16,128]{4,3,2,1,0:T(8,128)S(1)}, f32[2,4,2,16,128]{4,3,2,1,0:T(8,128)S(1)}, u32[]{:S(2)}, u32[]{:S(2)}) %collective-permute-start.36) | collective-permute-done | bytes 131104 | tf_op jit(solution)/shard_map/ppermute | solution.py:108
  49.4 0.0 collective-permute-done.34
  49.4 0.0 copy-done.9
  49.4 0.0 copy-done.12
  49.4 46.5 %conditional.1 = (f32[1,2,2,32,2048]{4,3,2,1,0:T(8,128)S(1)}) conditional(s32[]{:T(128)} %bitcast.79, (s32[1,4]{1,0:T(1,128)S(1)}, s32[1,20,2]{1,2,0:T(2,128)S(1)}, f32[1,20,2,128,128]{4,3,2,1,0:T(8,128)}, f32[1,2,2,32,2048]{4,3,2,1,0:T(8,128)S(1)}) %tuple.42, (s32[24,128]{1,0:T(8,128)S(1)}, bf16[10,128,256]{2,1,0:T(8,128)(2,1)S(1)}, ...), branch_computations={%region_0.3_spmd, %region_2.4_spmd} | conditional | flops 1425904896 | bytes 126296072 | solution.py:657
  49.7 2.8 %tick_0.1 = (f32[20,2,16,128]{3,2,1,0:T(8,128)S(1)}, f32[8,2,16,128]{3,2,1,0:T(8,128)S(1)}, f32[8,2,16,128]{3,2,1,0:T(8,128)S(1)}) custom-call(s32[24,128]{1,0:T(8,128)S(1)} %get-tuple-element.60.lists_ref, bf16[10,128,256]{2,1,0:T(8,128)(2,1)S(1)} %get-tuple-element.61.refs_0_, bf16[10,128,256]{2,1,0:T(8,128)(2,1)} %get-tuple-element.62.refs_1_, ...), custom_call_target="tpu_custom_call" | custom-call | tf_op jit(solution)/shard_map/cond/branch_1_fun/tick_0/pallas_call | solution.py:583
  52.4 3.1 %collective-permute-start = (f32[8,2,16,128]{3,2,1,0:T(8,128)S(1)}, f32[8,2,16,128]{3,2,1,0:T(8,128)S(1)}, u32[]{:S(2)}, u32[]{:S(2)}) collective-permute-start(f32[8,2,16,128]{3,2,1,0:T(8,128)S(1)} %get-tuple-element.74), channel_id=1, source_target_pairs={{4,8},{12,16},{20,24},{8,4},{16,12},{24,20},{5,9},{13,17},{21,25},... | collective-permute-start | bytes 393224 | tf_op jit(solution)/shard_map/cond/branch_1_fun/ppermute | solution.py:116
  55.5 0.4 collective-permute-start.1
  55.9 4.2 %collective-permute-done.refs_8_ = f32[8,2,16,128]{3,2,1,0:T(8,128)S(1)} collective-permute-done((f32[8,2,16,128]{3,2,1,0:T(8,128)S(1)}, f32[8,2,16,128]{3,2,1,0:T(8,128)S(1)}, u32[]{:S(2)}, u32[]{:S(2)}) %collective-permute-start) | collective-permute-done | bytes 131104 | tf_op jit(solution)/shard_map/cond/branch_1_fun/ppermute | solution.py:116
  60.1 3.3 %collective-permute-done.1.refs_9_ = f32[8,2,16,128]{3,2,1,0:T(8,128)S(1)} collective-permute-done((f32[8,2,16,128]{3,2,1,0:T(8,128)S(1)}, f32[8,2,16,128]{3,2,1,0:T(8,128)S(1)}, u32[]{:S(2)}, u32[]{:S(2)}) %collective-permute-start.1) | collective-permute-done | bytes 131104 | tf_op jit(solution)/shard_map/cond/branch_1_fun/ppermute | solution.py:116
  63.5 0.0 copy-done.2
  63.5 1.8 %tick_1.1 = (f32[20,2,16,128]{3,2,1,0:T(8,128)S(1)}, f32[5,2,16,128]{3,2,1,0:T(8,128)S(1)}, f32[5,2,16,128]{3,2,1,0:T(8,128)S(1)}) custom-call(s32[24,128]{1,0:T(8,128)S(1)} %get-tuple-element.60.lists_ref, bf16[10,128,256]{2,1,0:T(8,128)(2,1)S(1)} %get-tuple-element.61.refs_0_, ...), custom_call_target="tpu_custom_call", output_to_operand_aliasing={{0}: (11, {})} | custom-call | tf_op jit(solution)/shard_map/cond/branch_1_fun/tick_1/pallas_call | solution.py:583
  65.3 2.9 %collective-permute-start.2 = (f32[5,2,16,128]{3,2,1,0:T(8,128)S(1)}, f32[5,2,16,128]{3,2,1,0:T(8,128)S(1)}, u32[]{:S(2)}, u32[]{:S(2)}) collective-permute-start(f32[5,2,16,128]{3,2,1,0:T(8,128)S(1)} %get-tuple-element.77), channel_id=1, source_target_pairs={{4,8},{12,16},{20,24},{8,4},{16,12},{24,20},{5,9},{13,17},{21,25},... | collective-permute-start | bytes 245768 | tf_op jit(solution)/shard_map/cond/branch_1_fun/ppermute | solution.py:116
  68.2 0.5 collective-permute-start.3
  68.8 2.7 %collective-permute-done.2.refs_8_ = f32[5,2,16,128]{3,2,1,0:T(8,128)S(1)} collective-permute-done((f32[5,2,16,128]{3,2,1,0:T(8,128)S(1)}, f32[5,2,16,128]{3,2,1,0:T(8,128)S(1)}, u32[]{:S(2)}, u32[]{:S(2)}) %collective-permute-start.2) | collective-permute-done | bytes 81952 | tf_op jit(solution)/shard_map/cond/branch_1_fun/ppermute | solution.py:116
  71.5 2.7 %collective-permute-done.3.refs_9_ = f32[5,2,16,128]{3,2,1,0:T(8,128)S(1)} collective-permute-done((f32[5,2,16,128]{3,2,1,0:T(8,128)S(1)}, f32[5,2,16,128]{3,2,1,0:T(8,128)S(1)}, u32[]{:S(2)}, u32[]{:S(2)}) %collective-permute-start.3) | collective-permute-done | bytes 81952 | tf_op jit(solution)/shard_map/cond/branch_1_fun/ppermute | solution.py:116
  74.2 1.5 %tick_2.1 = (f32[20,2,16,128]{3,2,1,0:T(8,128)S(1)}, f32[4,2,16,128]{3,2,1,0:T(8,128)S(1)}, f32[4,2,16,128]{3,2,1,0:T(8,128)S(1)}) custom-call(s32[24,128]{1,0:T(8,128)S(1)} %get-tuple-element.60.lists_ref, bf16[10,128,256]{2,1,0:T(8,128)(2,1)S(1)} %get-tuple-element.61.refs_0_, ...), custom_call_target="tpu_custom_call", output_to_operand_aliasing={{0}: (11, {})} | custom-call | tf_op jit(solution)/shard_map/cond/branch_1_fun/tick_2/pallas_call | solution.py:583
  75.7 2.8 %collective-permute-start.4 = (f32[4,2,16,128]{3,2,1,0:T(8,128)S(1)}, f32[4,2,16,128]{3,2,1,0:T(8,128)S(1)}, u32[]{:S(2)}, u32[]{:S(2)}) collective-permute-start(f32[4,2,16,128]{3,2,1,0:T(8,128)S(1)} %get-tuple-element.80), channel_id=1, source_target_pairs={{4,8},{12,16},{20,24},{8,4},{16,12},{24,20},{5,9},{13,17},{21,25},... | collective-permute-start | bytes 196616 | tf_op jit(solution)/shard_map/cond/branch_1_fun/ppermute | solution.py:116
  78.5 0.5 collective-permute-start.5
  79.0 2.7 %collective-permute-done.4.refs_8_ = f32[4,2,16,128]{3,2,1,0:T(8,128)S(1)} collective-permute-done((f32[4,2,16,128]{3,2,1,0:T(8,128)S(1)}, f32[4,2,16,128]{3,2,1,0:T(8,128)S(1)}, u32[]{:S(2)}, u32[]{:S(2)}) %collective-permute-start.4) | collective-permute-done | bytes 65568 | tf_op jit(solution)/shard_map/cond/branch_1_fun/ppermute | solution.py:116
  81.7 2.0 %collective-permute-done.5.refs_9_ = f32[4,2,16,128]{3,2,1,0:T(8,128)S(1)} collective-permute-done((f32[4,2,16,128]{3,2,1,0:T(8,128)S(1)}, f32[4,2,16,128]{3,2,1,0:T(8,128)S(1)}, u32[]{:S(2)}, u32[]{:S(2)}) %collective-permute-start.5) | collective-permute-done | bytes 65568 | tf_op jit(solution)/shard_map/cond/branch_1_fun/ppermute | solution.py:116
  83.7 1.2 %tick_3.1 = (f32[20,2,16,128]{3,2,1,0:T(8,128)S(1)}, f32[3,2,16,128]{3,2,1,0:T(8,128)S(1)}, f32[3,2,16,128]{3,2,1,0:T(8,128)S(1)}) custom-call(s32[24,128]{1,0:T(8,128)S(1)} %get-tuple-element.60.lists_ref, bf16[10,128,256]{2,1,0:T(8,128)(2,1)S(1)} %get-tuple-element.61.refs_0_, ...), custom_call_target="tpu_custom_call", output_to_operand_aliasing={{0}: (11, {})} | custom-call | tf_op jit(solution)/shard_map/cond/branch_1_fun/tick_3/pallas_call | solution.py:583
  84.9 2.5 %collective-permute-start.6 = (f32[3,2,16,128]{3,2,1,0:T(8,128)S(1)}, f32[3,2,16,128]{3,2,1,0:T(8,128)S(1)}, u32[]{:S(2)}, u32[]{:S(2)}) collective-permute-start(f32[3,2,16,128]{3,2,1,0:T(8,128)S(1)} %get-tuple-element.83), channel_id=1, source_target_pairs={{4,8},{12,16},{20,24},{8,4},{16,12},{24,20},{5,9},{13,17},{21,25},... | collective-permute-start | bytes 147464 | tf_op jit(solution)/shard_map/cond/branch_1_fun/ppermute | solution.py:116
  87.4 0.8 collective-permute-start.7
  88.2 2.6 %collective-permute-done.6.refs_8_ = f32[3,2,16,128]{3,2,1,0:T(8,128)S(1)} collective-permute-done((f32[3,2,16,128]{3,2,1,0:T(8,128)S(1)}, f32[3,2,16,128]{3,2,1,0:T(8,128)S(1)}, u32[]{:S(2)}, u32[]{:S(2)}) %collective-permute-start.6) | collective-permute-done | bytes 49184 | tf_op jit(solution)/shard_map/cond/branch_1_fun/ppermute | solution.py:116
  90.8 0.2 collective-permute-done.7.refs_9_
  91.0 1.0 tick_4.1.total_ref
  91.9 2.1 %collective-permute-start.8 = (f32[10,2,16,128]{3,2,1,0:T(8,128)S(1)}, f32[10,2,16,128]{3,2,1,0:T(8,128)S(1)}, u32[]{:S(2)}, u32[]{:S(2)}) collective-permute-start(f32[10,2,16,128]{3,2,1,0:T(8,128)S(1)} %slice.172), channel_id=1, source_target_pairs={{0,1},{1,0},{2,3},{3,2},{4,5},{5,4},{6,7},{7,6},{8,9},{9,8},{10,11... | collective-permute-start | bytes 491528 | tf_op jit(solution)/shard_map/cond/branch_1_fun/ppermute | solution.py:108
  94.1 1.0 %collective-permute-done.8.back_ref = f32[10,2,16,128]{3,2,1,0:T(8,128)S(1)} collective-permute-done((f32[10,2,16,128]{3,2,1,0:T(8,128)S(1)}, f32[10,2,16,128]{3,2,1,0:T(8,128)S(1)}, u32[]{:S(2)}, u32[]{:S(2)}) %collective-permute-start.8) | collective-permute-done | bytes 163872 | tf_op jit(solution)/shard_map/cond/branch_1_fun/ppermute | solution.py:108
  95.1 0.0 copy-done.11
  95.1 0.7 finish.1
  95.9 0.0 copy-start.8
  95.9 1.0 copy-done.8
  (17 shorter events, 0.0 us)
Async XLA Ops:
  0.8 15.5 %copy-start.10 = (s32[2]{0:T(128)}, s32[2]{0:T(128)S(1)}, u32[]{:S(2)}) copy-start(s32[2]{0:T(128)S(1)} %pad_add_fusion.where_ref) | copy-start | bytes 28
  2.5 16.9 %copy-start = (f32[1,2,2,32,2048]{4,3,2,1,0:T(8,128)S(1)}, f32[1,2,2,32,2048]{4,3,2,1,0:T(8,128)}, u32[]{:S(2)}) copy-start(f32[1,2,2,32,2048]{4,3,2,1,0:T(8,128)} %param.8) | copy-start | bytes 3145732
  4.5 42.2 %collective-permute-start.29 = (f32[10,2,128,128]{3,2,1,0:T(8,128)S(1)}, f32[10,2,128,128]{3,2,1,0:T(8,128)S(1)}, u32[]{:S(2)}, u32[]{:S(2)}) collective-permute-start(f32[10,2,128,128]{3,2,1,0:T(8,128)S(1)} %pack_green.1.green_ref.packed_ref), channel_id=1, source_target_pairs={{0,1},{1,0},{2,3},{3,2},{4,5},{5,4},{6,7},{7,6},{8,9},{9,8},{10,11... | collective-permute-start | bytes 3932168 | tf_op jit(solution)/shard_map/ppermute | solution.py:108
  20.9 12.7 %collective-permute-start.30 = (f32[4,2,128,128]{3,2,1,0:T(8,128)S(1)}, f32[4,2,128,128]{3,2,1,0:T(8,128)S(1)}, u32[]{:S(2)}, u32[]{:S(2)}) collective-permute-start(f32[4,2,128,128]{3,2,1,0:T(8,128)S(1)} %get-tuple-element.107), channel_id=1, source_target_pairs={{0,2},{1,3},{2,0},{3,1},{4,6},{5,7},{6,4},{7,5},{8,10},{9,11},{10,... | collective-permute-start | bytes 1572872 | tf_op jit(solution)/shard_map/ppermute | solution.py:108
  21.3 13.9 %collective-permute-start.32 = (f32[9,2,32,128]{3,2,1,0:T(8,128)S(1)}, f32[9,2,32,128]{3,2,1,0:T(8,128)S(1)}, u32[]{:S(2)}, u32[]{:S(2)}) collective-permute-start(f32[9,2,32,128]{3,2,1,0:T(8,128)S(1)} %get-tuple-element.114), channel_id=1, source_target_pairs={{4,8},{12,16},{20,24},{8,4},{16,12},{24,20},{5,9},{13,17},{21,25},... | collective-permute-start | bytes 884744 | tf_op jit(solution)/shard_map/ppermute | solution.py:116
  24.4 15.0 %collective-permute-start.33 = (f32[9,2,32,128]{3,2,1,0:T(8,128)S(1)}, f32[9,2,32,128]{3,2,1,0:T(8,128)S(1)}, u32[]{:S(2)}, u32[]{:S(2)}) collective-permute-start(f32[9,2,32,128]{3,2,1,0:T(8,128)S(1)} %get-tuple-element.115), channel_id=1, source_target_pairs={{0,4},{8,12},{16,20},{24,28},{4,0},{12,8},{20,16},{28,24},{1,5},{9... | collective-permute-start | bytes 884744 | tf_op jit(solution)/shard_map/ppermute | solution.py:116
  33.6 12.1 %collective-permute-start.31 = (f32[4,2,128,128]{3,2,1,0:T(8,128)S(1)}, f32[4,2,128,128]{3,2,1,0:T(8,128)S(1)}, u32[]{:S(2)}, u32[]{:S(2)}) collective-permute-start(f32[4,2,128,128]{3,2,1,0:T(8,128)S(1)} %collective-permute-done.30.green_ref), channel_id=1, source_target_pairs={{0,1},{1,0},{2,3},{3,2},{4,5},{5,4},{6,7},{7,6},{8,9},{9,8},{10,11... | collective-permute-start | bytes 1572872 | tf_op jit(solution)/shard_map/ppermute | solution.py:108
  35.3 10.2 %copy-start.7 = (f32[9,2,32,128]{3,2,1,0:T(8,128)}, f32[9,2,32,128]{3,2,1,0:T(8,128)S(1)}, u32[]{:S(2)}) copy-start(f32[9,2,32,128]{3,2,1,0:T(8,128)S(1)} %collective-permute-done.32.first_ref) | copy-start | bytes 884740
  40.8 8.6 %collective-permute-start.34 = (f32[2,9,2,16,128]{4,3,2,1,0:T(8,128)S(1)}, f32[2,9,2,16,128]{4,3,2,1,0:T(8,128)S(1)}, u32[]{:S(2)}, u32[]{:S(2)}) collective-permute-start(f32[2,9,2,16,128]{4,3,2,1,0:T(8,128)S(1)} %get-tuple-element.116), channel_id=1, source_target_pairs={{0,1},{1,0},{2,3},{3,2},{4,5},{5,4},{6,7},{7,6},{8,9},{9,8},{10,11... | collective-permute-start | bytes 884744 | tf_op jit(solution)/shard_map/ppermute | solution.py:108
  41.3 6.9 %collective-permute-start.35 = (f32[2,4,2,16,128]{4,3,2,1,0:T(8,128)S(1)}, f32[2,4,2,16,128]{4,3,2,1,0:T(8,128)S(1)}, u32[]{:S(2)}, u32[]{:S(2)}) collective-permute-start(f32[2,4,2,16,128]{4,3,2,1,0:T(8,128)S(1)} %get-tuple-element.117), channel_id=1, source_target_pairs={{0,2},{1,3},{2,0},{3,1},{4,6},{5,7},{6,4},{7,5},{8,10},{9,11},{10,... | collective-permute-start | bytes 393224 | tf_op jit(solution)/shard_map/ppermute | solution.py:108
  42.4 7.0 %collective-permute-start.36 = (f32[2,4,2,16,128]{4,3,2,1,0:T(8,128)S(1)}, f32[2,4,2,16,128]{4,3,2,1,0:T(8,128)S(1)}, u32[]{:S(2)}, u32[]{:S(2)}) collective-permute-start(f32[2,4,2,16,128]{4,3,2,1,0:T(8,128)S(1)} %get-tuple-element.118), channel_id=1, source_target_pairs={{0,3},{1,2},{2,1},{3,0},{4,7},{5,6},{6,5},{7,4},{8,11},{9,10},{10,... | collective-permute-start | bytes 393224 | tf_op jit(solution)/shard_map/ppermute | solution.py:108
  43.0 6.3 %copy-start.9 = (s32[1,4]{1,0:T(1,128)S(1)}, s32[1,4]{1,0:T(1,128)}, u32[]{:S(2)}) copy-start(s32[1,4]{1,0:T(1,128)} %param.11) | copy-start | bytes 52
  43.0 6.3 %copy-start.12 = (s32[1,20,2]{1,2,0:T(2,128)S(1)}, s32[1,20,2]{1,2,0:T(2,128)}, u32[]{:S(2)}) copy-start(s32[1,20,2]{1,2,0:T(2,128)} %param.10) | copy-start | bytes 484
  49.6 13.9 %copy-start.1 = (bf16[10,128,256]{2,1,0:T(8,128)(2,1)S(1)}, bf16[10,128,256]{2,1,0:T(8,128)(2,1)}, u32[]{:S(2)}) copy-start(bf16[10,128,256]{2,1,0:T(8,128)(2,1)} %get-tuple-element.65.refs_4_) | copy-start | bytes 1966084 | tf_op jit(solution)/shard_map/cond
  49.6 13.9 %copy-start.2 = (bf16[10,128,256]{2,1,0:T(8,128)(2,1)S(1)}, bf16[10,128,256]{2,1,0:T(8,128)(2,1)}, u32[]{:S(2)}) copy-start(bf16[10,128,256]{2,1,0:T(8,128)(2,1)} %get-tuple-element.62.refs_1_) | copy-start | bytes 1966084 | tf_op jit(solution)/shard_map/cond
  49.6 13.8 %copy-start.3 = (bf16[10,128,256]{2,1,0:T(8,128)(2,1)S(1)}, bf16[10,128,256]{2,1,0:T(8,128)(2,1)}, u32[]{:S(2)}) copy-start(bf16[10,128,256]{2,1,0:T(8,128)(2,1)} %get-tuple-element.66.refs_5_) | copy-start | bytes 1966084 | tf_op jit(solution)/shard_map/cond
  49.6 13.8 %copy-start.4 = (bf16[4,128,256]{2,1,0:T(8,128)(2,1)S(1)}, bf16[4,128,256]{2,1,0:T(8,128)(2,1)}, u32[]{:S(2)}) copy-start(bf16[4,128,256]{2,1,0:T(8,128)(2,1)} %get-tuple-element.64.refs_3_) | copy-start | bytes 786436 | tf_op jit(solution)/shard_map/cond
  49.7 13.8 %copy-start.5 = (bf16[4,128,256]{2,1,0:T(8,128)(2,1)S(1)}, bf16[4,128,256]{2,1,0:T(8,128)(2,1)}, u32[]{:S(2)}) copy-start(bf16[4,128,256]{2,1,0:T(8,128)(2,1)} %get-tuple-element.68.refs_7_) | copy-start | bytes 786436 | tf_op jit(solution)/shard_map/cond
  52.4 7.7 %collective-permute-start = (f32[8,2,16,128]{3,2,1,0:T(8,128)S(1)}, f32[8,2,16,128]{3,2,1,0:T(8,128)S(1)}, u32[]{:S(2)}, u32[]{:S(2)}) collective-permute-start(f32[8,2,16,128]{3,2,1,0:T(8,128)S(1)} %get-tuple-element.74), channel_id=1, source_target_pairs={{4,8},{12,16},{20,24},{8,4},{16,12},{24,20},{5,9},{13,17},{21,25},... | collective-permute-start | bytes 393224 | tf_op jit(solution)/shard_map/cond/branch_1_fun/ppermute | solution.py:116
  55.5 8.0 %collective-permute-start.1 = (f32[8,2,16,128]{3,2,1,0:T(8,128)S(1)}, f32[8,2,16,128]{3,2,1,0:T(8,128)S(1)}, u32[]{:S(2)}, u32[]{:S(2)}) collective-permute-start(f32[8,2,16,128]{3,2,1,0:T(8,128)S(1)} %get-tuple-element.75), channel_id=1, source_target_pairs={{0,4},{8,12},{16,20},{24,28},{4,0},{12,8},{20,16},{28,24},{1,5},{9... | collective-permute-start | bytes 393224 | tf_op jit(solution)/shard_map/cond/branch_1_fun/ppermute | solution.py:116
  65.3 6.2 %collective-permute-start.2 = (f32[5,2,16,128]{3,2,1,0:T(8,128)S(1)}, f32[5,2,16,128]{3,2,1,0:T(8,128)S(1)}, u32[]{:S(2)}, u32[]{:S(2)}) collective-permute-start(f32[5,2,16,128]{3,2,1,0:T(8,128)S(1)} %get-tuple-element.77), channel_id=1, source_target_pairs={{4,8},{12,16},{20,24},{8,4},{16,12},{24,20},{5,9},{13,17},{21,25},... | collective-permute-start | bytes 245768 | tf_op jit(solution)/shard_map/cond/branch_1_fun/ppermute | solution.py:116
  68.2 6.0 %collective-permute-start.3 = (f32[5,2,16,128]{3,2,1,0:T(8,128)S(1)}, f32[5,2,16,128]{3,2,1,0:T(8,128)S(1)}, u32[]{:S(2)}, u32[]{:S(2)}) collective-permute-start(f32[5,2,16,128]{3,2,1,0:T(8,128)S(1)} %get-tuple-element.78), channel_id=1, source_target_pairs={{0,4},{8,12},{16,20},{24,28},{4,0},{12,8},{20,16},{28,24},{1,5},{9... | collective-permute-start | bytes 245768 | tf_op jit(solution)/shard_map/cond/branch_1_fun/ppermute | solution.py:116
  75.7 6.0 %collective-permute-start.4 = (f32[4,2,16,128]{3,2,1,0:T(8,128)S(1)}, f32[4,2,16,128]{3,2,1,0:T(8,128)S(1)}, u32[]{:S(2)}, u32[]{:S(2)}) collective-permute-start(f32[4,2,16,128]{3,2,1,0:T(8,128)S(1)} %get-tuple-element.80), channel_id=1, source_target_pairs={{4,8},{12,16},{20,24},{8,4},{16,12},{24,20},{5,9},{13,17},{21,25},... | collective-permute-start | bytes 196616 | tf_op jit(solution)/shard_map/cond/branch_1_fun/ppermute | solution.py:116
  78.5 5.2 %collective-permute-start.5 = (f32[4,2,16,128]{3,2,1,0:T(8,128)S(1)}, f32[4,2,16,128]{3,2,1,0:T(8,128)S(1)}, u32[]{:S(2)}, u32[]{:S(2)}) collective-permute-start(f32[4,2,16,128]{3,2,1,0:T(8,128)S(1)} %get-tuple-element.81), channel_id=1, source_target_pairs={{0,4},{8,12},{16,20},{24,28},{4,0},{12,8},{20,16},{28,24},{1,5},{9... | collective-permute-start | bytes 196616 | tf_op jit(solution)/shard_map/cond/branch_1_fun/ppermute | solution.py:116
  84.9 5.8 %collective-permute-start.6 = (f32[3,2,16,128]{3,2,1,0:T(8,128)S(1)}, f32[3,2,16,128]{3,2,1,0:T(8,128)S(1)}, u32[]{:S(2)}, u32[]{:S(2)}) collective-permute-start(f32[3,2,16,128]{3,2,1,0:T(8,128)S(1)} %get-tuple-element.83), channel_id=1, source_target_pairs={{4,8},{12,16},{20,24},{8,4},{16,12},{24,20},{5,9},{13,17},{21,25},... | collective-permute-start | bytes 147464 | tf_op jit(solution)/shard_map/cond/branch_1_fun/ppermute | solution.py:116
  87.4 3.5 %collective-permute-start.7 = (f32[3,2,16,128]{3,2,1,0:T(8,128)S(1)}, f32[3,2,16,128]{3,2,1,0:T(8,128)S(1)}, u32[]{:S(2)}, u32[]{:S(2)}) collective-permute-start(f32[3,2,16,128]{3,2,1,0:T(8,128)S(1)} %get-tuple-element.84), channel_id=1, source_target_pairs={{0,4},{8,12},{16,20},{24,28},{4,0},{12,8},{20,16},{28,24},{1,5},{9... | collective-permute-start | bytes 147464 | tf_op jit(solution)/shard_map/cond/branch_1_fun/ppermute | solution.py:116
  91.0 4.2 %copy-start.11 = (s32[2]{0:T(128)S(1)}, s32[2]{0:T(128)}, u32[]{:S(2)}) copy-start(s32[2]{0:T(128)} %get-tuple-element.57.where_ref) | copy-start | bytes 28 | tf_op jit(solution)/shard_map/cond
  91.0 4.2 %copy-start.13 = (s32[2,16]{1,0:T(2,128)S(1)}, s32[2,16]{1,0:T(2,128)}, u32[]{:S(2)}) copy-start(s32[2,16]{1,0:T(2,128)} %get-tuple-element.58.rows_ref) | copy-start | bytes 388 | tf_op jit(solution)/shard_map/cond
  91.9 3.2 %collective-permute-start.8 = (f32[10,2,16,128]{3,2,1,0:T(8,128)S(1)}, f32[10,2,16,128]{3,2,1,0:T(8,128)S(1)}, u32[]{:S(2)}, u32[]{:S(2)}) collective-permute-start(f32[10,2,16,128]{3,2,1,0:T(8,128)S(1)} %slice.172), channel_id=1, source_target_pairs={{0,1},{1,0},{2,3},{3,2},{4,5},{5,4},{6,7},{7,6},{8,9},{9,8},{10,11... | collective-permute-start | bytes 491528 | tf_op jit(solution)/shard_map/cond/branch_1_fun/ppermute | solution.py:108
  95.9 1.0 %copy-start.8 = (f32[1,2,2,32,2048]{4,3,2,1,0:T(8,128)}, f32[1,2,2,32,2048]{4,3,2,1,0:T(8,128)S(1)}, u32[]{:S(2)}) copy-start(f32[1,2,2,32,2048]{4,3,2,1,0:T(8,128)S(1)} %get-tuple-element.193) | copy-start | bytes 3145732

commit v5 on v4

--- a/solution.py
+++ b/solution.py
@@ -15,7 +15,7 @@
 SLOTS = KINDS * CAP
 LIVE = 2 * CAP
 STRIDE = 16
-READ = 9
+READ = 15
 CROSS = 4
 EXTRA = 4
 ROUNDS = (8, 5, 4, 3)
@@ -24,10 +24,11 @@
 VMEM = pl.BlockSpec(memory_space=pltpu.VMEM)
 SMEM = pl.BlockSpec(memory_space=pltpu.SMEM)
 ANY = pl.BlockSpec(memory_space=pl.ANY)
-PARAMS = pltpu.CompilerParams(vmem_limit_bytes=32 * 1024 * 1024)
-
-SEND, RECV, SOURCE, FOREIGN, OFFER, READS, LEND, COPY_OUT, COPY_IN, CODE, FACTS = 0, 4, 8, 9, 10, 11, 12, 13, 14, 15, 16
-TABLE_ROWS = 24
+HBM = pl.BlockSpec(memory_space=pltpu.HBM)
+PARAMS = pltpu.CompilerParams(vmem_limit_bytes=16 * 1024 * 1024)
+
+LEND, COPY_OUT, FACTS = range(3)
+SEND, RECV, COPY_IN, CODE, SOURCE, FOREIGN, STEP_FACTS = range(7)
 
 
 def from_behind(block, axis, distance):
@@ -186,7 +187,8 @@
     )(order, green)
 
 
-def lists_kernel(layers, devices, tiles_dev, where_ref, table_ref, out_ref, writes, reads, active, changed, now, sets, seen):
+def lists_kernel(layers, devices, tiles_dev, where_ref, table_ref, share_ref, *refs):
+    step_refs, (writes, reads, active, changed, now, sets, seen) = refs[:-7], refs[-7:]
     lanes = 128
     tiles = tiles_dev * devices
     pad = 2
@@ -267,10 +269,10 @@
         each(collect)
 
     same_half = (down >= tiles) == (across >= tiles)
-    same_group = (down >> 4) == (across >> 4)
-    half_total, group_total = as_mask(same_half), as_mask(same_group)
+    same_pair = (down >> 5) == (across >> 5)
+    half_total, pair_total = as_mask(same_half), as_mask(same_pair)
     half_before = as_mask(same_half & (down < across))
-    group_before = as_mask(same_group & (down < across))
+    pair_before = as_mask(same_pair & (down < across))
     room = jnp.zeros((8, lanes), jnp.float32)
     for j, most in enumerate(ROUNDS):
         room = jnp.where(row8 == j, float(most), room)
@@ -292,10 +294,10 @@
         for which in range(2):
             counts = by_columns(changed[index + pad] * wanted_by(which, index), half_total)
             over = jnp.maximum(over, jnp.where(row8 < len(ROUNDS), counts - room, -1.0))
-        counts = by_columns(seen[index + pad], group_total)
+        counts = by_columns(seen[index + pad], pair_total)
         over = jnp.maximum(over, jnp.where(row8 == 2, counts - READ, -1.0))
         over = jnp.maximum(over, jnp.where((row8 < 2) & (tile_pair != row8), counts - CROSS, -1.0))
-        counts = by_columns(sets[index], group_total)
+        counts = by_columns(sets[index], pair_total)
         over = jnp.maximum(over, jnp.where((row8 < 2) & (slot_pair != row8) & (slot_pair < 2), counts - EXTRA, -1.0))
         now[0] = over
 
@@ -313,7 +315,7 @@
         return sent * (by_columns(sent, half_before) + 1.0)
 
     def ranked(flags):
-        return flags * (by_columns(flags, group_before) + 1.0)
+        return flags * (by_columns(flags, pair_before) + 1.0)
 
     mine = travelling(layer)
     above = travelling(jnp.maximum(layer - 1, 0))
@@ -324,14 +326,11 @@
     send = jnp.where((send >= 0) & (wdir == odd), send + SHIFT, send)
     recv = jnp.where((recv >= 0) & (rdir != odd), recv + SHIFT, recv)
     here = seen[layer + pad]
-    ahead, behind = seen[layer + pad + 1], seen[layer + pad - 1]
     foreign = pick(here, pair) * jnp.where(tile_pair[:1] != pair, 1.0, 0.0)
     lent = pick(here, other)
-    offered = jnp.where(low[:1], ahead[2:3], behind[2:3])
     flags = jnp.where(row8 == 0, here[2:3], 0.0)
     flags = jnp.where(row8 == 1, foreign, flags)
-    flags = jnp.where(row8 == 2, offered, flags)
-    flags = jnp.where(row8 == 3, lent, flags)
+    flags = jnp.where(row8 == 2, lent, flags)
     ranks = ranked(flags)
     sources = by_columns(ranks, reads[layer]).astype(jnp.int32) - 1
     chosen = sets[layer]
@@ -339,18 +338,27 @@
     flags = jnp.where(row8 == 1, pick(chosen, pair) * jnp.where(slot_pair[:1] != pair, 1.0, 0.0), flags)
     copies = ranked(flags).astype(jnp.int32)
     ranks = ranks.astype(jnp.int32)
-    out_ref[...] = jnp.zeros_like(out_ref)
-    rounds = len(ROUNDS)
-    out_ref[SEND : SEND + rounds] = send[:rounds]
-    out_ref[RECV : RECV + rounds] = recv[:rounds]
-    out_ref[SOURCE : SOURCE + 2] = sources[:2]
-    out_ref[OFFER : OFFER + 1] = ranks[2:3]
-    out_ref[READS : READS + 1] = ranks[0:1]
-    out_ref[LEND : LEND + 1] = ranks[3:4]
-    out_ref[COPY_OUT : COPY_OUT + 2] = copies[:2]
-    out_ref[CODE : CODE + 1] = code
     facts = jnp.where(lane == 0, jnp.where(over > 0.0, 1, 0), jnp.where(lane == 1, layer, place))
-    out_ref[FACTS : FACTS + 1] = facts
+
+    def write(ref, rows):
+        ref[...] = jnp.zeros_like(ref)
+        for j, values in rows.items():
+            ref[j : j + 1] = values
+
+    lend_rank = jnp.where(tile_pair[:1] == pair, ranks[2:3], 0)
+    chosen = (lend_rank == (down & (tiles - 1)) + 1) & ((across >= tiles) == (down >= tiles))
+    read_at = jnp.where(chosen, (ranks[0:1] - 1).astype(jnp.float32), 0.0)
+    lend = by_rows(jnp.ones((8, lanes), jnp.float32), narrow(read_at)).astype(jnp.int32)
+    write(share_ref, {LEND: lend[0:1], COPY_OUT: copies[0:1], FACTS: facts})
+    for step, ref in enumerate(step_refs):
+        rows = {COPY_IN: copies[1:2], STEP_FACTS: facts}
+        if step < len(ROUNDS):
+            rows[SEND] = send[step : step + 1]
+        if step:
+            rows[RECV] = recv[step - 1 : step]
+        else:
+            rows.update({CODE: code, SOURCE: sources[0:1], FOREIGN: sources[1:2]})
+        write(ref, rows)
 
 
 def build_lists(where, table, layers, devices, tiles_dev):
@@ -359,9 +367,9 @@
     square = pltpu.VMEM((layers, lanes, lanes), jnp.bfloat16)
     return pl.pallas_call(
         functools.partial(lists_kernel, layers, devices, tiles_dev),
-        out_shape=jax.ShapeDtypeStruct((TABLE_ROWS, lanes), jnp.int32),
+        out_shape=(jax.ShapeDtypeStruct((8, lanes), jnp.int32),) * (len(ROUNDS) + 2),
         in_specs=[SMEM, VMEM],
-        out_specs=VMEM,
+        out_specs=(VMEM,) * (len(ROUNDS) + 2),
         scratch_shapes=[square, square, rows(layers), rows(layers + 4), rows(layers + 4), rows(layers), rows(layers + 4)],
         compiler_params=PARAMS,
         name="build_lists",
@@ -390,79 +398,116 @@
     )(packed)
 
 
-def pick_kernel(tiles, lists_ref, sources_ref, packed_ref, first_ref, second_ref, copy_ref):
-    odd, place = lists_ref[FACTS, 1] & 1, lists_ref[FACTS, 2]
-    tiles_dev = sources_ref.shape[3] // TILE
-    first_ref[...] = jnp.zeros_like(first_ref)
-    second_ref[...] = jnp.zeros_like(second_ref)
+def pick_kernel(layers, devices, tiles_dev, where_ref, table_ref, own_ref, partner_ref, first_ref, second_ref, ranks, scalars, sem):
+    lanes = table_ref.shape[-1]
+    tiles = tiles_dev * devices
+    layer, place = where_ref[0], where_ref[1]
+    odd = layer & 1
+    down = lax.broadcasted_iota(jnp.int32, (lanes, lanes), 0)
+    across = lax.broadcasted_iota(jnp.int32, (lanes, lanes), 1)
+    as_mask = lambda mask: jnp.where(mask, 1.0, 0.0).astype(jnp.bfloat16)
+
+    def offered(index, direction):
+        at = jnp.clip(index, 0, layers - 1)
+        code = table_ref[at * devices]
+        for device in range(1, devices):
+            code = code + table_ref[at * devices + device]
+        kind = (code >> 1) & 3
+        rdir = (kind ^ (kind >> 1)) & 1
+        live = ((code & 1) == 1) & (rdir == direction) & (index == at)
+        reads = as_mask(down == jnp.where(live, direction * tiles + ((code >> 3) & 8191), -1))
+        ones = jnp.ones((8, lanes), jnp.bfloat16)
+        total = lax.dot_general(ones, reads, (((1,), (1,)), ((), ())), preferred_element_type=jnp.float32)
+        return jnp.minimum(total, 1.0)
+
+    flags = offered(layer + 1, 0) + offered(layer - 1, 1)
+    before = as_mask(((down >> 5) == (across >> 5)) & (down < across))
+    position = jnp.dot(flags.astype(jnp.bfloat16), before, preferred_element_type=jnp.float32)
+    lane = across[:1]
+    in_pair = ((lane & (tiles - 1)) >> 5) == (place >> 1)
+    rank = jnp.where(in_pair, (flags * (position + 1.0))[:1], 0.0).astype(jnp.int32)
+    chosen = (rank == (down & (tiles - 1)) + 1) & ((across >= tiles) == (down >= tiles))
+    tile_of = jnp.where(chosen, (across & (tiles - 1)).astype(jnp.float32), 0.0).astype(jnp.bfloat16)
+    ones = jnp.ones((8, lanes), jnp.bfloat16)
+    ids = lax.dot_general(ones, tile_of, (((1,), (1,)), ((), ())), preferred_element_type=jnp.float32)
+    ranks[...] = ids.astype(jnp.int32)
+    copy = pltpu.make_async_copy(ranks, scalars, sem)
+    copy.start()
+    copy.wait()
+    for j in range(READ):
+        found = []
+        for direction in range(2):
+            tile = scalars[0, direction * tiles + j]
+            start = pl.multiple_of((tile & (tiles_dev - 1)) * TILE, TILE)
+            mine = ((tile // tiles_dev) ^ place) & 1 == 0
+            at = (direction, slice(None), slice(None), pl.ds(start, TILE))
+            found.append(jnp.where(mine, own_ref[at], partner_ref[at]))
+        first_ref[j] = jnp.where(odd == 1, found[0], found[1])
+        second_ref[j] = jnp.where(odd == 1, found[1], found[0])
+
+
+def pick_tiles(where, table, own, partner, layers, devices, tiles_dev):
+    shape = jax.ShapeDtypeStruct((READ, 2, own.shape[2], TILE), jnp.float32)
+    lanes = table.shape[-1]
+    return pl.pallas_call(
+        functools.partial(pick_kernel, layers, devices, tiles_dev),
+        out_shape=(shape, shape),
+        in_specs=[SMEM, VMEM, VMEM, VMEM],
+        out_specs=(VMEM, VMEM),
+        scratch_shapes=[
+            pltpu.VMEM((8, lanes), jnp.int32),
+            pltpu.SMEM((8, lanes), jnp.int32),
+            pltpu.SemaphoreType.DMA,
+        ],
+        compiler_params=PARAMS,
+        name="pick_tiles",
+    )(where, table, own, partner)
+
+
+def lend_kernel(share_ref, packed_ref, partner_ref, *copy_refs):
+    place = share_ref[FACTS, 2]
+    half = len(copy_refs)
+    for copy_ref in copy_refs:
+        copy_ref[...] = jnp.zeros_like(copy_ref)
+    for group, ref in enumerate((packed_ref, partner_ref)):
+        for j in range(LIVE):
+            rank = share_ref[COPY_OUT, (place ^ group) * STRIDE + j]
+            at = rank - 1 - (place & 1) * half
+            for k, copy_ref in enumerate(copy_refs):
+
+                @pl.when((rank > 0) & (at == k))
+                def _():
+                    copy_ref[...] = ref[j]
+
+
+def lend_blocks(share, packed, partner):
+    return pl.pallas_call(
+        lend_kernel,
+        out_shape=(jax.ShapeDtypeStruct(packed.shape[1:], packed.dtype),) * (EXTRA // 2),
+        in_specs=[SMEM, VMEM, VMEM],
+        out_specs=(VMEM,) * (EXTRA // 2),
+        compiler_params=PARAMS,
+        name="lend_blocks",
+    )(share, packed, partner)
+
+
+def share_kernel(tiles, share_ref, first_ref, second_ref, cross_ref):
+    odd = share_ref[FACTS, 1] & 1
     for direction in range(2):
-        for tile in range(tiles_dev):
-            rank = lists_ref[OFFER, direction * tiles + place * tiles_dev + tile]
-            found = (rank > 0) & (rank <= READ)
-
-            def copy_to(ref):
-                ref[jnp.clip(rank - 1, 0, READ - 1)] = sources_ref[direction, :, :, tile * TILE : (tile + 1) * TILE]
-
-            pl.when(found & (odd != direction))(functools.partial(copy_to, first_ref))
-            pl.when(found & (odd == direction))(functools.partial(copy_to, second_ref))
-    for j in range(LIVE):
-        rank = lists_ref[COPY_OUT, place * STRIDE + j]
-
-        @pl.when((rank > 0) & (rank <= EXTRA))
-        def _():
-            copy_ref[jnp.clip(rank - 1, 0, EXTRA - 1)] = packed_ref[j]
-
-
-def pick_tiles(lists, sources, packed, tiles):
-    shots = sources.shape[2]
-    shape = jax.ShapeDtypeStruct((READ, 2, shots, TILE), jnp.float32)
-    return pl.pallas_call(
-        functools.partial(pick_kernel, tiles),
-        out_shape=(shape, shape, jax.ShapeDtypeStruct((EXTRA,) + packed.shape[1:], packed.dtype)),
+        for j in range(CROSS):
+            at = jnp.clip(share_ref[LEND, direction * tiles + j], 0, READ - 1)
+            cross_ref[direction, j] = jnp.where(odd == direction, first_ref[at], second_ref[at])
+
+
+def share_tiles(share, first, second, tiles):
+    return pl.pallas_call(
+        functools.partial(share_kernel, tiles),
+        out_shape=jax.ShapeDtypeStruct((2, CROSS) + first.shape[1:], jnp.float32),
         in_specs=[SMEM, VMEM, VMEM],
-        out_specs=(VMEM, VMEM, VMEM),
-        compiler_params=PARAMS,
-        name="pick_tiles",
-    )(lists, sources, packed)
-
-
-def share_kernel(tiles, tiles_dev, lists_ref, first_ref, second_ref, core_ref, *cross_refs):
-    odd, place = lists_ref[FACTS, 1] & 1, lists_ref[FACTS, 2]
-    sub = core_ref.shape[3]
-    core = place & 1
-    theirs = pl.multiple_of((1 - core) * sub, sub)
-    core_ref[0] = first_ref[:, :, pl.ds(theirs, sub), :]
-    core_ref[1] = second_ref[:, :, pl.ds(theirs, sub), :]
-    for cross_ref in cross_refs:
-        cross_ref[...] = jnp.zeros_like(cross_ref)
-    for direction in range(2):
-        for tile in range(tiles_dev):
-            lane = direction * tiles + place * tiles_dev + tile
-            rank = lists_ref[LEND, lane]
-            at = jnp.clip(lists_ref[READS, lane] - 1, 0, READ - 1)
-
-            def copy_from(ref):
-                for flip, cross_ref in enumerate(cross_refs):
-                    shot = pl.multiple_of((core ^ flip) * sub, sub)
-                    cross_ref[direction, jnp.clip(rank - 1, 0, CROSS - 1)] = ref[at, :, pl.ds(shot, sub), :]
-
-            found = (rank > 0) & (rank <= CROSS)
-            pl.when(found & (odd == direction))(functools.partial(copy_from, first_ref))
-            pl.when(found & (odd != direction))(functools.partial(copy_from, second_ref))
-
-
-def share_tiles(lists, first, second, tiles, tiles_dev):
-    sub = first.shape[2] // 2
-    piece = jax.ShapeDtypeStruct((2, READ, 2, sub, TILE), jnp.float32)
-    cross = jax.ShapeDtypeStruct((2, CROSS, 2, sub, TILE), jnp.float32)
-    return pl.pallas_call(
-        functools.partial(share_kernel, tiles, tiles_dev),
-        out_shape=(piece, cross, cross),
-        in_specs=[SMEM, VMEM, VMEM],
-        out_specs=(VMEM, VMEM, VMEM),
+        out_specs=VMEM,
         compiler_params=PARAMS,
         name="share_tiles",
-    )(lists, first, second)
+    )(share, first, second)
 
 
 def block_term(x, high, low):
@@ -478,32 +523,27 @@
     return real, imag
 
 
-def tick_kernel(step, tiles_dev, lists_ref, *refs):
+def tick_kernel(step, tiles_dev, table_ref, *refs):
     refs = list(refs)
-    highs = [refs.pop(0) for _ in range(4)]
-    lows = [refs.pop(0) for _ in range(4)]
+    highs = [refs.pop(0) for _ in range(3)]
+    lows = [refs.pop(0) for _ in range(3)]
     first_ref, second_ref = refs.pop(0), refs.pop(0)
     last = step == len(ROUNDS)
     if step == 0:
-        core_ref, cross_refs, (total_ref, out_a, out_b, traces, acc) = refs[0], refs[1:3], refs[3:]
+        cross_ref, total_ref, out_a, out_b, traces, acc = refs
     elif last:
         _, total_ref = refs
     else:
         _, total_ref, out_a, out_b, acc = refs
-    odd, place = lists_ref[FACTS, 1] & 1, lists_ref[FACTS, 2]
+    odd, place = table_ref[STEP_FACTS, 1] & 1, table_ref[STEP_FACTS, 2]
     core = place & 1
     if step == 0:
-        sub = core_ref.shape[3]
-        shot = pl.multiple_of(core * sub, sub)
-        traces[:READ] = first_ref[:, :, pl.ds(shot, sub), :]
-        traces[READ : 2 * READ] = second_ref[:, :, pl.ds(shot, sub), :]
-        traces[2 * READ : 3 * READ] = core_ref[0]
-        traces[3 * READ : 4 * READ] = core_ref[1]
-        for j, ref in enumerate(cross_refs):
-            for direction in range(2):
-                at = 4 * READ + (2 * j + direction) * CROSS
-                traces[at : at + CROSS] = ref[direction]
-        empty = 4 * READ + 4 * CROSS
+        traces[:READ] = first_ref[...]
+        traces[READ : 2 * READ] = second_ref[...]
+        for direction in range(2):
+            at = 2 * READ + direction * CROSS
+            traces[at : at + CROSS] = cross_ref[direction]
+        empty = 2 * READ + 2 * CROSS
         traces[empty] = jnp.zeros(traces.shape[1:], jnp.float32)
     if not last:
         cap = out_a.shape[0]
@@ -511,19 +551,19 @@
 
     def entering(lane):
         if step:
-            value = lists_ref[RECV + step - 1, lane]
-            at = value & (SHIFT - 1)
-            return jnp.where(value < SHIFT, first_ref[at], second_ref[at])
-        code = lists_ref[CODE, lane]
+            value = table_ref[RECV, lane]
+            at = jnp.minimum(value & (SHIFT - 1), first_ref.shape[0] - 1)
+            x = jnp.where(value < SHIFT, first_ref[at], second_ref[at])
+            return x if step > 1 else jnp.where(value < 0, jnp.zeros_like(x), x)
+        code = table_ref[CODE, lane]
         kind = lax.shift_right_logical(code, 1) & 3
         rdir = (kind ^ lax.shift_right_logical(kind, 1)) & 1
         group = lax.div(lax.shift_right_logical(code, 3) & 8191, tiles_dev)
-        relative = group ^ place
-        near = lists_ref[SOURCE, lane]
-        far = lists_ref[FOREIGN, lane]
-        near_at = relative * 2 * READ + jnp.where(rdir == odd, 0, READ) + near
-        far_at = 4 * READ + (2 * (relative - 2) + rdir) * CROSS + far
-        at = jnp.where(relative < 2, jnp.where(near < 0, empty, near_at), jnp.where(far < 0, empty, far_at))
+        near = table_ref[SOURCE, lane]
+        far = table_ref[FOREIGN, lane]
+        near_at = jnp.where(near < 0, empty, jnp.where(rdir == odd, 0, READ) + near)
+        far_at = jnp.where(far < 0, empty, 2 * READ + rdir * CROSS + far)
+        at = jnp.where((group ^ place) < 2, near_at, far_at)
         return traces[jnp.clip(at, 0, empty)]
 
     def apply(lane, group, row, slot):
@@ -536,9 +576,9 @@
                 total_ref[slot, 0] += real
                 total_ref[slot, 1] += imag
         if not last:
-            value = lists_ref[SEND + step, lane]
+            value = table_ref[SEND, lane]
             at = jnp.where(value < SHIFT, value, value - SHIFT + cap)
-            at = jnp.where(value < 0, 2 * cap, at)
+            at = jnp.where(value < 0, 2 * cap, jnp.minimum(at, 2 * cap))
             acc[at, 0] += real
             acc[at, 1] += imag
 
@@ -546,25 +586,27 @@
         base = (place ^ group) * STRIDE
         for j in range(LIVE):
             step_in = functools.partial(apply, base + j, group, j, group * LIVE + j)
-            if step == 0:
+            if step < 2:
                 step_in()
             else:
-                pl.when(lists_ref[RECV + step - 1, base + j] >= 0)(step_in)
+                pl.when(table_ref[RECV, base + j] >= 0)(step_in)
     if not last:
         for group in range(2, 4):
             base = (place ^ group) * STRIDE
             for j in range(LIVE):
-                rank = lists_ref[COPY_IN, base + j]
+                rank = table_ref[COPY_IN, base + j]
                 wanted = rank > 0
                 if step:
-                    wanted = wanted & (lists_ref[RECV + step - 1, base + j] >= 0)
-                row = jnp.clip(rank - 1, 0, EXTRA - 1)
-                pl.when(wanted)(functools.partial(apply, base + j, group, row, None))
+                    wanted = wanted & (table_ref[RECV, base + j] >= 0)
+                entry = jnp.clip(rank - 1, 0, EXTRA - 1)
+                half = EXTRA // 2
+                row = jnp.where(lax.div(entry, half) == core, 0, half) + lax.rem(entry, half)
+                pl.when(wanted)(functools.partial(apply, base + j, 2, row, None))
         out_a[...] = acc[:cap]
         out_b[...] = acc[cap : 2 * cap]
 
 
-def tick(step, tiles_dev, lists, blocks, first, second, *data):
+def tick(step, tiles_dev, table, blocks, first, second, *data):
     sub = data[0].shape[-2]
     tile_shape = lambda count: jax.ShapeDtypeStruct((count, 2, sub, TILE), jnp.float32)
     room = lambda count: pltpu.VMEM((count, 2, sub, TILE), jnp.float32)
@@ -572,7 +614,7 @@
     scratch = []
     aliases = {}
     if step == 0:
-        scratch.append(room(4 * READ + 4 * CROSS + 1))
+        scratch.append(room(2 * READ + 2 * CROSS + 1))
     else:
         aliases = {1 + len(blocks) + 2: 0}
     if step < len(ROUNDS):
@@ -589,47 +631,49 @@
         input_output_aliases=aliases,
         compiler_params=PARAMS,
         name=f"tick_{step}",
-    )(lists, *operands)
-
-
-def finish_kernel(where_ref, rows_ref, sources_ref, total_ref, back_ref, out_ref):
-    out_ref[...] = sources_ref[...]
-    sub = total_ref.shape[2]
-    core = where_ref[1] & 1
+    )(table, *operands)
+
+
+def finish_kernel(share_ref, rows_ref, base_ref, total_ref, back_ref, out_ref, sums, sems):
+    sub = back_ref.shape[2]
+    core = share_ref[FACTS, 2] & 1
+    short = share_ref[FACTS, 0] == 0
+
+    def tile(j):
+        return rows_ref[0, j], slice(None), slice(None), pl.ds(pl.multiple_of(rows_ref[1, j] * TILE, TILE), TILE)
+
+    def move(source, target):
+        copies = [pltpu.make_async_copy(source.at[tile(j)], target.at[tile(j)], sems.at[j]) for j in range(LIVE)]
+        for copy in copies:
+            copy.start()
+        for copy in copies:
+            copy.wait()
+
+    move(base_ref, sums)
     for j in range(LIVE):
-        direction = rows_ref[0, j]
-        start = pl.multiple_of(rows_ref[1, j] * TILE, TILE)
+        direction, _, _, columns = tile(j)
         for flip, ref in enumerate((total_ref, back_ref)):
             shot = pl.multiple_of((core ^ flip) * sub, sub)
             for part in range(2):
-                out_ref[direction, part, pl.ds(shot, sub), pl.ds(start, TILE)] += ref[j, part]
-
-
-def finish(where, rows, sources, total, back):
+                sums[direction, part, pl.ds(shot, sub), columns] += jnp.where(short, ref[j, part], 0.0)
+    move(sums, out_ref)
+
+
+def finish(share, rows, base, total, back):
     return pl.pallas_call(
         finish_kernel,
-        out_shape=jax.ShapeDtypeStruct(sources.shape, sources.dtype),
-        in_specs=[SMEM, SMEM, VMEM, VMEM, VMEM],
-        out_specs=VMEM,
+        out_shape=jax.ShapeDtypeStruct(base.shape, base.dtype),
+        in_specs=[SMEM, SMEM, HBM, VMEM, VMEM],
+        out_specs=HBM,
+        scratch_shapes=[pltpu.VMEM(base.shape, base.dtype), pltpu.SemaphoreType.DMA((LIVE,))],
+        input_output_aliases={2: 0},
         compiler_params=PARAMS,
         name="finish",
-    )(where, rows, sources, total, back)
-
-
-def short_sweeps(where, rows, sources, lists, blocks, near, pieces, *unused):
-    tiles_dev = sources.shape[-1] // TILE
-    total, out_a, out_b = tick(0, tiles_dev, lists, blocks, *near, *pieces)
-    for step in range(1, len(ROUNDS) + 1):
-        got = swap_layers(out_a, out_b)
-        total, *out = tick(step, tiles_dev, lists, blocks, *got, total)
-        if out:
-            out_a, out_b = out
-    back = swap_tile(total[LIVE:], 1)
-    return finish(where, rows, sources, total, back)
-
-
-def long_sweeps(where, rows, sources, lists, blocks, near, pieces, green, rowcol, counts):
-    return full_sweeps(sources[None], green, rowcol, counts)
+    )(share, rows, base, total, back)
+
+
+def keep_sources(sources, green, rowcol, counts):
+    return sources[0]
 
 
 def body(sources, green, rowcol, counts):
@@ -643,32 +687,34 @@
     where = jnp.stack([lax.axis_index("layer"), lax.axis_index("tile")]).astype(jnp.int32)
 
     codes, rows, order = slot_codes(where, rowcol[0], counts[0], layers * devices, 2 * tiles, tiles_dev)
-    packed = pack_green(order, green[0])
+    core, sub = lax.axis_index("tile") % 2, local.shape[2] // 2
+    half_of = lambda which: lax.dynamic_slice_in_dim(local, which * sub, sub, axis=2)
+    mine, theirs = half_of(core), swap_tile(half_of(1 - core), 1)
     table = lax.all_to_all(codes, ("layer", "tile"), 0, 0, tiled=True)
-    lists = build_lists(where, table, layers, devices, tiles_dev)
-    first, second, copies = pick_tiles(lists, local, packed, tiles)
-    near = swap_layers(first, second)
+    packed, mine, theirs, table = lax.optimization_barrier((pack_green(order, green[0]), mine, theirs, table))
+    picked = pick_tiles(where, table, mine, theirs, layers, devices, tiles_dev)
+    picked, table = lax.optimization_barrier((picked, table))
+    near = swap_layers(*picked)
+    share, *steps = build_lists(where, table, layers, devices, tiles_dev)
     partner = swap_tile(packed, 1)
-    copies = swap_tile(copies, 2)
-    copies_partner = swap_tile(copies, 1)
-    core, *cross = share_tiles(lists, *near, tiles, tiles_dev)
-    pieces = (swap_tile(core, 1), swap_tile(cross[0], 2), swap_tile(cross[1], 3))
-    highs, lows = zip(*[split_green(group) for group in (packed, partner, copies, copies_partner)])
-    out = lax.cond(
-        lists[FACTS, 0] == 0,
-        short_sweeps,
-        long_sweeps,
-        where,
-        rows,
-        local,
-        lists,
-        highs + lows,
-        near,
-        pieces,
-        green,
-        rowcol,
-        counts,
-    )
+    copies = [swap_tile(block, 2) for block in lend_blocks(share, packed, partner)]
+    shared, copies = lax.optimization_barrier((share_tiles(share, *near, tiles), copies))
+    cross = swap_tile(shared, 2)
+    copies = jnp.stack(copies)
+    extra = split_green(jnp.concatenate([copies, swap_tile(copies, 1)]))
+    highs, lows = zip(split_green(packed), split_green(partner), extra)
+    blocks = highs + lows
+    total, out_a, out_b = tick(0, tiles_dev, steps[0], blocks, *near, cross)
+    out_a, out_b, sources = lax.optimization_barrier((out_a, out_b, sources))
+    got = swap_layers(out_a, out_b)
+    base = lax.cond(share[FACTS, 0] == 0, keep_sources, full_sweeps, sources, green, rowcol, counts)
+    got, base = lax.optimization_barrier((got, base))
+    for step in range(1, len(ROUNDS) + 1):
+        total, *out = tick(step, tiles_dev, steps[step], blocks, *got, total)
+        if out:
+            got = swap_layers(*out)
+    back = swap_tile(total[LIVE:], 1)
+    out = finish(share, rows, base, total, back)
     return out[None]
 
 

time: 97.9 us -> 87.7 us (0.90)
  blocking collectives: 11.1 us -> 0 us
  starting transfers between devices: 24.2 us -> 29.7 us
  Pallas kernels: 22.4 us -> 19.1 us
  waiting for transfers between devices: 35.6 us -> 32.7 us
  local copies, waits for them, and re-layouts: 2.31 us -> 3.87 us
    all_to_all x1 -> x0, blocking collectives: 11.1 us -> none  [body(): table = lax.all_to_all(codes, ('layer', 'tile'), 0, 0, tiled=True)]
    ppermute x7, waiting for transfers between devices: 11 us -> 4.77 us  [swap_tile(): lax.ppermute(block, 'tile', [(i, i ^ offset) for i in range(lax.axis_size...]
    all_to_all x0 -> x1, starting transfers between devices: none -> 5.8 us  [body(): table = lax.all_to_all(codes, ('layer', 'tile'), 0, 0, tiled=True)]
    all_to_all x0 -> x1, waiting for transfers between devices: none -> 3.47 us  [body(): table = lax.all_to_all(codes, ('layer', 'tile'), 0, 0, tiled=True)]
    pallas_call x4 -> x3, Pallas kernels: 3.94 us -> 1.01 us  [split_green(): pl.pallas_call(split_kernel, out_shape=(shape, shape), in_specs=[VMEM], o...]
    ppermute x7, starting transfers between devices: 7.28 us -> 5.9 us  [swap_tile(): lax.ppermute(block, 'tile', [(i, i ^ offset) for i in range(lax.axis_size...]
    dynamic_slice x0 -> x1, local copies, waits for them, and re-layouts: none -> 1.3 us  [body(): lax.dynamic_slice_in_dim(local, which * sub, sub, axis=2)]
    pallas_call x5, Pallas kernels: 8.23 us -> 7.1 us  [tick(): pl.pallas_call(functools.partial(tick_kernel, step, tiles_dev), out_shape...]
  transfers between devices with their start and end apart: 17 -> 18, of which waited for: 12 -> 14; matrix products, arithmetic and copies ran while one was open for 1% -> 2% of each run, Pallas kernels for 10% -> 13%
where the time goes in v5:
time: 87.7 us; the launch traced here: 86.6 us
  waiting for transfers between devices  32.7 us (37%)
  starting transfers between devices  29.7 us (34%)
  Pallas kernels  19.1 us (22%)
  local copies, waits for them, and re-layouts  3.87 us (4%)
  between operations  0.88 us (1%)
    ppermute x10, waiting for transfers between devices, swap(): return lax.ppermute(block, 'layer', pairs + [(b, a) for a, b in pairs])  24.4 us
    ppermute x10, starting transfers between devices, swap(): return lax.ppermute(block, 'layer', pairs + [(b, a) for a, b in pairs])  18 us
    pallas_call x5, Pallas kernels, tick(): pl.pallas_call(functools.partial(tick_kernel, step, tiles_dev), out_shape...  7.1 us
    ppermute x7, starting transfers between devices, swap_tile(): lax.ppermute(block, 'tile', [(i, i ^ offset) for i in range(lax.axis_size...  5.9 us
    all_to_all x1, starting transfers between devices, body(): table = lax.all_to_all(codes, ('layer', 'tile'), 0, 0, tiled=True)  5.8 us
    ppermute x7, waiting for transfers between devices, swap_tile(): lax.ppermute(block, 'tile', [(i, i ^ offset) for i in range(lax.axis_size...  4.77 us
    all_to_all x1, waiting for transfers between devices, body(): table = lax.all_to_all(codes, ('layer', 'tile'), 0, 0, tiled=True)  3.47 us
    pallas_call x1, Pallas kernels, build_lists(): pl.pallas_call(functools.partial(lists_kernel, layers, devices, tiles_dev...  3.03 us
  transfers between devices with their start and end apart: 18, of which 14 were waited for; matrix products, arithmetic and copies ran while one was open for 2% of the time, Pallas kernels for 13%

profile of v5, /device:TPU:9, one launch (start us, length us, event | category | flops | bytes accessed | tf_op | source)
XLA Modules:
  0.0 86.6 jit_solution(4922602112609635325)
XLA Ops:
  0.0 0.0 copy-start.5
  0.0 1.3 %dynamic-slice_bitcast_fusion = (f32[2,2,16,2048]{3,2,1,0:T(8,128)S(1)}, f32[2,2,16,2048]{3,2,1,0:T(8,128)S(1)}) fusion(f32[1,2,2,32,2048]{4,3,2,1,0:T(8,128)} %param.8, s32[]{:T(128)S(6)} %select_n.146, s32[]{:T(128)S(6)} %select_n.145), kind=kLoop, calls=%fused_computation.191 | loop fusion | bytes 2097160 | tf_op jit(solution)/shard_map/dynamic_slice | solution.py:691
  1.3 0.7 collective-permute-start.20
  2.0 0.0 copy-done.5
  2.0 0.1 copy.62.rowcol_ref
  2.1 0.1 pad_add_fusion.where_ref
  2.2 0.0 copy-done.4
  2.2 1.5 %slot_codes.1 = (s32[32,1,128]{2,1,0:T(1,128)}, s32[2,16]{1,0:T(2,128)S(1)}, s32[16]{0:T(128)S(1)}) custom-call(s32[2]{0:T(128)S(1)} %pad_add_fusion.where_ref, s32[20,2]{1,0:T(8,128)S(1)} %copy.62.rowcol_ref, s32[4]{0:T(128)S(1)} %bitcast.301), custom_call_target="tpu_custom_call" | custom-call | tf_op jit(solution)/shard_map/slot_codes/pallas_call | solution.py:154
  3.8 5.8 %all-to-all-start = ((s32[32,1,128]{2,1,0:T(1,128)}), s32[32,1,128]{2,1,0:T(1,128)S(1)}, u32[]{:S(2)}, u32[]{:S(2)}) async-start(s32[32,1,128]{2,1,0:T(1,128)} %get-tuple-element.71), calls=%async_computation | async-start | bytes 32768 | tf_op jit(solution)/shard_map/all_to_all | solution.py:693
  9.6 2.0 %pack_green.1.green_ref.packed_ref = f32[10,2,128,128]{3,2,1,0:T(8,128)S(1)} custom-call(s32[16]{0:T(128)S(1)} %get-tuple-element.70.order_ref, f32[20,2,128,128]{3,2,1,0:T(8,128)} %bitcast.279), custom_call_target="tpu_custom_call" | custom-call | tf_op jit(solution)/shard_map/pack_green/pallas_call | solution.py:179
  11.6 3.5 %all-to-all-done.table_ref = s32[32,1,128]{2,1,0:T(1,128)S(1)} async-done(((s32[32,1,128]{2,1,0:T(1,128)}), s32[32,1,128]{2,1,0:T(1,128)S(1)}, u32[]{:S(2)}, u32[]{:S(2)}) %all-to-all-start) | async-done | bytes 16416 | tf_op jit(solution)/shard_map/all_to_all | solution.py:693
  15.0 0.0 collective-permute-done.20.partner_ref
  15.0 0.8 collective-permute-start.21
  15.8 1.8 %pick_tiles.1 = (f32[15,2,16,128]{3,2,1,0:T(8,128)S(1)}, f32[15,2,16,128]{3,2,1,0:T(8,128)S(1)}) custom-call(s32[2]{0:T(128)S(1)} %pad_add_fusion.where_ref, s32[32,1,128]{2,1,0:T(1,128)S(1)} %all-to-all-done.table_ref, f32[2,2,16,2048]{3,2,1,0:T(8,128)S(1)} %get-tuple-element.73.own_ref, f32[2,2,16,2048]{3,2,1,0:T(8,128)S(1)} %collective-permute-done.20.partner_ref), custom_call_target="tpu_custom_call" | custom-call | tf_op jit(solution)/shard_map/pick_tiles/pallas_call | solution.py:452
  17.6 3.1 %collective-permute-start.22 = (f32[15,2,16,128]{3,2,1,0:T(8,128)S(1)}, f32[15,2,16,128]{3,2,1,0:T(8,128)S(1)}, u32[]{:S(2)}, u32[]{:S(2)}) collective-permute-start(f32[15,2,16,128]{3,2,1,0:T(8,128)S(1)} %get-tuple-element.84), channel_id=1, source_target_pairs={{4,8},{12,16},{20,24},{8,4},{16,12},{24,20},{5,9},{13,17},{21,25},... | collective-permute-start | bytes 737288 | tf_op jit(solution)/shard_map/ppermute | solution.py:117
  20.7 0.4 collective-permute-start.23
  21.1 3.0 %build_lists.1 = (s32[8,128]{1,0:T(8,128)S(1)}, s32[8,128]{1,0:T(8,128)S(1)}, s32[8,128]{1,0:T(8,128)S(1)}, s32[8,128]{1,0:T(8,128)S(1)}, s32[8,128]{1,0:T(8,128)S(1)}, /*index=5*/s32[8,128]{1,0:T(8,128)S(1)}) custom-call(s32[2]{0:T(128)S(1)} %pad_add_fusion.where_ref, s32[32,1,128]{2,1,0:T(1,128)S(1)} %all-to-all-done.table_ref), custom_call_target="tpu_custom_call" | custom-call | tf_op jit(solution)/shard_map/build_lists/pallas_call | solution.py:368
  24.1 0.0 collective-permute-done.21.green_ref.partner_ref
  24.1 1.0 %lend_blocks.1 = (f32[2,128,128]{2,1,0:T(8,128)S(1)}, f32[2,128,128]{2,1,0:T(8,128)S(1)}) custom-call(s32[8,128]{1,0:T(8,128)S(1)} %get-tuple-element.78.share_ref, f32[10,2,128,128]{3,2,1,0:T(8,128)S(1)} %pack_green.1.green_ref.packed_ref, f32[10,2,128,128]{3,2,1,0:T(8,128)S(1)} %collective-permute-done.21.green_ref.partner_ref), custom_call_target="tpu_custom_call" | custom-call | tf_op jit(solution)/shard_map/lend_blocks/pallas_call | solution.py:484
  25.1 0.3 collective-permute-start.24
  25.4 1.2 %collective-permute-start.25 = (f32[2,128,128]{2,1,0:T(8,128)S(1)}, f32[2,128,128]{2,1,0:T(8,128)S(1)}, u32[]{:S(2)}, u32[]{:S(2)}) collective-permute-start(f32[2,128,128]{2,1,0:T(8,128)S(1)} %get-tuple-element.87), channel_id=1, source_target_pairs={{0,2},{1,3},{2,0},{3,1},{4,6},{5,7},{6,4},{7,5},{8,10},{9,11},{10,... | collective-permute-start | bytes 393224 | tf_op jit(solution)/shard_map/ppermute | solution.py:109
  26.7 1.4 %collective-permute-done.22.first_ref.refs_6_ = f32[15,2,16,128]{3,2,1,0:T(8,128)S(1)} collective-permute-done((f32[15,2,16,128]{3,2,1,0:T(8,128)S(1)}, f32[15,2,16,128]{3,2,1,0:T(8,128)S(1)}, u32[]{:S(2)}, u32[]{:S(2)}) %collective-permute-start.22) | collective-permute-done | bytes 245792 | tf_op jit(solution)/shard_map/ppermute | solution.py:117
  28.1 5.5 %collective-permute-done.23.second_ref.refs_7_ = f32[15,2,16,128]{3,2,1,0:T(8,128)S(1)} collective-permute-done((f32[15,2,16,128]{3,2,1,0:T(8,128)S(1)}, f32[15,2,16,128]{3,2,1,0:T(8,128)S(1)}, u32[]{:S(2)}, u32[]{:S(2)}) %collective-permute-start.23) | collective-permute-done | bytes 245792 | tf_op jit(solution)/shard_map/ppermute | solution.py:117
  33.6 0.6 share_tiles.1
  34.2 0.0 collective-permute-done.24
  34.2 0.0 collective-permute-done.25
  34.3 0.5 collective-permute-start.26
  34.8 0.3 collective-permute-start.27
  35.1 0.4 split_green.3
  35.5 0.4 split_green.4
  35.9 0.1 collective-permute-done.26
  36.0 0.2 split_green.5
  36.2 3.7 %collective-permute-done.27.refs_8_ = f32[2,4,2,16,128]{4,3,2,1,0:T(8,128)S(1)} collective-permute-done((f32[2,4,2,16,128]{4,3,2,1,0:T(8,128)S(1)}, f32[2,4,2,16,128]{4,3,2,1,0:T(8,128)S(1)}, u32[]{:S(2)}, u32[]{:S(2)}) %collective-permute-start.27) | collective-permute-done | bytes 131104 | tf_op jit(solution)/shard_map/ppermute | solution.py:109
  39.9 2.2 %tick_0.1 = (f32[20,2,16,128]{3,2,1,0:T(8,128)S(1)}, f32[8,2,16,128]{3,2,1,0:T(8,128)}, f32[8,2,16,128]{3,2,1,0:T(8,128)}) custom-call(s32[8,128]{1,0:T(8,128)S(1)} %get-tuple-element.80.table_ref, bf16[10,128,256]{2,1,0:T(8,128)(2,1)S(1)} %get-tuple-element.82.refs_0_, bf16[10,128,256]{2,1,0:T(8,128)(2,1)S(1)} %get-tuple-element.83.refs_1_, ...), custom_call_target="tpu_custom_call" | custom-call | tf_op jit(solution)/shard_map/tick_0/pallas_call | solution.py:625
  42.1 3.2 %collective-permute-start.28 = (f32[8,2,16,128]{3,2,1,0:T(8,128)}, f32[8,2,16,128]{3,2,1,0:T(8,128)}, u32[]{:S(2)}, u32[]{:S(2)}) collective-permute-start(f32[8,2,16,128]{3,2,1,0:T(8,128)} %get-tuple-element.97), channel_id=1, source_target_pairs={{4,8},{12,16},{20,24},{8,4},{16,12},{24,20},{5,9},{13,17},{21,25},... | collective-permute-start | bytes 393224 | tf_op jit(solution)/shard_map/ppermute | solution.py:117
  45.3 0.4 collective-permute-start.29
  45.7 0.5 slice.141
  46.8 0.0 copy-done
  46.8 1.2 %conditional.1 = (f32[2,2,32,2048]{3,2,1,0:T(8,128)}) conditional(s32[]{:T(128)} %bitcast.84, (f32[1,2,2,32,2048]{4,3,2,1,0:T(8,128)S(1)}, s32[1,4]{1,0:T(1,128)S(1)}, s32[1,20,2]{1,2,0:T(2,128)S(1)}, f32[1,20,2,128,128]{4,3,2,1,0:T(8,128)}) %tuple.44, f32[1,2,2,32,2048]{4,3,2,1,0:T(8,128)S(1)} %copy-done), branch_computations={%region_0.3_spmd, %region_2.4_spmd} | conditional | flops 1425904896 | bytes 128393224 | solution.py:710
  47.1 1.0 %copy.111 = f32[2,2,32,2048]{3,2,1,0:T(8,128)} copy(f32[2,2,32,2048]{3,2,1,0:T(8,128)S(1)} %bitcast.278) | data formatting | bytes 2097152 | tf_op jit(solution)/shard_map/cond
  48.0 1.3 %collective-permute-done.28.refs_6_ = f32[8,2,16,128]{3,2,1,0:T(8,128)} collective-permute-done((f32[8,2,16,128]{3,2,1,0:T(8,128)}, f32[8,2,16,128]{3,2,1,0:T(8,128)}, u32[]{:S(2)}, u32[]{:S(2)}) %collective-permute-start.28) | collective-permute-done | bytes 131104 | tf_op jit(solution)/shard_map/ppermute | solution.py:117
  49.3 4.1 %collective-permute-done.29.refs_7_ = f32[8,2,16,128]{3,2,1,0:T(8,128)} collective-permute-done((f32[8,2,16,128]{3,2,1,0:T(8,128)}, f32[8,2,16,128]{3,2,1,0:T(8,128)}, u32[]{:S(2)}, u32[]{:S(2)}) %collective-permute-start.29) | collective-permute-done | bytes 131104 | tf_op jit(solution)/shard_map/ppermute | solution.py:117
  53.4 1.8 %tick_1.1 = (f32[20,2,16,128]{3,2,1,0:T(8,128)S(1)}, f32[5,2,16,128]{3,2,1,0:T(8,128)S(1)}, f32[5,2,16,128]{3,2,1,0:T(8,128)S(1)}) custom-call(s32[8,128]{1,0:T(8,128)S(1)} %get-tuple-element.104.table_ref, bf16[10,128,256]{2,1,0:T(8,128)(2,1)S(1)} %get-tuple-element.82.refs_0_, ...), custom_call_target="tpu_custom_call", output_to_operand_aliasing={{0}: (9, {})} | custom-call | tf_op jit(solution)/shard_map/tick_1/pallas_call | solution.py:625
  55.2 3.2 %collective-permute-start.30 = (f32[5,2,16,128]{3,2,1,0:T(8,128)S(1)}, f32[5,2,16,128]{3,2,1,0:T(8,128)S(1)}, u32[]{:S(2)}, u32[]{:S(2)}) collective-permute-start(f32[5,2,16,128]{3,2,1,0:T(8,128)S(1)} %get-tuple-element.108), channel_id=1, source_target_pairs={{4,8},{12,16},{20,24},{8,4},{16,12},{24,20},{5,9},{13,17},{21,25},... | collective-permute-start | bytes 245768 | tf_op jit(solution)/shard_map/ppermute | solution.py:117
  58.4 0.4 collective-permute-start.31
  58.8 2.5 %collective-permute-done.30.refs_6_ = f32[5,2,16,128]{3,2,1,0:T(8,128)S(1)} collective-permute-done((f32[5,2,16,128]{3,2,1,0:T(8,128)S(1)}, f32[5,2,16,128]{3,2,1,0:T(8,128)S(1)}, u32[]{:S(2)}, u32[]{:S(2)}) %collective-permute-start.30) | collective-permute-done | bytes 81952 | tf_op jit(solution)/shard_map/ppermute | solution.py:117
  61.3 2.8 %collective-permute-done.31.refs_7_ = f32[5,2,16,128]{3,2,1,0:T(8,128)S(1)} collective-permute-done((f32[5,2,16,128]{3,2,1,0:T(8,128)S(1)}, f32[5,2,16,128]{3,2,1,0:T(8,128)S(1)}, u32[]{:S(2)}, u32[]{:S(2)}) %collective-permute-start.31) | collective-permute-done | bytes 81952 | tf_op jit(solution)/shard_map/ppermute | solution.py:117
  64.1 1.2 %tick_2.1 = (f32[20,2,16,128]{3,2,1,0:T(8,128)S(1)}, f32[4,2,16,128]{3,2,1,0:T(8,128)S(1)}, f32[4,2,16,128]{3,2,1,0:T(8,128)S(1)}) custom-call(s32[8,128]{1,0:T(8,128)S(1)} %get-tuple-element.103.table_ref, bf16[10,128,256]{2,1,0:T(8,128)(2,1)S(1)} %get-tuple-element.82.refs_0_, ...), custom_call_target="tpu_custom_call", output_to_operand_aliasing={{0}: (9, {})} | custom-call | tf_op jit(solution)/shard_map/tick_2/pallas_call | solution.py:625
  65.3 3.1 %collective-permute-start.32 = (f32[4,2,16,128]{3,2,1,0:T(8,128)S(1)}, f32[4,2,16,128]{3,2,1,0:T(8,128)S(1)}, u32[]{:S(2)}, u32[]{:S(2)}) collective-permute-start(f32[4,2,16,128]{3,2,1,0:T(8,128)S(1)} %get-tuple-element.111), channel_id=1, source_target_pairs={{4,8},{12,16},{20,24},{8,4},{16,12},{24,20},{5,9},{13,17},{21,25},... | collective-permute-start | bytes 196616 | tf_op jit(solution)/shard_map/ppermute | solution.py:117
  68.4 0.5 collective-permute-start.33
  68.9 2.3 %collective-permute-done.32.refs_6_ = f32[4,2,16,128]{3,2,1,0:T(8,128)S(1)} collective-permute-done((f32[4,2,16,128]{3,2,1,0:T(8,128)S(1)}, f32[4,2,16,128]{3,2,1,0:T(8,128)S(1)}, u32[]{:S(2)}, u32[]{:S(2)}) %collective-permute-start.32) | collective-permute-done | bytes 65568 | tf_op jit(solution)/shard_map/ppermute | solution.py:117
  71.2 2.0 %collective-permute-done.33.refs_7_ = f32[4,2,16,128]{3,2,1,0:T(8,128)S(1)} collective-permute-done((f32[4,2,16,128]{3,2,1,0:T(8,128)S(1)}, f32[4,2,16,128]{3,2,1,0:T(8,128)S(1)}, u32[]{:S(2)}, u32[]{:S(2)}) %collective-permute-start.33) | collective-permute-done | bytes 65568 | tf_op jit(solution)/shard_map/ppermute | solution.py:117
  73.3 1.1 %tick_3.1 = (f32[20,2,16,128]{3,2,1,0:T(8,128)S(1)}, f32[3,2,16,128]{3,2,1,0:T(8,128)S(1)}, f32[3,2,16,128]{3,2,1,0:T(8,128)S(1)}) custom-call(s32[8,128]{1,0:T(8,128)S(1)} %get-tuple-element.102.table_ref, bf16[10,128,256]{2,1,0:T(8,128)(2,1)S(1)} %get-tuple-element.82.refs_0_, ...), custom_call_target="tpu_custom_call", output_to_operand_aliasing={{0}: (9, {})} | custom-call | tf_op jit(solution)/shard_map/tick_3/pallas_call | solution.py:625
  74.4 3.1 %collective-permute-start.34 = (f32[3,2,16,128]{3,2,1,0:T(8,128)S(1)}, f32[3,2,16,128]{3,2,1,0:T(8,128)S(1)}, u32[]{:S(2)}, u32[]{:S(2)}) collective-permute-start(f32[3,2,16,128]{3,2,1,0:T(8,128)S(1)} %get-tuple-element.114), channel_id=1, source_target_pairs={{4,8},{12,16},{20,24},{8,4},{16,12},{24,20},{5,9},{13,17},{21,25},... | collective-permute-start | bytes 147464 | tf_op jit(solution)/shard_map/ppermute | solution.py:117
  77.5 0.7 collective-permute-start.35
  78.1 2.0 %collective-permute-done.34.refs_6_ = f32[3,2,16,128]{3,2,1,0:T(8,128)S(1)} collective-permute-done((f32[3,2,16,128]{3,2,1,0:T(8,128)S(1)}, f32[3,2,16,128]{3,2,1,0:T(8,128)S(1)}, u32[]{:S(2)}, u32[]{:S(2)}) %collective-permute-start.34) | collective-permute-done | bytes 49184 | tf_op jit(solution)/shard_map/ppermute | solution.py:117
  80.1 0.5 collective-permute-done.35.refs_7_
  80.6 0.8 tick_4.1.total_ref
  81.5 2.1 %collective-permute-start.36 = (f32[10,2,16,128]{3,2,1,0:T(8,128)S(1)}, f32[10,2,16,128]{3,2,1,0:T(8,128)S(1)}, u32[]{:S(2)}, u32[]{:S(2)}) collective-permute-start(f32[10,2,16,128]{3,2,1,0:T(8,128)S(1)} %slice.201), channel_id=1, source_target_pairs={{0,1},{1,0},{2,3},{3,2},{4,5},{5,4},{6,7},{7,6},{8,9},{9,8},{10,11... | collective-permute-start | bytes 491528 | tf_op jit(solution)/shard_map/ppermute | solution.py:109
  83.6 1.0 %collective-permute-done.36.back_ref = f32[10,2,16,128]{3,2,1,0:T(8,128)S(1)} collective-permute-done((f32[10,2,16,128]{3,2,1,0:T(8,128)S(1)}, f32[10,2,16,128]{3,2,1,0:T(8,128)S(1)}, u32[]{:S(2)}, u32[]{:S(2)}) %collective-permute-start.36) | collective-permute-done | bytes 163872 | tf_op jit(solution)/shard_map/ppermute | solution.py:109
  84.6 0.0 copy-done.2
  84.6 1.0 %finish.1 = f32[2,2,32,2048]{3,2,1,0:T(8,128)S(1)} custom-call(s32[8,128]{1,0:T(8,128)S(1)} %get-tuple-element.78.share_ref, s32[2,16]{1,0:T(2,128)S(1)} %get-tuple-element.79.rows_ref, f32[2,2,32,2048]{3,2,1,0:T(8,128)S(1)} %copy-done.2, f32[20,2,16,128]{3,2,1,0:T(8,128)S(1)} %tick_4.1.total_ref, ...), custom_call_target="tpu_custom_call", output_to_operand_aliasing={{}: (2, {})} | custom-call | tf_op jit(solution)/shard_map/finish/pallas_call | solution.py:663
  85.6 0.0 copy-start.3
  85.6 1.0 %copy-done.3 = f32[2,2,32,2048]{3,2,1,0:T(8,128)} copy-done((f32[2,2,32,2048]{3,2,1,0:T(8,128)}, f32[2,2,32,2048]{3,2,1,0:T(8,128)S(1)}, u32[]{:S(2)}) %copy-start.3) | copy-done | bytes 1048600
  (6 shorter events, 0.1 us)
Async XLA Ops:
  0.0 2.0 %copy-start.5 = (s32[1,20,2]{1,2,0:T(2,128)S(1)}, s32[1,20,2]{1,2,0:T(2,128)}, u32[]{:S(2)}) copy-start(s32[1,20,2]{1,2,0:T(2,128)} %param.10) | copy-start | bytes 484
  0.0 2.2 %copy-start.4 = (s32[1,4]{1,0:T(1,128)S(1)}, s32[1,4]{1,0:T(1,128)}, u32[]{:S(2)}) copy-start(s32[1,4]{1,0:T(1,128)} %param.11) | copy-start | bytes 52
  1.3 13.7 %collective-permute-start.20 = (f32[2,2,16,2048]{3,2,1,0:T(8,128)S(1)}, f32[2,2,16,2048]{3,2,1,0:T(8,128)S(1)}, u32[]{:S(2)}, u32[]{:S(2)}) collective-permute-start(f32[2,2,16,2048]{3,2,1,0:T(8,128)S(1)} %get-tuple-element.147), channel_id=1, source_target_pairs={{0,1},{1,0},{2,3},{3,2},{4,5},{5,4},{6,7},{7,6},{8,9},{9,8},{10,11... | collective-permute-start | bytes 1572872 | tf_op jit(solution)/shard_map/ppermute | solution.py:109
  3.8 11.3 %all-to-all-start = ((s32[32,1,128]{2,1,0:T(1,128)}), s32[32,1,128]{2,1,0:T(1,128)S(1)}, u32[]{:S(2)}, u32[]{:S(2)}) async-start(s32[32,1,128]{2,1,0:T(1,128)} %get-tuple-element.71), calls=%async_computation | async-start | bytes 32768 | tf_op jit(solution)/shard_map/all_to_all | solution.py:693
  15.0 9.1 %collective-permute-start.21 = (f32[10,2,128,128]{3,2,1,0:T(8,128)S(1)}, f32[10,2,128,128]{3,2,1,0:T(8,128)S(1)}, u32[]{:S(2)}, u32[]{:S(2)}) collective-permute-start(f32[10,2,128,128]{3,2,1,0:T(8,128)S(1)} %pack_green.1.green_ref.packed_ref), channel_id=1, source_target_pairs={{0,1},{1,0},{2,3},{3,2},{4,5},{5,4},{6,7},{7,6},{8,9},{9,8},{10,11... | collective-permute-start | bytes 3932168 | tf_op jit(solution)/shard_map/ppermute | solution.py:109
  17.6 10.4 %collective-permute-start.22 = (f32[15,2,16,128]{3,2,1,0:T(8,128)S(1)}, f32[15,2,16,128]{3,2,1,0:T(8,128)S(1)}, u32[]{:S(2)}, u32[]{:S(2)}) collective-permute-start(f32[15,2,16,128]{3,2,1,0:T(8,128)S(1)} %get-tuple-element.84), channel_id=1, source_target_pairs={{4,8},{12,16},{20,24},{8,4},{16,12},{24,20},{5,9},{13,17},{21,25},... | collective-permute-start | bytes 737288 | tf_op jit(solution)/shard_map/ppermute | solution.py:117
  20.7 12.9 %collective-permute-start.23 = (f32[15,2,16,128]{3,2,1,0:T(8,128)S(1)}, f32[15,2,16,128]{3,2,1,0:T(8,128)S(1)}, u32[]{:S(2)}, u32[]{:S(2)}) collective-permute-start(f32[15,2,16,128]{3,2,1,0:T(8,128)S(1)} %get-tuple-element.85), channel_id=1, source_target_pairs={{0,4},{8,12},{16,20},{24,28},{4,0},{12,8},{20,16},{28,24},{1,5},{9... | collective-permute-start | bytes 737288 | tf_op jit(solution)/shard_map/ppermute | solution.py:117
  25.1 9.1 %collective-permute-start.24 = (f32[2,128,128]{2,1,0:T(8,128)S(1)}, f32[2,128,128]{2,1,0:T(8,128)S(1)}, u32[]{:S(2)}, u32[]{:S(2)}) collective-permute-start(f32[2,128,128]{2,1,0:T(8,128)S(1)} %get-tuple-element.86), channel_id=1, source_target_pairs={{0,2},{1,3},{2,0},{3,1},{4,6},{5,7},{6,4},{7,5},{8,10},{9,11},{10,... | collective-permute-start | bytes 393224 | tf_op jit(solution)/shard_map/ppermute | solution.py:109
  25.4 8.8 %collective-permute-start.25 = (f32[2,128,128]{2,1,0:T(8,128)S(1)}, f32[2,128,128]{2,1,0:T(8,128)S(1)}, u32[]{:S(2)}, u32[]{:S(2)}) collective-permute-start(f32[2,128,128]{2,1,0:T(8,128)S(1)} %get-tuple-element.87), channel_id=1, source_target_pairs={{0,2},{1,3},{2,0},{3,1},{4,6},{5,7},{6,4},{7,5},{8,10},{9,11},{10,... | collective-permute-start | bytes 393224 | tf_op jit(solution)/shard_map/ppermute | solution.py:109
  34.3 1.7 %collective-permute-start.26 = (f32[2,2,128,128]{3,2,1,0:T(8,128)S(1)}, f32[2,2,128,128]{3,2,1,0:T(8,128)S(1)}, u32[]{:S(2)}, u32[]{:S(2)}) collective-permute-start(f32[2,2,128,128]{3,2,1,0:T(8,128)S(1)} %pad_maximum_fusion.16), channel_id=1, source_target_pairs={{0,1},{1,0},{2,3},{3,2},{4,5},{5,4},{6,7},{7,6},{8,9},{9,8},{10,11... | collective-permute-start | bytes 786440 | tf_op jit(solution)/shard_map/ppermute | solution.py:109
  34.8 5.1 %collective-permute-start.27 = (f32[2,4,2,16,128]{4,3,2,1,0:T(8,128)S(1)}, f32[2,4,2,16,128]{4,3,2,1,0:T(8,128)S(1)}, u32[]{:S(2)}, u32[]{:S(2)}) collective-permute-start(f32[2,4,2,16,128]{4,3,2,1,0:T(8,128)S(1)} %share_tiles.1), channel_id=1, source_target_pairs={{0,2},{1,3},{2,0},{3,1},{4,6},{5,7},{6,4},{7,5},{8,10},{9,11},{10,... | collective-permute-start | bytes 393224 | tf_op jit(solution)/shard_map/ppermute | solution.py:109
  39.9 6.9 %copy-start = (f32[1,2,2,32,2048]{4,3,2,1,0:T(8,128)S(1)}, f32[1,2,2,32,2048]{4,3,2,1,0:T(8,128)}, u32[]{:S(2)}) copy-start(f32[1,2,2,32,2048]{4,3,2,1,0:T(8,128)} %param.8) | copy-start | bytes 3145732
  42.1 7.3 %collective-permute-start.28 = (f32[8,2,16,128]{3,2,1,0:T(8,128)}, f32[8,2,16,128]{3,2,1,0:T(8,128)}, u32[]{:S(2)}, u32[]{:S(2)}) collective-permute-start(f32[8,2,16,128]{3,2,1,0:T(8,128)} %get-tuple-element.97), channel_id=1, source_target_pairs={{4,8},{12,16},{20,24},{8,4},{16,12},{24,20},{5,9},{13,17},{21,25},... | collective-permute-start | bytes 393224 | tf_op jit(solution)/shard_map/ppermute | solution.py:117
  45.3 8.1 %collective-permute-start.29 = (f32[8,2,16,128]{3,2,1,0:T(8,128)}, f32[8,2,16,128]{3,2,1,0:T(8,128)}, u32[]{:S(2)}, u32[]{:S(2)}) collective-permute-start(f32[8,2,16,128]{3,2,1,0:T(8,128)} %get-tuple-element.98), channel_id=1, source_target_pairs={{0,4},{8,12},{16,20},{24,28},{4,0},{12,8},{20,16},{28,24},{1,5},{9... | collective-permute-start | bytes 393224 | tf_op jit(solution)/shard_map/ppermute | solution.py:117
  55.2 6.1 %collective-permute-start.30 = (f32[5,2,16,128]{3,2,1,0:T(8,128)S(1)}, f32[5,2,16,128]{3,2,1,0:T(8,128)S(1)}, u32[]{:S(2)}, u32[]{:S(2)}) collective-permute-start(f32[5,2,16,128]{3,2,1,0:T(8,128)S(1)} %get-tuple-element.108), channel_id=1, source_target_pairs={{4,8},{12,16},{20,24},{8,4},{16,12},{24,20},{5,9},{13,17},{21,25},... | collective-permute-start | bytes 245768 | tf_op jit(solution)/shard_map/ppermute | solution.py:117
  58.4 5.7 %collective-permute-start.31 = (f32[5,2,16,128]{3,2,1,0:T(8,128)S(1)}, f32[5,2,16,128]{3,2,1,0:T(8,128)S(1)}, u32[]{:S(2)}, u32[]{:S(2)}) collective-permute-start(f32[5,2,16,128]{3,2,1,0:T(8,128)S(1)} %get-tuple-element.109), channel_id=1, source_target_pairs={{0,4},{8,12},{16,20},{24,28},{4,0},{12,8},{20,16},{28,24},{1,5},{9... | collective-permute-start | bytes 245768 | tf_op jit(solution)/shard_map/ppermute | solution.py:117
  65.3 5.9 %collective-permute-start.32 = (f32[4,2,16,128]{3,2,1,0:T(8,128)S(1)}, f32[4,2,16,128]{3,2,1,0:T(8,128)S(1)}, u32[]{:S(2)}, u32[]{:S(2)}) collective-permute-start(f32[4,2,16,128]{3,2,1,0:T(8,128)S(1)} %get-tuple-element.111), channel_id=1, source_target_pairs={{4,8},{12,16},{20,24},{8,4},{16,12},{24,20},{5,9},{13,17},{21,25},... | collective-permute-start | bytes 196616 | tf_op jit(solution)/shard_map/ppermute | solution.py:117
  68.4 4.9 %collective-permute-start.33 = (f32[4,2,16,128]{3,2,1,0:T(8,128)S(1)}, f32[4,2,16,128]{3,2,1,0:T(8,128)S(1)}, u32[]{:S(2)}, u32[]{:S(2)}) collective-permute-start(f32[4,2,16,128]{3,2,1,0:T(8,128)S(1)} %get-tuple-element.112), channel_id=1, source_target_pairs={{0,4},{8,12},{16,20},{24,28},{4,0},{12,8},{20,16},{28,24},{1,5},{9... | collective-permute-start | bytes 196616 | tf_op jit(solution)/shard_map/ppermute | solution.py:117
  74.4 5.7 %collective-permute-start.34 = (f32[3,2,16,128]{3,2,1,0:T(8,128)S(1)}, f32[3,2,16,128]{3,2,1,0:T(8,128)S(1)}, u32[]{:S(2)}, u32[]{:S(2)}) collective-permute-start(f32[3,2,16,128]{3,2,1,0:T(8,128)S(1)} %get-tuple-element.114), channel_id=1, source_target_pairs={{4,8},{12,16},{20,24},{8,4},{16,12},{24,20},{5,9},{13,17},{21,25},... | collective-permute-start | bytes 147464 | tf_op jit(solution)/shard_map/ppermute | solution.py:117
  77.5 3.2 %collective-permute-start.35 = (f32[3,2,16,128]{3,2,1,0:T(8,128)S(1)}, f32[3,2,16,128]{3,2,1,0:T(8,128)S(1)}, u32[]{:S(2)}, u32[]{:S(2)}) collective-permute-start(f32[3,2,16,128]{3,2,1,0:T(8,128)S(1)} %get-tuple-element.115), channel_id=1, source_target_pairs={{0,4},{8,12},{16,20},{24,28},{4,0},{12,8},{20,16},{28,24},{1,5},{9... | collective-permute-start | bytes 147464 | tf_op jit(solution)/shard_map/ppermute | solution.py:117
  80.6 3.9 %copy-start.2 = (f32[2,2,32,2048]{3,2,1,0:T(8,128)S(1)}, f32[2,2,32,2048]{3,2,1,0:T(8,128)}, u32[]{:S(2)}) copy-start(f32[2,2,32,2048]{3,2,1,0:T(8,128)} %get-tuple-element.149.base_ref) | copy-start | bytes 3145732
  81.5 3.1 %collective-permute-start.36 = (f32[10,2,16,128]{3,2,1,0:T(8,128)S(1)}, f32[10,2,16,128]{3,2,1,0:T(8,128)S(1)}, u32[]{:S(2)}, u32[]{:S(2)}) collective-permute-start(f32[10,2,16,128]{3,2,1,0:T(8,128)S(1)} %slice.201), channel_id=1, source_target_pairs={{0,1},{1,0},{2,3},{3,2},{4,5},{5,4},{6,7},{7,6},{8,9},{9,8},{10,11... | collective-permute-start | bytes 491528 | tf_op jit(solution)/shard_map/ppermute | solution.py:109
  85.6 1.0 %copy-start.3 = (f32[2,2,32,2048]{3,2,1,0:T(8,128)}, f32[2,2,32,2048]{3,2,1,0:T(8,128)S(1)}, u32[]{:S(2)}) copy-start(f32[2,2,32,2048]{3,2,1,0:T(8,128)S(1)} %finish.1) | copy-start | bytes 3145732
